TPU v7x, 32 devices: a whole 2x2x4 slice. The times are simulated.
32 devices in a mesh: rows: 8 (over y, x, core), cols: 4 (over z).
Axes of the slice: x: 2, y: 2, z: 4, core: 2. Of those that a mesh axis runs over, the one named last changes fastest.
Arguments:
- mantissa: bfloat16 [8192, 8192], P('rows', 'cols'), may hold values from 0.5 to 1
- exponents: int32 [512, 64], P('rows'), may hold values from -3 to 1
Outputs:
- spectrum_real: float32 [8192, 8192], P(('rows', 'cols'))
- spectrum_imag: float32 [8192, 8192], P(('rows', 'cols'))
Inputs may be any that keep to these rules, and one draw needn't show every extreme that they name: `exponents`: each entry scales its block of 16 rows and 128 columns of the table by 2 to that power.
All inputs are finite; a program needn't handle non-finite values.
Results may differ from a plain program's by a relative error of at most 0.0013.
Values may be sent and summed in bfloat16 or wider, within the bound.
No kernel may reach another device: no remote copies, remote signals or barrier semaphores. Data moves between devices by JAX's collectives and lax.ppermute only.
A program may use at most 128 MiB of HBM per device.

v0:
```python
import math

import jax
import jax.numpy as jnp
from jax import lax
from jax.sharding import PartitionSpec as P

NR = 8192
NC = 8192


two_pi = 2.0 * math.pi
inner_len = 64


def shifted(value, axis, steps):
    count = lax.axis_size(axis)
    first, last = (max(0, -steps), min(count, count - steps))
    return lax.ppermute(value, axis, [(source, source + steps) for source in range(first, last)])


def dft_tables(length):
    index = jnp.arange(length, dtype=jnp.int32)
    angle = (index[:, None] * index[None, :] % length).astype(jnp.float32) * (two_pi / length)
    return (jnp.cos(angle), -jnp.sin(angle))


def twiddle_tables(total, first_len, second_len):
    first = jnp.arange(first_len, dtype=jnp.int32)
    second = jnp.arange(second_len, dtype=jnp.int32)
    angle = (first[:, None] * second[None, :]).astype(jnp.float32) * (two_pi / total)
    return (jnp.cos(angle), -jnp.sin(angle))


def product(form, left, right):
    return jnp.einsum(
        form, left, right, precision=lax.Precision.HIGHEST, preferred_element_type=jnp.float32
    )


def dequantize(mantissa, exponents):
    row_count, col_count = mantissa.shape
    scaling = jnp.exp2(exponents.astype(jnp.float32))
    blocks = mantissa.astype(jnp.float32).reshape(row_count // 16, 16, col_count // 128, 128)
    return (blocks * scaling[:, None, :, None]).reshape(row_count, col_count)


def transform_rows(masses, devices):
    row_count, length = masses.shape
    outer_len = length // inner_len
    cos_inner, sin_inner = dft_tables(inner_len)
    cos_outer, sin_outer = dft_tables(outer_len)
    cos_twist, sin_twist = twiddle_tables(length, inner_len, outer_len)
    grid = masses.reshape(row_count, inner_len, outer_len)
    first_real = product("bc,icj->ibj", cos_inner, grid)
    first_imag = product("bc,icj->ibj", sin_inner, grid)
    twist_real = first_real * cos_twist - first_imag * sin_twist
    twist_imag = first_real * sin_twist + first_imag * cos_twist
    real_part = product("aj,ibj->iab", cos_outer, twist_real) - product(
        "aj,ibj->iab", sin_outer, twist_imag
    )
    imag_part = product("aj,ibj->iab", cos_outer, twist_imag) + product(
        "aj,ibj->iab", sin_outer, twist_real
    )
    slab = length // devices
    return jnp.concatenate(
        (real_part.reshape(row_count, devices, slab), imag_part.reshape(row_count, devices, slab)),
        axis=2,
    )


def transform_columns(gathered):
    row_count, devices, width = gathered.shape
    slab = width // 2
    total = row_count * devices
    cos_dev, sin_dev = dft_tables(devices)
    cos_local, sin_local = dft_tables(row_count)
    cos_twist, sin_twist = twiddle_tables(total, row_count, devices)
    part_real = gathered[:, :, :slab]
    part_imag = gathered[:, :, slab:]
    first_real = product("bc,jcx->jbx", cos_dev, part_real) - product(
        "bc,jcx->jbx", sin_dev, part_imag
    )
    first_imag = product("bc,jcx->jbx", cos_dev, part_imag) + product(
        "bc,jcx->jbx", sin_dev, part_real
    )
    twist_real = first_real * cos_twist[:, :, None] - first_imag * sin_twist[:, :, None]
    twist_imag = first_real * sin_twist[:, :, None] + first_imag * cos_twist[:, :, None]
    real_part = product("aj,jbx->xab", cos_local, twist_real) - product(
        "aj,jbx->xab", sin_local, twist_imag
    )
    imag_part = product("aj,jbx->xab", cos_local, twist_imag) + product(
        "aj,jbx->xab", sin_local, twist_real
    )
    norming = 1.0 / math.sqrt(NR * NC)
    return (real_part.reshape(slab, total) * norming, imag_part.reshape(slab, total) * norming)


def local(mantissa, exponents):
    devices = lax.axis_size("rows") * lax.axis_size("cols")
    col_index = lax.axis_index("cols")
    local_rows, local_cols = mantissa.shape
    col_blocks = local_cols // 128
    own_scales = lax.dynamic_slice_in_dim(exponents, col_index * col_blocks, col_blocks, 1)
    cumulative = dequantize(mantissa, own_scales)
    left_column = shifted(cumulative[:, -1], "cols", 1)
    widened = jnp.concatenate((left_column[:, None], cumulative), axis=1)
    upper_line = shifted(widened[-1], "rows", 1)
    above = jnp.concatenate((upper_line[None, :], widened[:-1]), axis=0)
    masses = cumulative - above[:, 1:] - (widened[:, :-1] - above[:, :-1])
    row_masses = lax.all_to_all(
        masses.astype(jnp.bfloat16), "cols", split_axis=0, concat_axis=1, tiled=True
    ).astype(masses.dtype)
    packed = transform_rows(row_masses, devices)
    gathered = lax.all_to_all(packed, ("rows", "cols"), split_axis=1, concat_axis=1, tiled=True)
    return transform_columns(gathered)


def solution(mesh):
    in_specs = (P("rows", "cols"), P("rows", None))
    out_specs = (P(("rows", "cols"), None), P(("rows", "cols"), None))
    return jax.shard_map(local, mesh=mesh, in_specs=in_specs, out_specs=out_specs, check_vma=False)
```

profile of v0, /device:TPU:17, one launch (start us, length us, event | category | flops | bytes accessed | tf_op | source)
XLA Modules:
  0.0 846.0 jit_solution(74870026389369485)
XLA Ops:
  0.6 0.0 copy-start.6
  0.6 1.0 multiply_exponential_fusion
  1.6 4.0 mul.371
  5.6 0.0 copy-done.6
  5.7 7.9 bitcast_multiply_fusion
  13.5 0.0 copy-start
  13.5 3.4 copy-done
  16.9 0.4 slice_reduce_fusion
  17.3 3.2 collective-permute-start
  20.5 1.1 collective-permute-done
  21.6 0.2 copy.31
  21.9 0.0 copy-start.1
  21.9 1.1 maximum_reduce_fusion
  23.0 5.1 collective-permute-start.1
  28.1 0.0 copy-done.1
  28.1 4.7 slice_maximum_fusion
  32.8 0.0 collective-permute-done.1
  32.8 10.2 %fusion.3 = bf16[1024,2048]{1,0:T(8,128)(2,1)} fusion(f32[1024,2048]{1,0:T(8,128)S(1)} %copy-done.1, f32[1,2049]{1,0:T(1,128)S(1)} %broadcast_in_dim.5, f32[1023,2049]{1,0:T(8,128)} %slice_maximum_fusion, f32[1024,1]{1,0:T(8,128)S(1)} %copy.31), kind=kLoop, calls=%fused_computation.7 | loop fusion | flops 14680064 | bytes 20979712 | tf_op jit(solution)/shard_map/convert_element_type | solution.py:112
  43.0 5.0 all-to-all-start
  48.1 0.1 sine_negate_fusion.7
  48.2 90.1 %all-to-all-done = bf16[4,256,2048]{2,1,0:T(8,128)(2,1)} async-done(((bf16[4,256,2048]{2,1,0:T(8,128)(2,1)}), bf16[4,256,2048]{2,1,0:T(8,128)(2,1)}, u32[]{:S(2)}, u32[]{:S(2)}) %all-to-all-start) | async-done | bytes 4194336 | tf_op jit(solution)/shard_map/all_to_all | solution.py:111
  138.3 7.4 copy.32
  145.8 7.6 reshape.79
  153.4 9.1 %fusion.70 = f32[256,128,64]{1,2,0:T(8,128)} fusion(bf16[256,64,128]{2,1,0:T(8,128)(2,1)} %reshape.79), kind=kOutput, calls=%fused_computation.89 | convolution fusion | flops 1610670080 | bytes 12582912 | tf_op jit(solution)/shard_map/bc,icj->ibj/dot_general | solution.py:36
  162.5 9.9 %fusion.5 = (f32[256,64,128]{2,1,0:T(8,128)S(1)}, f32[256,64,128]{2,1,0:T(8,128)S(1)}) fusion(f32[256,128,64]{1,2,0:T(8,128)} %fusion.70, f32[64,128]{1,0:T(8,128)S(1)} %get-tuple-element.12, f32[64,128]{1,0:T(8,128)S(1)} %get-tuple-element.13, bf16[256,64,128]{2,1,0:T(8,128)(2,1)} %reshape.79), kind=kOutput, calls=%fused_computation.14 | convolution fusion | flops 1623257088 | bytes 29425664 | tf_op jit(solution)/shard_map/bc,icj->ibj/dot_general | solution.py:36
  172.4 17.4 %fusion.25 = f32[256,64,128]{0,2,1:T(8,128)} fusion(f32[256,64,128]{2,1,0:T(8,128)S(1)} %get-tuple-element.9), kind=kOutput, calls=%fused_computation.42 | convolution fusion | flops 3221471232 | bytes 16777216 | tf_op jit(solution)/shard_map/aj,ibj->iab/dot_general | solution.py:36
  189.8 17.1 %fusion.23 = f32[256,64,128]{0,2,1:T(8,128)} fusion(f32[256,64,128]{2,1,0:T(8,128)S(1)} %get-tuple-element.9), kind=kOutput, calls=%fused_computation.40 | convolution fusion | flops 3221454848 | bytes 16777216 | tf_op jit(solution)/shard_map/aj,ibj->iab/dot_general | solution.py:36
  206.9 19.6 %subtract_bitcast_fusion.1 = f32[256,128,64]{0,1,2:T(8,128)} fusion(f32[256,64,128]{0,2,1:T(8,128)} %fusion.25, f32[256,64,128]{2,1,0:T(8,128)S(1)} %get-tuple-element.8), kind=kOutput, calls=%fused_computation.23 | convolution fusion | flops 3223552000 | bytes 25165824 | tf_op jit(solution)/shard_map/aj,ibj->iab/dot_general | solution.py:36
  226.5 0.0 copy-start.4
  226.6 11.6 %copy.35 = f32[256,128,64]{0,2,1:T(8,128)} copy(f32[256,128,64]{0,1,2:T(8,128)} %subtract_bitcast_fusion.1) | data formatting | bytes 16777216 | tf_op jit(solution)/shard_map/sub | solution.py:59
  238.2 0.0 copy-done.4
  238.2 18.2 %add_bitcast_fusion.1 = f32[256,128,64]{0,1,2:T(8,128)} fusion(f32[256,64,128]{0,2,1:T(8,128)S(1)} %copy-done.4, f32[256,64,128]{2,1,0:T(8,128)S(1)} %get-tuple-element.8), kind=kOutput, calls=%fused_computation.22 | convolution fusion | flops 3223568384 | bytes 25165824 | tf_op jit(solution)/shard_map/aj,ibj->iab/dot_general | solution.py:36
  256.4 0.0 copy-start.5
  256.4 8.4 copy.38
  264.8 0.0 copy-done.5
  264.8 6.1 pad_maximum_fusion
  270.9 17.5 %copy.39 = f32[256,32,512]{2,0,1:T(8,128)} copy(f32[256,32,512]{0,2,1:T(8,128)} %pad_maximum_fusion) | data formatting | bytes 33554432 | tf_op jit(solution)/shard_map/concatenate | solution.py:66
  288.3 7.0 all-to-all-start.1
  295.3 0.5 sine_negate_fusion.3
  295.8 371.2 %all-to-all-done.1 = f32[256,32,512]{2,0,1:T(8,128)} async-done(((f32[256,32,512]{2,0,1:T(8,128)}), f32[256,32,512]{2,0,1:T(8,128)}, u32[]{:S(2)}, u32[]{:S(2)}) %all-to-all-start.1) | async-done | bytes 16777248 | tf_op jit(solution)/shard_map/all_to_all | solution.py:115
  667.0 6.5 fusion.157
  673.6 0.0 copy-start.3
  673.6 13.1 %fusion.7 = f32[256,256,32]{1,2,0:T(8,128)} fusion(f32[256,32,256]{2,0,1:T(8,128)S(1)} %get-tuple-element.11), kind=kOutput, calls=%fused_computation.24 | convolution fusion | flops 805320704 | bytes 16777216 | tf_op jit(solution)/shard_map/bc,jcx->jbx/dot_general | solution.py:36
  686.7 13.3 %fusion.9 = f32[256,256,32]{1,2,0:T(8,128)} fusion(f32[256,32,256]{2,0,1:T(8,128)S(1)} %get-tuple-element.11), kind=kOutput, calls=%fused_computation.26 | convolution fusion | flops 805321728 | bytes 16777216 | tf_op jit(solution)/shard_map/bc,jcx->jbx/dot_general | solution.py:36
  700.0 0.0 copy-done.3
  700.0 13.1 %fusion.11 = f32[256,256,32]{1,2,0:T(8,128)} fusion(f32[256,32,256]{2,0,1:T(8,128)S(1)} %get-tuple-element.10), kind=kOutput, calls=%fused_computation.28 | convolution fusion | flops 805321728 | bytes 16777216 | tf_op jit(solution)/shard_map/bc,jcx->jbx/dot_general | solution.py:36
  713.1 26.8 %subtract_bitcast_fusion = (f32[256,32,256]{2,1,0:T(8,128)}, f32[256,32,256]{2,1,0:T(8,128)}) fusion(f32[256,32]{1,0:T(8,128)S(1)} %get-tuple-element.14, f32[256,32]{1,0:T(8,128)S(1)} %get-tuple-element.15, f32[256,256,32]{1,2,0:T(8,128)} %fusion.7, f32[256,256,32]{1,2,0:T(8,128)} %fusion.11, f32[256,256,32]{1,2,0:T(8,128)} %fusion.9, ...), kind=kOutput, calls=%fused_computation.21 | convolution fusion | flops 822097920 | bytes 50397184 | tf_op jit(solution)/shard_map/bc,jcx->jbx/dot_general | solution.py:36
  739.9 0.0 copy-start.2
  739.9 0.0 slice-start
  739.9 17.9 %fusion.15 = f32[32,256,256]{1,2,0:T(8,128)S(1)} fusion(f32[256,32,256]{2,1,0:T(8,128)} %get-tuple-element.7), kind=kOutput, calls=%fused_computation.32 | convolution fusion | flops 6443368448 | bytes 16777216 | tf_op jit(solution)/shard_map/aj,jbx->xab/dot_general | solution.py:36
  757.8 0.0 copy-done.2
  757.8 0.0 slice-start.1
  757.8 15.0 %fusion.17 = f32[32,256,256]{1,2,0:T(8,128)} fusion(f32[256,32,256]{2,1,0:T(8,128)S(1)} %copy-done.2), kind=kOutput, calls=%fused_computation.34 | convolution fusion | flops 6443433984 | bytes 16777216 | tf_op jit(solution)/shard_map/aj,jbx->xab/dot_general | solution.py:36
  772.8 0.0 slice-done
  772.8 0.0 slice-done.1
  772.8 15.6 %multiply_bitcast_fusion = f32[256,256,32]{0,1,2:T(8,128)} fusion(f32[32,256,256]{1,2,0:T(8,128)S(1)} %fusion.15, f32[256,32,256]{2,1,0:T(8,128)S(1)} %bitcast.80), kind=kOutput, calls=%fused_computation.18 | convolution fusion | flops 6447628288 | bytes 25165824 | tf_op jit(solution)/shard_map/aj,jbx->xab/dot_general | solution.py:36
  788.4 11.5 %copy.47 = f32[256,256,32]{0,2,1:T(8,128)} copy(f32[256,256,32]{0,1,2:T(8,128)} %multiply_bitcast_fusion) | data formatting | bytes 16777216 | tf_op jit(solution)/shard_map/mul | solution.py:96
  799.9 9.1 %copy.49 = f32[256,8192]{1,0:T(8,128)} copy(f32[256,8192]{0,1:T(8,128)} %bitcast.82) | data formatting | bytes 16777216
  809.0 19.5 %multiply_bitcast_fusion.1 = f32[256,256,32]{0,1,2:T(8,128)S(1)} fusion(f32[32,256,256]{1,2,0:T(8,128)} %fusion.17, f32[256,32,256]{2,1,0:T(8,128)} %get-tuple-element.6), kind=kOutput, calls=%fused_computation.19 | convolution fusion | flops 6447562752 | bytes 25165824 | tf_op jit(solution)/shard_map/aj,jbx->xab/dot_general | solution.py:36
  828.5 8.1 copy.44
  836.6 8.9 %copy.48 = f32[256,8192]{1,0:T(8,128)} copy(f32[256,8192]{0,1:T(8,128)} %bitcast.83) | data formatting | bytes 16777216
  (2 shorter events, 0.0 us)
Async XLA Ops:
  0.6 5.0 copy-start.6
  13.5 3.4 copy-start
  17.3 4.4 collective-permute-start
  21.9 6.2 copy-start.1
  23.0 9.8 %collective-permute-start.1 = (f32[2049]{0:T(1024)S(1)}, f32[2049]{0:T(1024)S(1)}, u32[]{:S(2)}, u32[]{:S(2)}) collective-permute-start(f32[2049]{0:T(1024)S(1)} %maximum_reduce_fusion), channel_id=1, source_target_pairs={{0,4},{4,8},{8,12},{12,16},{16,20},{20,24},{24,28},{1,5},{5,9},{9,... | collective-permute-start | bytes 24596 | tf_op jit(solution)/shard_map/ppermute | solution.py:19
  43.0 95.3 %all-to-all-start = ((bf16[4,256,2048]{2,1,0:T(8,128)(2,1)}), bf16[4,256,2048]{2,1,0:T(8,128)(2,1)}, u32[]{:S(2)}, u32[]{:S(2)}) async-start(bf16[4,256,2048]{2,1,0:T(8,128)(2,1)} %bitcast.86), calls=%async_computation | async-start | bytes 8388608 | tf_op jit(solution)/shard_map/all_to_all | solution.py:111
  226.5 11.6 %copy-start.4 = (f32[256,64,128]{0,2,1:T(8,128)S(1)}, f32[256,64,128]{0,2,1:T(8,128)}, u32[]{:S(2)}) copy-start(f32[256,64,128]{0,2,1:T(8,128)} %fusion.23) | copy-start | bytes 25165828
  256.4 8.4 copy-start.5
  288.3 378.7 %all-to-all-start.1 = ((f32[256,32,512]{2,0,1:T(8,128)}), f32[256,32,512]{2,0,1:T(8,128)}, u32[]{:S(2)}, u32[]{:S(2)}) async-start(f32[256,32,512]{2,0,1:T(8,128)} %copy.39), calls=%async_computation.1 | async-start | bytes 33554432 | tf_op jit(solution)/shard_map/all_to_all | solution.py:115
  673.6 26.5 %copy-start.3 = (f32[256,32,256]{2,0,1:T(8,128)}, f32[256,32,256]{2,0,1:T(8,128)S(1)}, u32[]{:S(2)}) copy-start(f32[256,32,256]{2,0,1:T(8,128)S(1)} %get-tuple-element.10) | copy-start | bytes 25165828
  739.9 17.9 %copy-start.2 = (f32[256,32,256]{2,1,0:T(8,128)S(1)}, f32[256,32,256]{2,1,0:T(8,128)}, u32[]{:S(2)}) copy-start(f32[256,32,256]{2,1,0:T(8,128)} %get-tuple-element.7) | copy-start | bytes 25165828
  739.9 32.9 %slice-start = ((s8[8388608]{0:T(1024)(128)(4,1)}), s8[4194304]{0:T(1024)(128)(4,1)S(1)}, s32[]{:S(2)}) async-start(s8[8388608]{0:T(1024)(128)(4,1)} %bitcast.79), calls=%async_computation.2 | async-start | bytes 8388608
  757.8 15.0 %slice-start.1 = ((s8[8388608]{0:T(1024)(128)(4,1)}), s8[4194304]{0:T(1024)(128)(4,1)S(1)}, s32[]{:S(2)}) async-start(s8[8388608]{0:T(1024)(128)(4,1)} %bitcast.79), calls=%async_computation.3 | async-start | bytes 8388608
where the time goes:
time: 854 us; the launch traced here: 846 us
  waiting for transfers between devices  462 us (54%)
  matrix products  226 us (26%)
  local copies, waits for them, and re-layouts  105 us (12%)
  other arithmetic  31.6 us (4%)
  starting transfers between devices  20.3 us (2%)
    all_to_all x1, waiting for transfers between devices, local(): lax.all_to_all(packed, ('rows', 'cols'), split_axis=1, concat_axis=1, til...  371 us
    dot_general x14, matrix products, product(): jnp.einsum(form, left, right, precision=lax.Precision.HIGHEST, preferred_...  226 us
    all_to_all x1, waiting for transfers between devices, local(): lax.all_to_all(masses.astype(jnp.bfloat16), 'cols', split_axis=0, concat_...  90.1 us
    unnamed x20, local copies, waits for them, and re-layouts  21.5 us
    concatenate x1, local copies, waits for them, and re-layouts, transform_rows(): jnp.concatenate((real_part.reshape(row_count, devices, slab), imag_part.r...  17.5 us
  transfers between devices with their start and end apart: 4, of which 3 were waited for; matrix products, arithmetic and copies ran while one was open for 1% of the time, Pallas kernels for 0%

commit v1 on v0

v1 whole, which is shorter than its diff:
```python
import functools
import math

import jax
import jax.numpy as jnp
import numpy as np
from jax import lax
from jax.experimental import pallas as pl
from jax.experimental.pallas import tpu as pltpu
from jax.sharding import PartitionSpec as P

LANES = 128
BLOCK_ROWS = 16
BLOCK_COLS = 128
f32 = jnp.float32
bf16 = jnp.bfloat16


def split(value):
    high = value.astype(bf16)
    return high, (value - high.astype(f32)).astype(bf16)


def split_np(table):
    high = np.asarray(table, np.float32).astype(jnp.bfloat16)
    return high, (np.asarray(table, np.float32) - high.astype(np.float32)).astype(jnp.bfloat16)


def product(left, right):
    return lax.dot_general(left, right, (((1,), (0,)), ((), ())), preferred_element_type=f32)


def product3(value, high, low):
    value_high, value_low = split(value)
    return product(value_high, high) + product(value_low, high) + product(value_high, low)


def times(value, angle_part, whole):
    real, imag = value
    angle_part %= whole
    if angle_part == 0:
        return real, imag
    if 4 * angle_part == whole:
        return imag, -real
    if 2 * angle_part == whole:
        return -real, -imag
    if 4 * angle_part == 3 * whole:
        return -imag, real
    if 8 * angle_part == whole:
        c = math.sqrt(0.5)
        return (real + imag) * c, (imag - real) * c
    if 8 * angle_part == 3 * whole:
        c = math.sqrt(0.5)
        return (imag - real) * c, (real + imag) * -c
    c, s = math.cos(2 * math.pi * angle_part / whole), math.sin(2 * math.pi * angle_part / whole)
    return real * c + imag * s, imag * c - real * s


def dft(values, keep=None):
    count = len(values)
    keep = count if keep is None else keep
    if count == 1:
        return values[:keep]
    half = count // 2
    even, odd = dft(values[0::2], min(keep, half)), dft(values[1::2], min(keep, half))
    odd = [times(odd[k], k, count) for k in range(len(odd))]
    low = [(e[0] + o[0], e[1] + o[1]) for e, o in zip(even, odd)]
    high = [(e[0] - o[0], e[1] - o[1]) for e, o in zip(even, odd)]
    return (low + high)[:keep]


def row_kernel(
    cols, group, z_ref, scale_ref, halo_ref, high_ref, low_ref, cos_ref, sin_ref, *refs
):
    pieces, (out_ref, last_ref, table, mixed, stage) = refs[:cols], refs[cols:]
    rows, piece_cols = pieces[0].shape
    halos = halo_ref.shape[0]
    segment = rows // halos
    scales = rows // BLOCK_ROWS
    outer = cos_ref.shape[0]
    slabs, kept = out_ref.shape[:2]
    pad = table.shape[0] - outer * LANES
    z = z_ref[0]
    table[0:pad, :] = jnp.zeros((pad, rows), f32)
    starts = lax.broadcasted_iota(jnp.int32, (rows, LANES), 0) % segment == 0

    for step, piece in enumerate(pieces):
        base = lax.bitwise_xor(z, step) * piece_cols

        def dequantize(block, carry, piece=piece, base=base):
            here = pl.multiple_of(block * LANES, LANES)
            there = pl.multiple_of(base + here, LANES)
            value = piece[:, pl.ds(here, LANES)].astype(f32).reshape(scales, BLOCK_ROWS, LANES)
            value = (value * scale_ref[:, pl.ds(there, LANES)][:, None, :]).reshape(rows, LANES)
            halo = jnp.broadcast_to(
                halo_ref[:, pl.ds(there, LANES)][:, None, :], (halos, segment, LANES)
            ).reshape(rows, LANES)
            above = jnp.where(starts, halo, pltpu.roll(value, 1, 0))
            last_ref[:, pl.ds(there, LANES)] = value.reshape(halos, segment, LANES)[:, segment - 1, :]
            table[pl.ds(pl.multiple_of(pad + there, 8), LANES), :] = (value - above).T
            return carry

        lax.fori_loop(0, piece_cols // LANES, dequantize, 0, unroll=2)

    def mix(index, carry):
        now = table[pl.ds(pad + index, LANES, stride=outer), :]
        before = table[pl.ds(pad + index - 1, LANES, stride=outer), :]
        spun = product3((now - before).T, high_ref[...], low_ref[...])
        real, imag = spun[:, :LANES], spun[:, LANES:]
        cos, sin = cos_ref[pl.ds(index, 1), :], sin_ref[pl.ds(index, 1), :]
        mixed[index, 0] = real * cos + imag * sin
        mixed[index, 1] = imag * cos - real * sin
        return carry

    lax.fori_loop(0, outer, mix, 0, unroll=2)

    inner = outer // slabs

    def finish(tile, carry):
        here = pl.ds(pl.multiple_of(tile * 8, 8), 8)
        for low in range(slabs):
            values = [
                (mixed[high * slabs + low, 0, here, :], mixed[high * slabs + low, 1, here, :])
                for high in range(inner)
            ]
            for k, value in enumerate(dft(values, kept)):
                stage[k, low, 0], stage[k, low, 1] = times(value, low * k, outer)
        for k in range(kept):
            for slab, value in enumerate(dft([(stage[k, low, 0], stage[k, low, 1]) for low in range(slabs)])):
                out_ref[slab, k, 0, here, :], out_ref[slab, k, 1, here, :] = value
        return carry

    lax.fori_loop(0, rows // 8, finish, 0)


def transform_rows(z, pieces, scale, halo, tables, slabs, kept, outer):
    rows, piece_cols = pieces[0].shape
    cols = len(pieces)
    total = cols * piece_cols
    vmem = pl.BlockSpec(memory_space=pltpu.VMEM)
    return pl.pallas_call(
        functools.partial(row_kernel, cols, None),
        out_shape=(
            jax.ShapeDtypeStruct((slabs, kept, 2, rows, LANES), f32),
            jax.ShapeDtypeStruct(halo.shape, f32),
        ),
        in_specs=[pl.BlockSpec(memory_space=pltpu.SMEM)] + [vmem] * (6 + cols),
        out_specs=(vmem, vmem),
        scratch_shapes=[
            pltpu.VMEM((8 + total, rows), f32),
            pltpu.VMEM((outer, 2, rows, LANES), f32),
            pltpu.VMEM((kept, slabs, 2, 8, LANES), f32),
        ],
        compiler_params=pltpu.CompilerParams(vmem_limit_bytes=48 * 1024 * 1024),
        cost_estimate=pl.CostEstimate(
            flops=12 * rows * total * LANES, bytes_accessed=rows * total * 8, transcendentals=0
        ),
        name="row_transform",
    )(z, scale, halo, *tables, *pieces)


def column_kernel(first, high_ref, low_ref, cos_ref, sin_ref, in_ref, out_ref, real, imag):
    sources, _, _, rows, width = in_ref.shape
    count = out_ref.shape[0]
    real[...] = in_ref[:, 0, 0].reshape(sources * rows, width)
    imag[...] = in_ref[:, 0, 1].reshape(sources * rows, width)

    def mix(index, carry):
        here = pl.ds(index, LANES, stride=count)
        value = jnp.concatenate((real[here, :].T, imag[here, :].T), axis=1)
        spun = product3(value, high_ref[...], low_ref[...])
        spun_real, spun_imag = spun[:, :LANES], spun[:, LANES:]
        cos, sin = cos_ref[pl.ds(first + index, 1), :], sin_ref[pl.ds(first + index, 1), :]
        out_ref[index, 0] = spun_real * cos + spun_imag * sin
        out_ref[index, 1] = spun_imag * cos - spun_real * sin
        return carry

    lax.fori_loop(0, count, mix, 0, unroll=2)


def mix_columns(gathered, tables, first, count):
    sources, planes, _, rows, width = gathered.shape
    whole = lambda table: pl.BlockSpec(table.shape, lambda plane: (0, 0))
    return pl.pallas_call(
        functools.partial(column_kernel, first),
        out_shape=jax.ShapeDtypeStruct((count, 2, planes * width, LANES), f32),
        grid=(planes,),
        in_specs=[whole(table) for table in tables]
        + [pl.BlockSpec((sources, 1, 2, rows, width), lambda plane: (0, plane, 0, 0, 0))],
        out_specs=pl.BlockSpec((count, 2, width, LANES), lambda plane: (0, 0, plane, 0)),
        scratch_shapes=[pltpu.VMEM((sources * rows, width), f32)] * 2,
        compiler_params=pltpu.CompilerParams(vmem_limit_bytes=48 * 1024 * 1024),
        cost_estimate=pl.CostEstimate(
            flops=24 * gathered.size * LANES, bytes_accessed=gathered.size * 8, transcendentals=0
        ),
        name="column_mix",
    )(*tables, gathered)


def finish_kernel(outer, *refs):
    parts, (real_ref, imag_ref, stage) = refs[:-3], refs[-3:]
    count = parts[0].shape[0]
    radix = 1 << ((outer.bit_length() - 1) // 2)
    rest = outer // radix

    def finish(tile, carry):
        here = pl.ds(pl.multiple_of(tile * 8, 8), 8)

        def load(index):
            part = parts[index // count]
            return part[index % count, 0, here, :], part[index % count, 1, here, :]

        for low in range(rest):
            values = dft([load(high * rest + low) for high in range(radix)])
            for k, value in enumerate(values):
                stage[k, low, 0], stage[k, low, 1] = times(value, low * k, outer)
        for k in range(radix):
            values = dft([(stage[k, low, 0], stage[k, low, 1]) for low in range(rest)])
            for high, value in enumerate(values):
                column = (k + radix * high) * LANES
                real_ref[here, column : column + LANES], imag_ref[here, column : column + LANES] = value
        return carry

    lax.fori_loop(0, real_ref.shape[0] // 8, finish, 0)


def finish_columns(parts, outer):
    slab = parts[0].shape[2]
    tile = min(32, slab)
    radix = 1 << ((outer.bit_length() - 1) // 2)
    shape = jax.ShapeDtypeStruct((slab, outer * LANES), f32)
    return pl.pallas_call(
        functools.partial(finish_kernel, outer),
        out_shape=(shape, shape),
        grid=(slab // tile,),
        in_specs=[
            pl.BlockSpec((part.shape[0], 2, tile, LANES), lambda step: (0, 0, step, 0)) for part in parts
        ],
        out_specs=(pl.BlockSpec((tile, outer * LANES), lambda step: (step, 0)),) * 2,
        scratch_shapes=[pltpu.VMEM((radix, outer // radix, 2, 8, LANES), f32)],
        compiler_params=pltpu.CompilerParams(vmem_limit_bytes=48 * 1024 * 1024),
        name="column_finish",
    )(*parts)


def local(mantissa, exponents):
    slabs, cols = lax.axis_size("rows"), lax.axis_size("cols")
    half = cols // 2
    z = lax.axis_index("cols")
    kind, side = z % half, z // half
    local_rows, local_cols = mantissa.shape
    total = local_cols * cols
    outer = total // LANES
    slab = total // (slabs * cols)
    inner = outer // slabs
    kept = inner // 2
    lines = local_rows // outer
    kind_lines = lines // half
    chunks = kind_lines * outer // LANES
    count = outer // chunks
    chunk_rows = kind_lines * count

    index = np.arange(LANES)
    angle = 2 * np.pi * (index[:, None] * index[None, :] % LANES) / LANES
    row_matrix = np.concatenate((np.cos(angle), -np.sin(angle)), axis=1)
    column_matrix = np.block([[np.cos(angle), -np.sin(angle)], [np.sin(angle), np.cos(angle)]])
    sides = np.arange(2)[:, None, None] * kept * LANES
    twist = np.arange(outer)[None, :, None] * (index[None, None, :] + sides) % total
    twist = 2 * np.pi * twist / total
    own_side = lambda table: lax.dynamic_index_in_dim(jnp.asarray(table, f32), side, 0, False)
    row_tables = (*split_np(row_matrix), own_side(np.cos(twist)), own_side(np.sin(twist)))
    column_tables = (
        *split_np(column_matrix),
        np.asarray(np.cos(twist[0]) / total, np.float32),
        np.asarray(np.sin(twist[0]) / total, np.float32),
    )

    by_kind = mantissa.reshape(half, kind_lines, chunks, count, local_cols)

    def raw_piece(chunk, step):
        target_kind = lax.bitwise_xor(z, step) % half
        piece = lax.dynamic_index_in_dim(by_kind[:, :, chunk], target_kind, 0, False)
        piece = piece.reshape(chunk_rows, local_cols)
        return trade(piece, step)

    def trade(value, step):
        if step == 0:
            return value
        return lax.ppermute(value, "cols", [(at, at ^ step) for at in range(cols)])

    scaling = jnp.exp2(exponents.astype(f32))
    own_scaling = lax.dynamic_slice_in_dim(scaling, z * (local_cols // BLOCK_COLS), local_cols // BLOCK_COLS, 1)
    ends = mantissa.reshape(lines, outer, local_cols)[:, -1].astype(f32)
    end_scaling = own_scaling.reshape(lines, outer // BLOCK_ROWS, -1)[:, -1]
    ends = (ends.reshape(lines, -1, BLOCK_COLS) * end_scaling[:, :, None]).reshape(lines, local_cols)
    ends = ends.astype(bf16)
    above = lax.ppermute(ends[-1:], "rows", [(at, at + 1) for at in range(slabs - 1)])
    above = jnp.concatenate((above, ends[:-1]), axis=0).reshape(half, kind_lines, local_cols)
    raw = [[raw_piece(chunk, step) for step in range(cols)] for chunk in range(chunks)]
    halos = [
        trade(lax.dynamic_index_in_dim(above, lax.bitwise_xor(z, step) % half, 0, False), step)
        for step in range(cols)
    ]
    halo = jnp.zeros((kind_lines, total), f32)
    for step in range(cols):
        at = lax.bitwise_xor(z, step) * local_cols
        halo = lax.dynamic_update_slice_in_dim(halo, halos[step].astype(f32), at, 1)

    own_rows = lax.dynamic_index_in_dim(
        scaling.reshape(half, kind_lines, chunks, count // BLOCK_ROWS, -1), kind, 0, False
    )
    own_rows = jnp.repeat(own_rows, BLOCK_COLS, axis=-1)

    groups = [
        [row * cols + col for row in range(slabs) for col in range(part * half, (part + 1) * half)]
        for part in range(2)
    ]
    z_word = jnp.full((1,), z, jnp.int32)
    parts = []
    for chunk in range(chunks):
        scale = own_rows[:, chunk].reshape(chunk_rows // BLOCK_ROWS, total)
        spectra, halo = transform_rows(z_word, raw[chunk], scale, halo, row_tables, slabs, kept, outer)
        spectra = spectra.astype(jnp.float16)
        width = min(slab, LANES)
        planes = slab // width
        if slab >= LANES:
            spectra = spectra.reshape(slabs * half, planes, 2, chunk_rows, LANES)
        else:
            spectra = spectra.reshape(slabs, kept, 2, chunk_rows, LANES // slab, slab)
            spectra = spectra.transpose(0, 1, 4, 2, 3, 5).reshape(slabs * half, 1, 2, chunk_rows, slab)
        gathered = lax.all_to_all(
            spectra, ("rows", "cols"), split_axis=0, concat_axis=0, tiled=True, axis_index_groups=groups
        )
        parts.append(mix_columns(gathered.astype(f32), column_tables, chunk * count, count))
    return tuple(finish_columns(parts, outer))


def solution(mesh):
    in_specs = (P("rows", "cols"), P("rows", None))
    out_specs = (P(("rows", "cols"), None), P(("rows", "cols"), None))
    return jax.shard_map(local, mesh=mesh, in_specs=in_specs, out_specs=out_specs, check_vma=False)
```

time: 854 us -> 414 us (0.48)
  waiting for transfers between devices: 462 us -> 170 us
  matrix products: 226 us -> 0 us
  Pallas kernels: 0 us -> 131 us
  local copies, waits for them, and re-layouts: 105 us -> 21 us
  starting transfers between devices: 20.3 us -> 58.1 us
    all_to_all x2 -> x4, waiting for transfers between devices: 461 us -> 22.9 us  [local(): lax.all_to_all(spectra, ('rows', 'cols'), split_axis=0, concat_axis=0, ti...]
    dot_general x14 -> x0, matrix products: 226 us -> none  [product(): jnp.einsum(form, left, right, precision=lax.Precision.HIGHEST, preferred_...]
    ppermute x2 -> x16, waiting for transfers between devices: 1.14 us -> 147 us  [the longest x15 147 us: trade(): return lax.ppermute(value, 'cols', [(at, at ^ step) for at in range(cols)])]
    pallas_call x0 -> x9, Pallas kernels: none -> 131 us  [the longest x4 83.8 us: transform_rows(): pl.pallas_call(functools.partial(row_kernel, cols, None), out_shape=(jax....]
    all_to_all x2 -> x4, starting transfers between devices: 12 us -> 37.2 us  [local(): lax.all_to_all(spectra, ('rows', 'cols'), split_axis=0, concat_axis=0, ti...]
    mul x3 -> x1, local copies, waits for them, and re-layouts: 23.6 us -> 0.09 us  [local(): ends.reshape(lines, -1, BLOCK_COLS) * end_scaling[:, :, None]]
    convert_element_type x1 -> x9, other arithmetic: 10.2 us -> 30.8 us  [the longest x4 16.3 us: local(): spectra = spectra.astype(jnp.float16)]
    concatenate x1 -> x0, local copies, waits for them, and re-layouts: 17.5 us -> none  [transform_rows(): jnp.concatenate((real_part.reshape(row_count, devices, slab), imag_part.r...]
  transfers between devices with their start and end apart: 4 -> 20, of which waited for: 3 -> 8; matrix products, arithmetic and copies ran while one was open for 1% -> 8% of each run, Pallas kernels for 0% -> 21%
where the time goes in v1:
time: 414 us; the launch traced here: 412 us
  waiting for transfers between devices  170 us (41%)
  Pallas kernels  131 us (32%)
  starting transfers between devices  58.1 us (14%)
  other arithmetic  31.6 us (8%)
  local copies, waits for them, and re-layouts  21 us (5%)
    ppermute x15, waiting for transfers between devices, trade(): return lax.ppermute(value, 'cols', [(at, at ^ step) for at in range(cols)])  147 us
    pallas_call x4, Pallas kernels, transform_rows(): pl.pallas_call(functools.partial(row_kernel, cols, None), out_shape=(jax....  83.8 us
    all_to_all x4, starting transfers between devices, local(): lax.all_to_all(spectra, ('rows', 'cols'), split_axis=0, concat_axis=0, ti...  37.2 us
    pallas_call x4, Pallas kernels, mix_columns(): pl.pallas_call(functools.partial(column_kernel, first), out_shape=jax.Sha...  31.7 us
    all_to_all x4, waiting for transfers between devices, local(): lax.all_to_all(spectra, ('rows', 'cols'), split_axis=0, concat_axis=0, ti...  22.9 us
    ppermute x15, starting transfers between devices, trade(): return lax.ppermute(value, 'cols', [(at, at ^ step) for at in range(cols)])  17.2 us
    convert_element_type x4, other arithmetic, local(): spectra = spectra.astype(jnp.float16)  16.3 us
    pallas_call x1, Pallas kernels, finish_columns(): pl.pallas_call(functools.partial(finish_kernel, outer), out_shape=(shape,...  15.3 us
  transfers between devices with their start and end apart: 20, of which 8 were waited for; matrix products, arithmetic and copies ran while one was open for 8% of the time, Pallas kernels for 21%

profile of v1, /device:TPU:17, one launch (start us, length us, event | category | flops | bytes accessed | tf_op | source)
XLA Modules:
  0.0 412.4 jit_solution(1836713952461421525)
XLA Ops:
  0.6 0.8 multiply_exponential_fusion
  1.4 0.1 constant_dynamic-slice_fusion.16
  1.5 1.2 slice.61
  2.7 0.1 mul.30
  2.8 0.1 fusion
  2.9 3.7 collective-permute-start
  6.7 4.0 fusion.1
  10.6 3.3 constant_dynamic-slice_fusion.11
  13.9 0.1 collective-permute-start.5
  14.0 2.4 collective-permute-start.6
  16.4 1.1 collective-permute-start.4
  17.5 0.1 copy.24
  17.6 0.3 broadcast_bitcast_fusion
  17.9 0.1 slice_bitcast_fusion
  18.1 0.0 collective-permute-done
  18.2 0.3 collective-permute-start.3
  18.4 1.1 collective-permute-start.1
  19.6 33.4 %collective-permute-done.1 = bf16[8,2048]{1,0:T(8,128)(2,1)S(1)} collective-permute-done((bf16[8,2048]{1,0:T(8,128)(2,1)S(1)}, bf16[8,2048]{1,0:T(8,128)(2,1)S(1)}, u32[]{:S(2)}, u32[]{:S(2)}) %collective-permute-start.1) | collective-permute-done | bytes 32800 | tf_op jit(solution)/shard_map/ppermute | solution.py:289
  53.0 0.5 collective-permute-start.2
  53.4 7.9 %collective-permute-done.2 = bf16[8,2048]{1,0:T(8,128)(2,1)S(1)} collective-permute-done((bf16[8,2048]{1,0:T(8,128)(2,1)S(1)}, bf16[8,2048]{1,0:T(8,128)(2,1)S(1)}, u32[]{:S(2)}, u32[]{:S(2)}) %collective-permute-start.2) | collective-permute-done | bytes 32800 | tf_op jit(solution)/shard_map/ppermute | solution.py:289
  61.4 2.6 collective-permute-done.3
  64.0 0.0 collective-permute-done.5.refs_2_
  64.0 0.0 collective-permute-done.4.refs_1_
  64.0 21.7 %row_transform.4 = (f32[8,4,2,128,128]{4,3,2,1,0:T(8,128)}, f32[8,8192]{1,0:T(8,128)S(1)}) custom-call(s32[1]{0:T(128)} %bitcast.z_ref, f32[8,8192]{1,0:T(8,128)S(1)} %get-tuple-element.27.scale_ref, f32[8,8192]{1,0:T(8,128)S(1)} %convert_dynamic-update-slice_fusion.1.halo_ref, bf16[128,256]{1,0:T(8,128)(2,1)S(1)} %copy-done.8, ...), custom_call_target="tpu_custom_call" | custom-call | flops 1610612736 | bytes 8388608 | tf_op jit(solution)/shard_map/row_transform/pallas_call | solution.py:141
  85.8 0.7 copy-done.11
  86.5 4.1 convert_element_type.62
  90.6 5.0 %all-to-all-start = ((f16[16,2,2,128,128]{4,3,2,1,0:T(8,128)(2,1)}), f16[16,2,2,128,128]{4,3,2,1,0:T(8,128)(2,1)}, u32[]{:S(2)}, u32[]{:S(2)}) async-start(f16[16,2,2,128,128]{4,3,2,1,0:T(8,128)(2,1)} %bitcast.105), calls=%async_computation | async-start | bytes 4194304 | tf_op jit(solution)/shard_map/all_to_all | solution.py:331
  95.6 3.0 constant_dynamic-slice_fusion.3
  98.6 1.4 collective-permute-start.7
  100.0 1.3 collective-permute-start.9
  101.3 40.8 %collective-permute-done.7.refs_1_ = bf16[128,2048]{1,0:T(8,128)(2,1)S(1)} collective-permute-done((bf16[128,2048]{1,0:T(8,128)(2,1)S(1)}, bf16[128,2048]{1,0:T(8,128)(2,1)S(1)}, u32[]{:S(2)}, u32[]{:S(2)}) %collective-permute-start.7) | collective-permute-done | bytes 524320 | tf_op jit(solution)/shard_map/ppermute | solution.py:289
  142.1 2.5 collective-permute-done.8.refs_2_
  144.5 0.0 collective-permute-done.9.refs_3_
  144.6 20.7 %row_transform.5 = (f32[8,4,2,128,128]{4,3,2,1,0:T(8,128)}, f32[8,8192]{1,0:T(8,128)S(1)}) custom-call(s32[1]{0:T(128)} %bitcast.z_ref, f32[8,8192]{1,0:T(8,128)S(1)} %get-tuple-element.26.scale_ref, f32[8,8192]{1,0:T(8,128)S(1)} %copy-done.12, bf16[128,256]{1,0:T(8,128)(2,1)S(1)} %copy-done.8, bf16[128,256]{1,0:T(8,128)(2,1)S(1)} %copy-done.7, ...), custom_call_target="tpu_custom_call" | custom-call | flops 1610612736 | bytes 8388608 | tf_op jit(solution)/shard_map/row_transform/pallas_call | solution.py:141
  165.3 4.1 %convert_element_type.64 = f16[8,4,2,128,128]{4,3,2,1,0:T(8,128)(2,1)} convert(f32[8,4,2,128,128]{4,3,2,1,0:T(8,128)} %get-tuple-element.11) | non-fusion elementwise | flops 1048576 | bytes 6291456 | tf_op jit(solution)/shard_map/convert_element_type | solution.py:323
  169.4 14.5 %all-to-all-start.1 = ((f16[16,2,2,128,128]{4,3,2,1,0:T(8,128)(2,1)}), f16[16,2,2,128,128]{4,3,2,1,0:T(8,128)(2,1)}, u32[]{:S(2)}, u32[]{:S(2)}) async-start(f16[16,2,2,128,128]{4,3,2,1,0:T(8,128)(2,1)} %bitcast.104), calls=%async_computation.1 | async-start | bytes 4194304 | tf_op jit(solution)/shard_map/all_to_all | solution.py:331
  183.9 4.2 %collective-permute-start.11 = (bf16[128,2048]{1,0:T(8,128)(2,1)}, bf16[128,2048]{1,0:T(8,128)(2,1)S(1)}, u32[]{:S(2)}, u32[]{:S(2)}) collective-permute-start(bf16[128,2048]{1,0:T(8,128)(2,1)} %bitcast.114), channel_id=1, source_target_pairs={{0,2},{1,3},{2,0},{3,1},{4,6},{5,7},{6,4},{7,5},{8,10},{9,11},{10,... | collective-permute-start | bytes 1572872 | tf_op jit(solution)/shard_map/ppermute | solution.py:289
  188.1 0.3 collective-permute-start.12
  188.4 1.1 collective-permute-start.10
  189.5 0.4 collective-permute-start.13
  189.9 3.2 collective-permute-start.14
  193.1 32.7 %collective-permute-done.11.refs_2_ = bf16[128,2048]{1,0:T(8,128)(2,1)S(1)} collective-permute-done((bf16[128,2048]{1,0:T(8,128)(2,1)}, bf16[128,2048]{1,0:T(8,128)(2,1)S(1)}, u32[]{:S(2)}, u32[]{:S(2)}) %collective-permute-start.11) | collective-permute-done | bytes 524320 | tf_op jit(solution)/shard_map/ppermute | solution.py:289
  225.7 27.2 %collective-permute-done.10.refs_1_ = bf16[128,2048]{1,0:T(8,128)(2,1)S(1)} collective-permute-done((bf16[128,2048]{1,0:T(8,128)(2,1)}, bf16[128,2048]{1,0:T(8,128)(2,1)S(1)}, u32[]{:S(2)}, u32[]{:S(2)}) %collective-permute-start.10) | collective-permute-done | bytes 524320 | tf_op jit(solution)/shard_map/ppermute | solution.py:289
  253.0 20.7 %row_transform.6 = (f32[8,4,2,128,128]{4,3,2,1,0:T(8,128)}, f32[8,8192]{1,0:T(8,128)S(1)}) custom-call(s32[1]{0:T(128)} %bitcast.z_ref, f32[8,8192]{1,0:T(8,128)S(1)} %get-tuple-element.25.scale_ref, f32[8,8192]{1,0:T(8,128)S(1)} %get-tuple-element.12.halo_ref, bf16[128,256]{1,0:T(8,128)(2,1)S(1)} %copy-done.8, bf16[128,256]{1,0:T(8,128)(2,1)S(1)} %copy-done.7, ...), custom_call_target="tpu_custom_call" | custom-call | flops 1610612736 | bytes 8388608 | tf_op jit(solution)/shard_map/row_transform/pallas_call | solution.py:141
  273.7 20.7 %row_transform.7 = (f32[8,4,2,128,128]{4,3,2,1,0:T(8,128)}, f32[8,8192]{1,0:T(8,128)}) custom-call(s32[1]{0:T(128)} %bitcast.z_ref, f32[8,8192]{1,0:T(8,128)S(1)} %get-tuple-element.24.scale_ref, f32[8,8192]{1,0:T(8,128)S(1)} %get-tuple-element.14.halo_ref, bf16[128,256]{1,0:T(8,128)(2,1)S(1)} %copy-done.8, bf16[128,256]{1,0:T(8,128)(2,1)S(1)} %copy-done.7, ...), custom_call_target="tpu_custom_call" | custom-call | flops 1610612736 | bytes 8388608 | tf_op jit(solution)/shard_map/row_transform/pallas_call | solution.py:141
  294.4 4.1 convert_element_type.68
  298.5 12.4 %all-to-all-start.3 = ((f16[16,2,2,128,128]{4,3,2,1,0:T(8,128)(2,1)}), f16[16,2,2,128,128]{4,3,2,1,0:T(8,128)(2,1)S(1)}, u32[]{:S(2)}, u32[]{:S(2)}) async-start(f16[16,2,2,128,128]{4,3,2,1,0:T(8,128)(2,1)} %bitcast.106), calls=%async_computation.3 | async-start | bytes 4194304 | tf_op jit(solution)/shard_map/all_to_all | solution.py:331
  310.9 4.0 convert_element_type.66
  314.9 22.9 %all-to-all-done.3 = f16[16,2,2,128,128]{4,3,2,1,0:T(8,128)(2,1)S(1)} async-done(((f16[16,2,2,128,128]{4,3,2,1,0:T(8,128)(2,1)}), f16[16,2,2,128,128]{4,3,2,1,0:T(8,128)(2,1)S(1)}, u32[]{:S(2)}, u32[]{:S(2)}) %all-to-all-start.3) | async-done | bytes 2097184 | tf_op jit(solution)/shard_map/all_to_all | solution.py:331
  337.8 5.2 %all-to-all-start.2 = ((f16[16,2,2,128,128]{4,3,2,1,0:T(8,128)(2,1)}), f16[16,2,2,128,128]{4,3,2,1,0:T(8,128)(2,1)}, u32[]{:S(2)}, u32[]{:S(2)}) async-start(f16[16,2,2,128,128]{4,3,2,1,0:T(8,128)(2,1)} %bitcast.33), calls=%async_computation.2 | async-start | bytes 4194304 | tf_op jit(solution)/shard_map/all_to_all | solution.py:331
  342.9 4.0 convert_element_type.65.in_ref
  346.9 4.0 convert_element_type.63.in_ref
  350.9 2.4 convert_element_type.69.in_ref
  353.3 7.9 %column_mix.5.refs_1_ = f32[16,2,256,128]{3,2,1,0:T(8,128)S(1)} custom-call(bf16[256,256]{1,0:T(8,128)(2,1)S(1)} %copy-done.6, bf16[256,256]{1,0:T(8,128)(2,1)S(1)} %copy-done.5, f32[64,128]{1,0:T(8,128)S(1)} %copy-done.10, f32[64,128]{1,0:T(8,128)S(1)} %copy-done.9, f32[16,2,2,128,128]{4,3,2,1,0:T(8,128)} %convert_element_type.65.in_ref), custom_call_target="tpu_custom_call" | custom-call | flops 3221225472 | bytes 8388608 | tf_op jit(solution)/shard_map/column_mix/pallas_call | solution.py:184
  361.2 2.0 copy-done
  363.2 7.9 %column_mix.4.refs_0_ = f32[16,2,256,128]{3,2,1,0:T(8,128)S(1)} custom-call(bf16[256,256]{1,0:T(8,128)(2,1)S(1)} %copy-done.6, bf16[256,256]{1,0:T(8,128)(2,1)S(1)} %copy-done.5, f32[64,128]{1,0:T(8,128)S(1)} %copy-done.10, f32[64,128]{1,0:T(8,128)S(1)} %copy-done.9, f32[16,2,2,128,128]{4,3,2,1,0:T(8,128)} %convert_element_type.63.in_ref), custom_call_target="tpu_custom_call" | custom-call | flops 3221225472 | bytes 8388608 | tf_op jit(solution)/shard_map/column_mix/pallas_call | solution.py:184
  371.1 0.0 copy-start.1
  371.1 2.0 copy-done.1
  373.1 7.9 %column_mix.7.refs_3_ = f32[16,2,256,128]{3,2,1,0:T(8,128)S(1)} custom-call(bf16[256,256]{1,0:T(8,128)(2,1)S(1)} %copy-done.6, bf16[256,256]{1,0:T(8,128)(2,1)S(1)} %copy-done.5, f32[64,128]{1,0:T(8,128)S(1)} %copy-done.10, f32[64,128]{1,0:T(8,128)S(1)} %copy-done.9, f32[16,2,2,128,128]{4,3,2,1,0:T(8,128)} %convert_element_type.69.in_ref), custom_call_target="tpu_custom_call" | custom-call | flops 3221225472 | bytes 8388608 | tf_op jit(solution)/shard_map/column_mix/pallas_call | solution.py:184
  381.0 2.0 copy-done.3
  383.0 4.0 convert_element_type.67.in_ref
  387.0 8.0 %column_mix.6.refs_2_ = f32[16,2,256,128]{3,2,1,0:T(8,128)S(1)} custom-call(bf16[256,256]{1,0:T(8,128)(2,1)S(1)} %copy-done.6, bf16[256,256]{1,0:T(8,128)(2,1)S(1)} %copy-done.5, f32[64,128]{1,0:T(8,128)S(1)} %copy-done.10, f32[64,128]{1,0:T(8,128)S(1)} %copy-done.9, f32[16,2,2,128,128]{4,3,2,1,0:T(8,128)} %convert_element_type.67.in_ref), custom_call_target="tpu_custom_call" | custom-call | flops 3221225472 | bytes 8388608 | tf_op jit(solution)/shard_map/column_mix/pallas_call | solution.py:184
  395.0 2.0 copy-done.4
  397.1 15.3 %column_finish.1 = (f32[256,8192]{1,0:T(8,128)}, f32[256,8192]{1,0:T(8,128)}) custom-call(f32[16,2,256,128]{3,2,1,0:T(8,128)S(1)} %copy-done.2, f32[16,2,256,128]{3,2,1,0:T(8,128)} %copy-done, f32[16,2,256,128]{3,2,1,0:T(8,128)} %copy-done.4, f32[16,2,256,128]{3,2,1,0:T(8,128)} %copy-done.3), custom_call_target="tpu_custom_call" | custom-call | tf_op jit(solution)/shard_map/column_finish/pallas_call | solution.py:232
  (51 shorter events, 0.2 us)
Async XLA Ops:
  2.9 15.2 %collective-permute-start = (bf16[1,2048]{1,0:T(2,128)(2,1)S(1)}, bf16[1,2048]{1,0:T(2,128)(2,1)S(1)}, u32[]{:S(2)}, u32[]{:S(2)}) collective-permute-start(bf16[1,2048]{1,0:T(2,128)(2,1)S(1)} %slice.63), channel_id=1, source_target_pairs={{0,4},{4,8},{8,12},{12,16},{16,20},{20,24},{24,28},{1,5},{5,9},{9,... | collective-permute-start | bytes 12296 | tf_op jit(solution)/shard_map/ppermute | solution.py:297
  10.6 7.4 %copy-start.16 = (f32[2,64,128]{2,1,0:T(8,128)S(1)}, f32[2,64,128]{2,1,0:T(8,128)}, u32[]{:S(2)}) copy-start(f32[2,64,128]{2,1,0:T(8,128)} %constant.177.clone) | copy-start | bytes 196612
  10.6 7.4 %copy-start.17 = (f32[2,64,128]{2,1,0:T(8,128)S(1)}, f32[2,64,128]{2,1,0:T(8,128)}, u32[]{:S(2)}) copy-start(f32[2,64,128]{2,1,0:T(8,128)} %constant.176.clone) | copy-start | bytes 196612
  13.9 50.1 %copy-start.7 = (bf16[128,256]{1,0:T(8,128)(2,1)S(1)}, bf16[128,256]{1,0:T(8,128)(2,1)}, u32[]{:S(2)}) copy-start(bf16[128,256]{1,0:T(8,128)(2,1)} %constant.179.clone.low_ref) | copy-start | bytes 196612
  13.9 50.1 %copy-start.8 = (bf16[128,256]{1,0:T(8,128)(2,1)S(1)}, bf16[128,256]{1,0:T(8,128)(2,1)}, u32[]{:S(2)}) copy-start(bf16[128,256]{1,0:T(8,128)(2,1)} %constant.178.clone.high_ref) | copy-start | bytes 196612
  13.9 50.1 %collective-permute-start.5 = (bf16[128,2048]{1,0:T(8,128)(2,1)}, bf16[128,2048]{1,0:T(8,128)(2,1)S(1)}, u32[]{:S(2)}, u32[]{:S(2)}) collective-permute-start(bf16[128,2048]{1,0:T(8,128)(2,1)} %bitcast.19), channel_id=1, source_target_pairs={{0,2},{1,3},{2,0},{3,1},{4,6},{5,7},{6,4},{7,5},{8,10},{9,11},{10,... | collective-permute-start | bytes 1572872 | tf_op jit(solution)/shard_map/ppermute | solution.py:289
  14.0 50.0 %collective-permute-start.6 = (bf16[128,2048]{1,0:T(8,128)(2,1)}, bf16[128,2048]{1,0:T(8,128)(2,1)S(1)}, u32[]{:S(2)}, u32[]{:S(2)}) collective-permute-start(bf16[128,2048]{1,0:T(8,128)(2,1)} %bitcast.20), channel_id=1, source_target_pairs={{0,3},{1,2},{2,1},{3,0},{4,7},{5,6},{6,5},{7,4},{8,11},{9,10},{10,... | collective-permute-start | bytes 1572872 | tf_op jit(solution)/shard_map/ppermute | solution.py:289
  16.4 47.6 %collective-permute-start.4 = (bf16[128,2048]{1,0:T(8,128)(2,1)}, bf16[128,2048]{1,0:T(8,128)(2,1)}, u32[]{:S(2)}, u32[]{:S(2)}) collective-permute-start(bf16[128,2048]{1,0:T(8,128)(2,1)} %bitcast.18), channel_id=1, source_target_pairs={{0,1},{1,0},{2,3},{3,2},{4,5},{5,4},{6,7},{7,6},{8,9},{9,8},{10,11... | collective-permute-start | bytes 1572872 | tf_op jit(solution)/shard_map/ppermute | solution.py:289
  18.2 45.8 %collective-permute-start.3 = (bf16[8,2048]{1,0:T(8,128)(2,1)S(1)}, bf16[8,2048]{1,0:T(8,128)(2,1)S(1)}, u32[]{:S(2)}, u32[]{:S(2)}) collective-permute-start(bf16[8,2048]{1,0:T(8,128)(2,1)S(1)} %get-tuple-element.40), channel_id=1, source_target_pairs={{0,3},{1,2},{2,1},{3,0},{4,7},{5,6},{6,5},{7,4},{8,11},{9,10},{10,... | collective-permute-start | bytes 98312 | tf_op jit(solution)/shard_map/ppermute | solution.py:289
  18.4 34.5 %collective-permute-start.1 = (bf16[8,2048]{1,0:T(8,128)(2,1)S(1)}, bf16[8,2048]{1,0:T(8,128)(2,1)S(1)}, u32[]{:S(2)}, u32[]{:S(2)}) collective-permute-start(bf16[8,2048]{1,0:T(8,128)(2,1)S(1)} %get-tuple-element.42), channel_id=1, source_target_pairs={{0,1},{1,0},{2,3},{3,2},{4,5},{5,4},{6,7},{7,6},{8,9},{9,8},{10,11... | collective-permute-start | bytes 98312 | tf_op jit(solution)/shard_map/ppermute | solution.py:289
  53.0 8.4 %collective-permute-start.2 = (bf16[8,2048]{1,0:T(8,128)(2,1)S(1)}, bf16[8,2048]{1,0:T(8,128)(2,1)S(1)}, u32[]{:S(2)}, u32[]{:S(2)}) collective-permute-start(bf16[8,2048]{1,0:T(8,128)(2,1)S(1)} %get-tuple-element.41), channel_id=1, source_target_pairs={{0,2},{1,3},{2,0},{3,1},{4,6},{5,7},{6,4},{7,5},{8,10},{9,11},{10,... | collective-permute-start | bytes 98312 | tf_op jit(solution)/shard_map/ppermute | solution.py:289
  85.8 0.7 copy-start.11
  86.5 9.1 %copy-start.13 = (bf16[2,8,1,16,2048]{4,3,2,1,0:T(8,128)(2,1)S(1)}, bf16[2,8,1,16,2048]{4,3,2,1,0:T(8,128)(2,1)}, u32[]{:S(2)}) copy-start(bf16[2,8,1,16,2048]{4,3,2,1,0:T(8,128)(2,1)} %get-tuple-element.17) | copy-start | bytes 3145732
  90.6 78.8 %all-to-all-start = ((f16[16,2,2,128,128]{4,3,2,1,0:T(8,128)(2,1)}), f16[16,2,2,128,128]{4,3,2,1,0:T(8,128)(2,1)}, u32[]{:S(2)}, u32[]{:S(2)}) async-start(f16[16,2,2,128,128]{4,3,2,1,0:T(8,128)(2,1)} %bitcast.105), calls=%async_computation | async-start | bytes 4194304 | tf_op jit(solution)/shard_map/all_to_all | solution.py:331
  95.6 49.0 %copy-start.12 = (f32[8,8192]{1,0:T(8,128)S(1)}, f32[8,8192]{1,0:T(8,128)}, u32[]{:S(2)}) copy-start(f32[8,8192]{1,0:T(8,128)} %copy-done.11) | copy-start | bytes 786436
  98.6 43.4 %collective-permute-start.7 = (bf16[128,2048]{1,0:T(8,128)(2,1)S(1)}, bf16[128,2048]{1,0:T(8,128)(2,1)S(1)}, u32[]{:S(2)}, u32[]{:S(2)}) collective-permute-start(bf16[128,2048]{1,0:T(8,128)(2,1)S(1)} %bitcast.117), channel_id=1, source_target_pairs={{0,1},{1,0},{2,3},{3,2},{4,5},{5,4},{6,7},{7,6},{8,9},{9,8},{10,11... | collective-permute-start | bytes 1572872 | tf_op jit(solution)/shard_map/ppermute | solution.py:289
  100.0 44.5 %collective-permute-start.8 = (bf16[128,2048]{1,0:T(8,128)(2,1)S(1)}, bf16[128,2048]{1,0:T(8,128)(2,1)S(1)}, u32[]{:S(2)}, u32[]{:S(2)}) collective-permute-start(bf16[128,2048]{1,0:T(8,128)(2,1)S(1)} %bitcast.116), channel_id=1, source_target_pairs={{0,2},{1,3},{2,0},{3,1},{4,6},{5,7},{6,4},{7,5},{8,10},{9,11},{10,... | collective-permute-start | bytes 1572872 | tf_op jit(solution)/shard_map/ppermute | solution.py:289
  100.0 44.5 %collective-permute-start.9 = (bf16[128,2048]{1,0:T(8,128)(2,1)S(1)}, bf16[128,2048]{1,0:T(8,128)(2,1)S(1)}, u32[]{:S(2)}, u32[]{:S(2)}) collective-permute-start(bf16[128,2048]{1,0:T(8,128)(2,1)S(1)} %bitcast.115), channel_id=1, source_target_pairs={{0,3},{1,2},{2,1},{3,0},{4,7},{5,6},{6,5},{7,4},{8,11},{9,10},{10,... | collective-permute-start | bytes 1572872 | tf_op jit(solution)/shard_map/ppermute | solution.py:289
  165.2 24.6 %copy-start.15 = (bf16[1,8,1,16,2048]{4,3,2,1,0:T(8,128)(2,1)S(1)}, bf16[1,8,1,16,2048]{4,3,2,1,0:T(8,128)(2,1)}, u32[]{:S(2)}) copy-start(bf16[1,8,1,16,2048]{4,3,2,1,0:T(8,128)(2,1)} %get-tuple-element.49) | copy-start | bytes 1572868
  165.3 60.5 %copy-start.14 = (bf16[1,8,1,16,2048]{4,3,2,1,0:T(8,128)(2,1)S(1)}, bf16[1,8,1,16,2048]{4,3,2,1,0:T(8,128)(2,1)}, u32[]{:S(2)}) copy-start(bf16[1,8,1,16,2048]{4,3,2,1,0:T(8,128)(2,1)} %get-tuple-element.50) | copy-start | bytes 1572868
  169.4 129.1 %all-to-all-start.1 = ((f16[16,2,2,128,128]{4,3,2,1,0:T(8,128)(2,1)}), f16[16,2,2,128,128]{4,3,2,1,0:T(8,128)(2,1)}, u32[]{:S(2)}, u32[]{:S(2)}) async-start(f16[16,2,2,128,128]{4,3,2,1,0:T(8,128)(2,1)} %bitcast.104), calls=%async_computation.1 | async-start | bytes 4194304 | tf_op jit(solution)/shard_map/all_to_all | solution.py:331
  183.9 41.8 %collective-permute-start.11 = (bf16[128,2048]{1,0:T(8,128)(2,1)}, bf16[128,2048]{1,0:T(8,128)(2,1)S(1)}, u32[]{:S(2)}, u32[]{:S(2)}) collective-permute-start(bf16[128,2048]{1,0:T(8,128)(2,1)} %bitcast.114), channel_id=1, source_target_pairs={{0,2},{1,3},{2,0},{3,1},{4,6},{5,7},{6,4},{7,5},{8,10},{9,11},{10,... | collective-permute-start | bytes 1572872 | tf_op jit(solution)/shard_map/ppermute | solution.py:289
  188.1 37.6 %collective-permute-start.12 = (bf16[128,2048]{1,0:T(8,128)(2,1)}, bf16[128,2048]{1,0:T(8,128)(2,1)S(1)}, u32[]{:S(2)}, u32[]{:S(2)}) collective-permute-start(bf16[128,2048]{1,0:T(8,128)(2,1)} %bitcast.113), channel_id=1, source_target_pairs={{0,3},{1,2},{2,1},{3,0},{4,7},{5,6},{6,5},{7,4},{8,11},{9,10},{10,... | collective-permute-start | bytes 1572872 | tf_op jit(solution)/shard_map/ppermute | solution.py:289
  188.4 64.6 %collective-permute-start.10 = (bf16[128,2048]{1,0:T(8,128)(2,1)}, bf16[128,2048]{1,0:T(8,128)(2,1)S(1)}, u32[]{:S(2)}, u32[]{:S(2)}) collective-permute-start(bf16[128,2048]{1,0:T(8,128)(2,1)} %bitcast.112), channel_id=1, source_target_pairs={{0,1},{1,0},{2,3},{3,2},{4,5},{5,4},{6,7},{7,6},{8,9},{9,8},{10,11... | collective-permute-start | bytes 1572872 | tf_op jit(solution)/shard_map/ppermute | solution.py:289
  189.5 84.2 %collective-permute-start.13 = (bf16[128,2048]{1,0:T(8,128)(2,1)}, bf16[128,2048]{1,0:T(8,128)(2,1)S(1)}, u32[]{:S(2)}, u32[]{:S(2)}) collective-permute-start(bf16[128,2048]{1,0:T(8,128)(2,1)} %bitcast.111), channel_id=1, source_target_pairs={{0,1},{1,0},{2,3},{3,2},{4,5},{5,4},{6,7},{7,6},{8,9},{9,8},{10,11... | collective-permute-start | bytes 1572872 | tf_op jit(solution)/shard_map/ppermute | solution.py:289
  189.9 83.8 %collective-permute-start.14 = (bf16[128,2048]{1,0:T(8,128)(2,1)S(1)}, bf16[128,2048]{1,0:T(8,128)(2,1)S(1)}, u32[]{:S(2)}, u32[]{:S(2)}) collective-permute-start(bf16[128,2048]{1,0:T(8,128)(2,1)S(1)} %bitcast.110), channel_id=1, source_target_pairs={{0,2},{1,3},{2,0},{3,1},{4,6},{5,7},{6,4},{7,5},{8,10},{9,11},{10,... | collective-permute-start | bytes 1572872 | tf_op jit(solution)/shard_map/ppermute | solution.py:289
  225.7 48.0 %collective-permute-start.15 = (bf16[128,2048]{1,0:T(8,128)(2,1)S(1)}, bf16[128,2048]{1,0:T(8,128)(2,1)S(1)}, u32[]{:S(2)}, u32[]{:S(2)}) collective-permute-start(bf16[128,2048]{1,0:T(8,128)(2,1)S(1)} %bitcast.109), channel_id=1, source_target_pairs={{0,3},{1,2},{2,1},{3,0},{4,7},{5,6},{6,5},{7,4},{8,11},{9,10},{10,... | collective-permute-start | bytes 1572872 | tf_op jit(solution)/shard_map/ppermute | solution.py:289
  298.5 39.3 %all-to-all-start.3 = ((f16[16,2,2,128,128]{4,3,2,1,0:T(8,128)(2,1)}), f16[16,2,2,128,128]{4,3,2,1,0:T(8,128)(2,1)S(1)}, u32[]{:S(2)}, u32[]{:S(2)}) async-start(f16[16,2,2,128,128]{4,3,2,1,0:T(8,128)(2,1)} %bitcast.106), calls=%async_computation.3 | async-start | bytes 4194304 | tf_op jit(solution)/shard_map/all_to_all | solution.py:331
  337.8 45.2 %all-to-all-start.2 = ((f16[16,2,2,128,128]{4,3,2,1,0:T(8,128)(2,1)}), f16[16,2,2,128,128]{4,3,2,1,0:T(8,128)(2,1)}, u32[]{:S(2)}, u32[]{:S(2)}) async-start(f16[16,2,2,128,128]{4,3,2,1,0:T(8,128)(2,1)} %bitcast.33), calls=%async_computation.2 | async-start | bytes 4194304 | tf_op jit(solution)/shard_map/all_to_all | solution.py:331
  350.9 2.4 copy-start.5
  350.9 2.4 copy-start.6
  350.9 2.4 copy-start.9
  350.9 2.4 copy-start.10
  361.2 2.0 copy-start
  371.1 2.0 copy-start.1
  381.0 2.0 copy-start.3
  387.0 10.1 %copy-start.2 = (f32[16,2,256,128]{3,2,1,0:T(8,128)S(1)}, f32[16,2,256,128]{3,2,1,0:T(8,128)}, u32[]{:S(2)}) copy-start(f32[16,2,256,128]{3,2,1,0:T(8,128)} %copy-done.1) | copy-start | bytes 12582916
  395.0 2.1 copy-start.4

commit v2 on v1

--- a/solution.py
+++ b/solution.py
@@ -12,6 +12,7 @@
 LANES = 128
 BLOCK_ROWS = 16
 BLOCK_COLS = 128
+UNITS = 2048
 f32 = jnp.float32
 bf16 = jnp.bfloat16
 
@@ -32,6 +33,9 @@
 
 def product3(value, high, low):
     value_high, value_low = split(value)
+    if value.shape[1] == LANES:
+        both = jnp.concatenate((value_high, value_low), axis=1)
+        return product(both, jnp.concatenate((high, high), axis=0)) + product(value_high, low)
     return product(value_high, high) + product(value_low, high) + product(value_high, low)
 
 
@@ -69,38 +73,94 @@
     return (low + high)[:keep]
 
 
-def row_kernel(
-    cols, group, z_ref, scale_ref, halo_ref, high_ref, low_ref, cos_ref, sin_ref, *refs
-):
-    pieces, (out_ref, last_ref, table, mixed, stage) = refs[:cols], refs[cols:]
+def step_kernel(first, z_ref, scale_ref, before_scale_ref, halo_ref, now_ref, before_ref, out_ref):
+    lines, _, segment, width = now_ref.shape[1:]
+    groups = segment // BLOCK_ROWS
+    starts = lax.broadcasted_iota(jnp.int32, (segment, LANES), 0) == 0
+
+    def take(block, carry):
+        here = pl.ds(pl.multiple_of(block * LANES, LANES), LANES)
+        last = halo_ref[0, :, here]
+        for line in range(lines):
+            value = now_ref[0, line, 0, :, here].astype(f32).reshape(groups, BLOCK_ROWS, LANES)
+            scale = scale_ref[0, line * groups : (line + 1) * groups, here]
+            value = (value * scale[:, None, :]).reshape(segment, LANES)
+            ends = before_ref[0, line, 0, segment - BLOCK_ROWS : segment, here].astype(f32)
+            ends = ends[BLOCK_ROWS - 1 : BLOCK_ROWS] * before_scale_ref[0, (line + 1) * groups - 1 : (line + 1) * groups, here]
+            above = last if first else ends
+            last = ends
+            change = value - jnp.where(starts, above, pltpu.roll(value, 1, 0))
+            out_ref[0, line * segment : (line + 1) * segment, here] = change.astype(jnp.int32).astype(jnp.int16)
+        return carry
+
+    lax.fori_loop(0, width // LANES, take, 0)
+
+
+def step_rows(z, by_kind, scales, halo, chunk):
+    kinds, lines, chunks, segment, width = by_kind.shape
+    before = (chunk - 1) % chunks
+    kind = lambda k, z: lax.rem(lax.bitwise_xor(z[0], k), kinds)
+    block = (1, lines, 1, segment, width)
+    row_block = (1,) + scales.shape[2:]
+    return pl.pallas_call(
+        functools.partial(step_kernel, chunk == 0),
+        out_shape=jax.ShapeDtypeStruct((kinds, lines * segment, width), jnp.int16),
+        grid_spec=pltpu.PrefetchScalarGridSpec(
+            num_scalar_prefetch=1,
+            grid=(kinds,),
+            in_specs=[
+                pl.BlockSpec(row_block, lambda k, z: (kind(k, z), 0, 0)),
+                pl.BlockSpec(row_block, lambda k, z: (kind(k, z), 0, 0)),
+                pl.BlockSpec((1, 1, width), lambda k, z: (kind(k, z), 0, 0)),
+                pl.BlockSpec(block, lambda k, z: (kind(k, z), 0, chunk, 0, 0)),
+                pl.BlockSpec(block, lambda k, z: (kind(k, z), 0, before, 0, 0)),
+            ],
+            out_specs=pl.BlockSpec((1, lines * segment, width), lambda k, z: (k, 0, 0)),
+        ),
+        compiler_params=pltpu.CompilerParams(vmem_limit_bytes=32 * 1024 * 1024),
+        cost_estimate=pl.CostEstimate(
+            flops=0, bytes_accessed=1024, transcendentals=0
+        ),
+        name="step_rows",
+    )(z, scales[chunk], scales[before], halo, by_kind, by_kind)
+
+
+SMALLEST = -22
+STEPS = 32000.0 / (15 - SMALLEST)
+
+
+def encode(value):
+    size = jnp.maximum(jnp.abs(value), 2.0 ** SMALLEST)
+    code = (jnp.log2(size) - SMALLEST) * STEPS + 0.5
+    return jnp.where(value < 0, -code, code).astype(jnp.int32).astype(jnp.int16)
+
+
+def decode(code):
+    code = code.astype(jnp.int32).astype(f32)
+    size = jnp.abs(code)
+    value = jnp.where(size > 0, jnp.exp2(size * (1 / STEPS) + SMALLEST), 0.0)
+    return jnp.where(code < 0, -value, value)
+
+
+def row_kernel(cols, z_ref, high_ref, low_ref, cos_ref, sin_ref, *refs):
+    pieces, (out_ref, table, mixed, stage) = refs[:cols], refs[cols:]
     rows, piece_cols = pieces[0].shape
-    halos = halo_ref.shape[0]
-    segment = rows // halos
-    scales = rows // BLOCK_ROWS
     outer = cos_ref.shape[0]
     slabs, kept = out_ref.shape[:2]
     pad = table.shape[0] - outer * LANES
     z = z_ref[0]
     table[0:pad, :] = jnp.zeros((pad, rows), f32)
-    starts = lax.broadcasted_iota(jnp.int32, (rows, LANES), 0) % segment == 0
 
     for step, piece in enumerate(pieces):
         base = lax.bitwise_xor(z, step) * piece_cols
 
-        def dequantize(block, carry, piece=piece, base=base):
+        def turn(block, carry, piece=piece, base=base):
             here = pl.multiple_of(block * LANES, LANES)
-            there = pl.multiple_of(base + here, LANES)
-            value = piece[:, pl.ds(here, LANES)].astype(f32).reshape(scales, BLOCK_ROWS, LANES)
-            value = (value * scale_ref[:, pl.ds(there, LANES)][:, None, :]).reshape(rows, LANES)
-            halo = jnp.broadcast_to(
-                halo_ref[:, pl.ds(there, LANES)][:, None, :], (halos, segment, LANES)
-            ).reshape(rows, LANES)
-            above = jnp.where(starts, halo, pltpu.roll(value, 1, 0))
-            last_ref[:, pl.ds(there, LANES)] = value.reshape(halos, segment, LANES)[:, segment - 1, :]
-            table[pl.ds(pl.multiple_of(pad + there, 8), LANES), :] = (value - above).T
+            value = piece[:, pl.ds(here, LANES)].astype(jnp.int32).astype(f32)
+            table[pl.ds(pl.multiple_of(pad + base + here, 8), LANES), :] = value.T
             return carry
 
-        lax.fori_loop(0, piece_cols // LANES, dequantize, 0, unroll=2)
+        lax.fori_loop(0, piece_cols // LANES, turn, 0, unroll=8)
 
     def mix(index, carry):
         now = table[pl.ds(pad + index, LANES, stride=outer), :]
@@ -112,12 +172,12 @@
         mixed[index, 1] = imag * cos - real * sin
         return carry
 
-    lax.fori_loop(0, outer, mix, 0, unroll=2)
+    lax.fori_loop(0, outer, mix, 0, unroll=8)
 
     inner = outer // slabs
 
     def finish(tile, carry):
-        here = pl.ds(pl.multiple_of(tile * 8, 8), 8)
+        here = pl.ds(pl.multiple_of(tile * 16, 16), 16)
         for low in range(slabs):
             values = [
                 (mixed[high * slabs + low, 0, here, :], mixed[high * slabs + low, 1, here, :])
@@ -127,43 +187,46 @@
                 stage[k, low, 0], stage[k, low, 1] = times(value, low * k, outer)
         for k in range(kept):
             for slab, value in enumerate(dft([(stage[k, low, 0], stage[k, low, 1]) for low in range(slabs)])):
-                out_ref[slab, k, 0, here, :], out_ref[slab, k, 1, here, :] = value
-        return carry
-
-    lax.fori_loop(0, rows // 8, finish, 0)
-
-
-def transform_rows(z, pieces, scale, halo, tables, slabs, kept, outer):
+                out_ref[slab, k, 0, here, :], out_ref[slab, k, 1, here, :] = encode(value[0]), encode(value[1])
+        return carry
+
+    lax.fori_loop(0, rows // 16, finish, 0)
+
+
+def transform_rows(z, pieces, tables, slabs, kept, outer):
     rows, piece_cols = pieces[0].shape
     cols = len(pieces)
     total = cols * piece_cols
     vmem = pl.BlockSpec(memory_space=pltpu.VMEM)
     return pl.pallas_call(
-        functools.partial(row_kernel, cols, None),
-        out_shape=(
-            jax.ShapeDtypeStruct((slabs, kept, 2, rows, LANES), f32),
-            jax.ShapeDtypeStruct(halo.shape, f32),
-        ),
-        in_specs=[pl.BlockSpec(memory_space=pltpu.SMEM)] + [vmem] * (6 + cols),
-        out_specs=(vmem, vmem),
+        functools.partial(row_kernel, cols),
+        out_shape=jax.ShapeDtypeStruct((slabs, kept, 2, rows, LANES), jnp.int16),
+        in_specs=[pl.BlockSpec(memory_space=pltpu.SMEM)] + [vmem] * (4 + cols),
+        out_specs=vmem,
         scratch_shapes=[
             pltpu.VMEM((8 + total, rows), f32),
             pltpu.VMEM((outer, 2, rows, LANES), f32),
-            pltpu.VMEM((kept, slabs, 2, 8, LANES), f32),
+            pltpu.VMEM((kept, slabs, 2, 16, LANES), f32),
         ],
         compiler_params=pltpu.CompilerParams(vmem_limit_bytes=48 * 1024 * 1024),
         cost_estimate=pl.CostEstimate(
-            flops=12 * rows * total * LANES, bytes_accessed=rows * total * 8, transcendentals=0
+            flops=800 * rows * total * LANES, bytes_accessed=rows * total * 8, transcendentals=0
         ),
         name="row_transform",
-    )(z, scale, halo, *tables, *pieces)
+    )(z, *tables, *pieces)
 
 
 def column_kernel(first, high_ref, low_ref, cos_ref, sin_ref, in_ref, out_ref, real, imag):
     sources, _, _, rows, width = in_ref.shape
     count = out_ref.shape[0]
-    real[...] = in_ref[:, 0, 0].reshape(sources * rows, width)
-    imag[...] = in_ref[:, 0, 1].reshape(sources * rows, width)
+
+    def take(source, carry):
+        here = pl.ds(pl.multiple_of(source * rows, rows), rows)
+        real[here, :] = decode(in_ref[source, 0, 0])
+        imag[here, :] = decode(in_ref[source, 0, 1])
+        return carry
+
+    lax.fori_loop(0, sources, take, 0)
 
     def mix(index, carry):
         here = pl.ds(index, LANES, stride=count)
@@ -175,7 +238,7 @@
         out_ref[index, 1] = spun_imag * cos - spun_real * sin
         return carry
 
-    lax.fori_loop(0, count, mix, 0, unroll=2)
+    lax.fori_loop(0, count, mix, 0, unroll=8)
 
 
 def mix_columns(gathered, tables, first, count):
@@ -189,9 +252,9 @@
         + [pl.BlockSpec((sources, 1, 2, rows, width), lambda plane: (0, plane, 0, 0, 0))],
         out_specs=pl.BlockSpec((count, 2, width, LANES), lambda plane: (0, 0, plane, 0)),
         scratch_shapes=[pltpu.VMEM((sources * rows, width), f32)] * 2,
-        compiler_params=pltpu.CompilerParams(vmem_limit_bytes=48 * 1024 * 1024),
+        compiler_params=pltpu.CompilerParams(vmem_limit_bytes=56 * 1024 * 1024),
         cost_estimate=pl.CostEstimate(
-            flops=24 * gathered.size * LANES, bytes_accessed=gathered.size * 8, transcendentals=0
+            flops=0, bytes_accessed=1024, transcendentals=0
         ),
         name="column_mix",
     )(*tables, gathered)
@@ -268,71 +331,68 @@
     twist = np.arange(outer)[None, :, None] * (index[None, None, :] + sides) % total
     twist = 2 * np.pi * twist / total
     own_side = lambda table: lax.dynamic_index_in_dim(jnp.asarray(table, f32), side, 0, False)
-    row_tables = (*split_np(row_matrix), own_side(np.cos(twist)), own_side(np.sin(twist)))
+    row_tables = (*split_np(row_matrix / UNITS), own_side(np.cos(twist)), own_side(np.sin(twist)))
     column_tables = (
         *split_np(column_matrix),
         np.asarray(np.cos(twist[0]) / total, np.float32),
         np.asarray(np.sin(twist[0]) / total, np.float32),
     )
 
+    scaling = jnp.exp2(exponents.astype(f32)) * UNITS
+    scaling = lax.dynamic_slice_in_dim(scaling, z * (local_cols // BLOCK_COLS), local_cols // BLOCK_COLS, 1)
+    scales = scaling.reshape(half, kind_lines, chunks, count // BLOCK_ROWS, -1).transpose(2, 0, 1, 3, 4)
+    scales = jnp.repeat(scales.reshape(chunks, half, kind_lines * (count // BLOCK_ROWS), -1), BLOCK_COLS, axis=-1)
+
     by_kind = mantissa.reshape(half, kind_lines, chunks, count, local_cols)
-
-    def raw_piece(chunk, step):
-        target_kind = lax.bitwise_xor(z, step) % half
-        piece = lax.dynamic_index_in_dim(by_kind[:, :, chunk], target_kind, 0, False)
-        piece = piece.reshape(chunk_rows, local_cols)
-        return trade(piece, step)
-
-    def trade(value, step):
-        if step == 0:
-            return value
-        return lax.ppermute(value, "cols", [(at, at ^ step) for at in range(cols)])
-
-    scaling = jnp.exp2(exponents.astype(f32))
-    own_scaling = lax.dynamic_slice_in_dim(scaling, z * (local_cols // BLOCK_COLS), local_cols // BLOCK_COLS, 1)
-    ends = mantissa.reshape(lines, outer, local_cols)[:, -1].astype(f32)
-    end_scaling = own_scaling.reshape(lines, outer // BLOCK_ROWS, -1)[:, -1]
-    ends = (ends.reshape(lines, -1, BLOCK_COLS) * end_scaling[:, :, None]).reshape(lines, local_cols)
-    ends = ends.astype(bf16)
-    above = lax.ppermute(ends[-1:], "rows", [(at, at + 1) for at in range(slabs - 1)])
-    above = jnp.concatenate((above, ends[:-1]), axis=0).reshape(half, kind_lines, local_cols)
-    raw = [[raw_piece(chunk, step) for step in range(cols)] for chunk in range(chunks)]
-    halos = [
-        trade(lax.dynamic_index_in_dim(above, lax.bitwise_xor(z, step) % half, 0, False), step)
-        for step in range(cols)
-    ]
-    halo = jnp.zeros((kind_lines, total), f32)
-    for step in range(cols):
-        at = lax.bitwise_xor(z, step) * local_cols
-        halo = lax.dynamic_update_slice_in_dim(halo, halos[step].astype(f32), at, 1)
-
-    own_rows = lax.dynamic_index_in_dim(
-        scaling.reshape(half, kind_lines, chunks, count // BLOCK_ROWS, -1), kind, 0, False
-    )
-    own_rows = jnp.repeat(own_rows, BLOCK_COLS, axis=-1)
-
+    ends = by_kind[:, -1, -1, -1].astype(f32) * scales[-1, :, -1]
+    above = lax.ppermute(ends[-1:].astype(bf16), "rows", [(at, at + 1) for at in range(slabs - 1)])
+    halo = jnp.concatenate((above.astype(f32), ends[:-1]), axis=0).reshape(half, 1, local_cols)
+
+    word = jnp.full((1,), z, jnp.int32)
     groups = [
         [row * cols + col for row in range(slabs) for col in range(part * half, (part + 1) * half)]
         for part in range(2)
     ]
-    z_word = jnp.full((1,), z, jnp.int32)
-    parts = []
-    for chunk in range(chunks):
-        scale = own_rows[:, chunk].reshape(chunk_rows // BLOCK_ROWS, total)
-        spectra, halo = transform_rows(z_word, raw[chunk], scale, halo, row_tables, slabs, kept, outer)
-        spectra = spectra.astype(jnp.float16)
-        width = min(slab, LANES)
-        planes = slab // width
+    width = min(slab, LANES)
+    planes = slab // width
+
+    def exchange(spectra):
         if slab >= LANES:
             spectra = spectra.reshape(slabs * half, planes, 2, chunk_rows, LANES)
         else:
             spectra = spectra.reshape(slabs, kept, 2, chunk_rows, LANES // slab, slab)
             spectra = spectra.transpose(0, 1, 4, 2, 3, 5).reshape(slabs * half, 1, 2, chunk_rows, slab)
-        gathered = lax.all_to_all(
+        return lax.all_to_all(
             spectra, ("rows", "cols"), split_axis=0, concat_axis=0, tiled=True, axis_index_groups=groups
         )
-        parts.append(mix_columns(gathered.astype(f32), column_tables, chunk * count, count))
-    return tuple(finish_columns(parts, outer))
+
+    order = [*range(1, chunks), 0]
+    raw, gathered, parts = {}, {}, {}
+
+    def send(place, source):
+        steps = step_rows(source, by_kind, scales, halo, order[place])
+        raw[place] = [
+            lax.ppermute(steps[step % half], "cols", [(at, at ^ step) for at in range(cols)]) if step else steps[0]
+            for step in range(cols)
+        ]
+
+    def mix(place):
+        chunk = order[place]
+        parts[chunk] = mix_columns(gathered[place], column_tables, chunk * count, count)
+
+    for place in range(min(2, chunks)):
+        send(place, word)
+    for place in range(chunks):
+        spectra = transform_rows(word, raw[place], row_tables, slabs, kept, outer)
+        if place + 2 < chunks:
+            source, spectra = lax.optimization_barrier((word, spectra))
+            send(place + 2, source)
+        if place >= 1:
+            spectra, gathered[place - 1] = lax.optimization_barrier((spectra, gathered[place - 1]))
+            mix(place - 1)
+        gathered[place] = exchange(spectra)
+    mix(chunks - 1)
+    return tuple(finish_columns([parts[chunk] for chunk in range(chunks)], outer))
 
 
 def solution(mesh):

time: 414 us -> 307 us (0.74)
  other arithmetic: 31.6 us -> 1.75 us
  waiting for transfers between devices: 170 us -> 142 us
  Pallas kernels: 131 us -> 106 us
  starting transfers between devices: 58.1 us -> 41.2 us
  local copies, waits for them, and re-layouts: 21 us -> 10.4 us
    ppermute x16 -> x13, waiting for transfers between devices: 147 us -> 67.9 us  [the longest x12 67.8 us: send(): lax.ppermute(steps[step % half], 'cols', [(at, at ^ step) for at in range...]
    all_to_all x4, waiting for transfers between devices: 22.9 us -> 74.2 us  [exchange(): lax.all_to_all(spectra, ('rows', 'cols'), split_axis=0, concat_axis=0, ti...]
    convert_element_type x9 -> x2, other arithmetic: 30.8 us -> 0.87 us  [the longest x1 0.86 us: local(): ends = by_kind[:, -1, -1, -1].astype(f32) * scales[-1, :, -1]]
    pallas_call x4 -> x8, Pallas kernels: 83.8 us -> 61.7 us  [the longest x4 56.8 us: transform_rows(): pl.pallas_call(functools.partial(row_kernel, cols), out_shape=jax.ShapeDt...]
    all_to_all x4, starting transfers between devices: 37.2 us -> 21.7 us  [exchange(): lax.all_to_all(spectra, ('rows', 'cols'), split_axis=0, concat_axis=0, ti...]
    dynamic_slice x3 -> x0, local copies, waits for them, and re-layouts: 6.37 us -> none  [the longest x2 6.29 us: raw_piece(): lax.dynamic_index_in_dim(by_kind[:, :, chunk], target_kind, 0, False)]
    slice x4 -> x7, local copies, waits for them, and re-layouts: 5.17 us -> 0.33 us  [the longest x3 0.17 us: step_rows(): scales[before]]
    unnamed x36 -> x22, local copies, waits for them, and re-layouts: 8.78 us -> 6.56 us
  transfers between devices with their start and end apart: 20 -> 17, of which waited for: 8 -> 10; matrix products, arithmetic and copies ran while one was open for 8% -> 1% of each run, Pallas kernels for 21% -> 27%
where the time goes in v2:
time: 307 us; the launch traced here: 302 us
  waiting for transfers between devices  142 us (46%)
  Pallas kernels  106 us (35%)
  starting transfers between devices  41.2 us (13%)
  local copies, waits for them, and re-layouts  10.4 us (3%)
    all_to_all x4, waiting for transfers between devices, exchange(): lax.all_to_all(spectra, ('rows', 'cols'), split_axis=0, concat_axis=0, ti...  74.2 us
    ppermute x12, waiting for transfers between devices, send(): lax.ppermute(steps[step % half], 'cols', [(at, at ^ step) for at in range...  67.8 us
    pallas_call x4, Pallas kernels, transform_rows(): pl.pallas_call(functools.partial(row_kernel, cols), out_shape=jax.ShapeDt...  56.8 us
    pallas_call x4, Pallas kernels, mix_columns(): pl.pallas_call(functools.partial(column_kernel, first), out_shape=jax.Sha...  28.7 us
    all_to_all x4, starting transfers between devices, exchange(): lax.all_to_all(spectra, ('rows', 'cols'), split_axis=0, concat_axis=0, ti...  21.7 us
    ppermute x12, starting transfers between devices, send(): lax.ppermute(steps[step % half], 'cols', [(at, at ^ step) for at in range...  15.9 us
    pallas_call x1, Pallas kernels, finish_columns(): pl.pallas_call(functools.partial(finish_kernel, outer), out_shape=(shape,...  15.3 us
    unnamed x22, local copies, waits for them, and re-layouts  6.56 us
  transfers between devices with their start and end apart: 17, of which 10 were waited for; matrix products, arithmetic and copies ran while one was open for 1% of the time, Pallas kernels for 27%

profile of v2, /device:TPU:17, one launch (start us, length us, event | category | flops | bytes accessed | tf_op | source)
XLA Modules:
  0.0 302.1 jit_solution(14609437830679882554)
XLA Ops:
  0.6 0.9 slice_convert_fusion
  1.5 0.8 fusion.2
  2.4 0.2 broadcast_in_dim.27
  2.6 0.3 reshape.60
  2.9 3.7 %collective-permute-start = (bf16[1,2048]{1,0:T(2,128)(2,1)S(1)}, bf16[1,2048]{1,0:T(2,128)(2,1)S(1)}, u32[]{:S(2)}, u32[]{:S(2)}) collective-permute-start(bf16[1,2048]{1,0:T(2,128)(2,1)S(1)} %slice.130), channel_id=1, source_target_pairs={{0,4},{4,8},{8,12},{12,16},{16,20},{20,24},{24,28},{1,5},{5,9},{9,... | collective-permute-start | bytes 12296 | tf_op jit(solution)/shard_map/ppermute | solution.py:348
  6.6 0.1 copy.24
  6.7 0.1 copy.25
  6.8 0.1 copy.21
  6.9 0.1 copy.20
  6.9 0.1 broadcast_bitcast_fusion.2
  7.1 0.1 broadcast_bitcast_fusion
  7.2 0.1 collective-permute-done
  7.4 0.0 copy-start
  7.4 2.2 copy-done
  9.6 1.2 step_rows.6
  10.8 0.1 slice_bitcast_fusion.2
  11.0 0.2 collective-permute-start.9
  11.2 1.2 collective-permute-start.7
  12.4 2.0 collective-permute-start.8
  14.4 0.0 copy-start.4
  14.4 0.0 copy-start.5
  14.4 1.2 step_rows.4
  15.7 0.9 slice_bitcast_fusion.6
  16.6 0.3 collective-permute-start.3
  16.9 1.2 collective-permute-start.1
  18.1 17.8 %collective-permute-done.9.refs_3_ = s16[128,2048]{1,0:T(8,128)(2,1)S(1)} collective-permute-done((s16[128,2048]{1,0:T(8,128)(2,1)S(1)}, s16[128,2048]{1,0:T(8,128)(2,1)S(1)}, u32[]{:S(2)}, u32[]{:S(2)}) %collective-permute-start.9) | collective-permute-done | bytes 524320 | tf_op jit(solution)/shard_map/ppermute | solution.py:375
  35.9 0.0 collective-permute-start.2
  35.9 1.1 collective-permute-done.7.refs_1_
  37.0 31.2 %collective-permute-done.8.refs_2_ = s16[128,2048]{1,0:T(8,128)(2,1)S(1)} collective-permute-done((s16[128,2048]{1,0:T(8,128)(2,1)S(1)}, s16[128,2048]{1,0:T(8,128)(2,1)S(1)}, u32[]{:S(2)}, u32[]{:S(2)}) %collective-permute-start.8) | collective-permute-done | bytes 524320 | tf_op jit(solution)/shard_map/ppermute | solution.py:375
  68.2 13.4 %row_transform.6 = s16[8,4,2,128,128]{4,3,2,1,0:T(8,128)(2,1)} custom-call(s32[1]{0:T(128)} %bitcast.z_ref, bf16[128,256]{1,0:T(8,128)(2,1)S(1)} %copy-done.5, bf16[128,256]{1,0:T(8,128)(2,1)S(1)} %copy-done.4, f32[64,128]{1,0:T(8,128)S(1)} %get-tuple-element.35.cos_ref, f32[64,128]{1,0:T(8,128)S(1)} %get-tuple-element.34.sin_ref, ...), custom_call_target="tpu_custom_call" | custom-call | flops 107374182400 | bytes 8388608 | tf_op jit(solution)/shard_map/row_transform/pallas_call | solution.py:201
  81.6 1.2 step_rows.7
  82.8 0.9 slice_bitcast_fusion
  83.7 1.0 collective-permute-start.12
  84.7 3.5 %collective-permute-start.10 = (s16[128,2048]{1,0:T(8,128)(2,1)}, s16[128,2048]{1,0:T(8,128)(2,1)S(1)}, u32[]{:S(2)}, u32[]{:S(2)}) collective-permute-start(s16[128,2048]{1,0:T(8,128)(2,1)} %get-tuple-element.22), channel_id=1, source_target_pairs={{0,1},{1,0},{2,3},{3,2},{4,5},{5,4},{6,7},{7,6},{8,9},{9,8},{10,11... | collective-permute-start | bytes 1572872 | tf_op jit(solution)/shard_map/ppermute | solution.py:375
  88.2 6.8 %all-to-all-start = ((s16[16,2,2,128,128]{4,3,2,1,0:T(8,128)(2,1)}), s16[16,2,2,128,128]{4,3,2,1,0:T(8,128)(2,1)}, u32[]{:S(2)}, u32[]{:S(2)}) async-start(s16[16,2,2,128,128]{4,3,2,1,0:T(8,128)(2,1)} %bitcast.26), calls=%async_computation | async-start | bytes 4194304 | tf_op jit(solution)/shard_map/all_to_all | solution.py:365
  95.0 8.7 %collective-permute-done.3.refs_3_ = s16[128,2048]{1,0:T(8,128)(2,1)S(1)} collective-permute-done((s16[128,2048]{1,0:T(8,128)(2,1)}, s16[128,2048]{1,0:T(8,128)(2,1)S(1)}, u32[]{:S(2)}, u32[]{:S(2)}) %collective-permute-start.3) | collective-permute-done | bytes 524320 | tf_op jit(solution)/shard_map/ppermute | solution.py:375
  103.7 0.0 collective-permute-start.11
  103.7 0.0 collective-permute-done.1.refs_1_
  103.7 9.0 %collective-permute-done.2.refs_2_ = s16[128,2048]{1,0:T(8,128)(2,1)} collective-permute-done((s16[128,2048]{1,0:T(8,128)(2,1)S(1)}, s16[128,2048]{1,0:T(8,128)(2,1)}, u32[]{:S(2)}, u32[]{:S(2)}) %collective-permute-start.2) | collective-permute-done | bytes 524320 | tf_op jit(solution)/shard_map/ppermute | solution.py:375
  112.7 0.8 copy-done.6
  113.6 14.4 %row_transform.4 = s16[8,4,2,128,128]{4,3,2,1,0:T(8,128)(2,1)} custom-call(s32[1]{0:T(128)} %bitcast.z_ref, bf16[128,256]{1,0:T(8,128)(2,1)S(1)} %copy-done.6, bf16[128,256]{1,0:T(8,128)(2,1)S(1)} %copy-done.4, f32[64,128]{1,0:T(8,128)S(1)} %get-tuple-element.35.cos_ref, f32[64,128]{1,0:T(8,128)S(1)} %get-tuple-element.34.sin_ref, ...), custom_call_target="tpu_custom_call" | custom-call | flops 107374182400 | bytes 8388608 | tf_op jit(solution)/shard_map/row_transform/pallas_call | solution.py:201
  128.0 1.2 step_rows.5
  129.2 0.0 copy-start.7
  129.2 0.9 slice_bitcast_fusion.4
  130.1 1.4 collective-permute-start.6
  131.6 2.7 collective-permute-start.4
  134.2 33.2 %all-to-all-done.in_ref = s16[16,2,2,128,128]{4,3,2,1,0:T(8,128)(2,1)} async-done(((s16[16,2,2,128,128]{4,3,2,1,0:T(8,128)(2,1)}), s16[16,2,2,128,128]{4,3,2,1,0:T(8,128)(2,1)}, u32[]{:S(2)}, u32[]{:S(2)}) %all-to-all-start) | async-done | bytes 2097184 | tf_op jit(solution)/shard_map/all_to_all | solution.py:365
  167.4 4.5 %all-to-all-start.1 = ((s16[16,2,2,128,128]{4,3,2,1,0:T(8,128)(2,1)}), s16[16,2,2,128,128]{4,3,2,1,0:T(8,128)(2,1)}, u32[]{:S(2)}, u32[]{:S(2)}) async-start(s16[16,2,2,128,128]{4,3,2,1,0:T(8,128)(2,1)} %bitcast.27), calls=%async_computation.1 | async-start | bytes 4194304 | tf_op jit(solution)/shard_map/all_to_all | solution.py:365
  171.9 0.0 collective-permute-done.12.refs_3_
  171.9 2.3 collective-permute-start.5
  174.3 14.5 %row_transform.7 = s16[8,4,2,128,128]{4,3,2,1,0:T(8,128)(2,1)} custom-call(s32[1]{0:T(128)} %bitcast.z_ref, bf16[128,256]{1,0:T(8,128)(2,1)S(1)} %copy-done.7, bf16[128,256]{1,0:T(8,128)(2,1)S(1)} %copy-done.4, f32[64,128]{1,0:T(8,128)S(1)} %get-tuple-element.35.cos_ref, f32[64,128]{1,0:T(8,128)S(1)} %get-tuple-element.34.sin_ref, ...), custom_call_target="tpu_custom_call" | custom-call | flops 107374182400 | bytes 8388608 | tf_op jit(solution)/shard_map/row_transform/pallas_call | solution.py:201
  188.8 23.4 %all-to-all-done.1.in_ref = s16[16,2,2,128,128]{4,3,2,1,0:T(8,128)(2,1)} async-done(((s16[16,2,2,128,128]{4,3,2,1,0:T(8,128)(2,1)}), s16[16,2,2,128,128]{4,3,2,1,0:T(8,128)(2,1)}, u32[]{:S(2)}, u32[]{:S(2)}) %all-to-all-start.1) | async-done | bytes 2097184 | tf_op jit(solution)/shard_map/all_to_all | solution.py:365
  212.2 5.0 %all-to-all-start.2 = ((s16[16,2,2,128,128]{4,3,2,1,0:T(8,128)(2,1)}), s16[16,2,2,128,128]{4,3,2,1,0:T(8,128)(2,1)}, u32[]{:S(2)}, u32[]{:S(2)}) async-start(s16[16,2,2,128,128]{4,3,2,1,0:T(8,128)(2,1)} %bitcast.28), calls=%async_computation.2 | async-start | bytes 4194304 | tf_op jit(solution)/shard_map/all_to_all | solution.py:365
  217.2 14.4 %row_transform.5 = s16[8,4,2,128,128]{4,3,2,1,0:T(8,128)(2,1)} custom-call(s32[1]{0:T(128)} %bitcast.z_ref, bf16[128,256]{1,0:T(8,128)(2,1)S(1)} %copy-done.7, bf16[128,256]{1,0:T(8,128)(2,1)S(1)} %copy-done.4, f32[64,128]{1,0:T(8,128)S(1)} %get-tuple-element.35.cos_ref, f32[64,128]{1,0:T(8,128)S(1)} %get-tuple-element.34.sin_ref, ...), custom_call_target="tpu_custom_call" | custom-call | flops 107374182400 | bytes 8388608 | tf_op jit(solution)/shard_map/row_transform/pallas_call | solution.py:201
  231.7 12.3 %all-to-all-done.2.in_ref = s16[16,2,2,128,128]{4,3,2,1,0:T(8,128)(2,1)} async-done(((s16[16,2,2,128,128]{4,3,2,1,0:T(8,128)(2,1)}), s16[16,2,2,128,128]{4,3,2,1,0:T(8,128)(2,1)}, u32[]{:S(2)}, u32[]{:S(2)}) %all-to-all-start.2) | async-done | bytes 2097184 | tf_op jit(solution)/shard_map/all_to_all | solution.py:365
  243.9 5.4 %all-to-all-start.3 = ((s16[16,2,2,128,128]{4,3,2,1,0:T(8,128)(2,1)}), s16[16,2,2,128,128]{4,3,2,1,0:T(8,128)(2,1)S(1)}, u32[]{:S(2)}, u32[]{:S(2)}) async-start(s16[16,2,2,128,128]{4,3,2,1,0:T(8,128)(2,1)} %bitcast.29), calls=%async_computation.3 | async-start | bytes 4194304 | tf_op jit(solution)/shard_map/all_to_all | solution.py:365
  249.3 7.2 %column_mix.5.refs_1_ = f32[16,2,256,128]{3,2,1,0:T(8,128)} custom-call(bf16[256,256]{1,0:T(8,128)(2,1)} %constant.54.clone.high_ref, bf16[256,256]{1,0:T(8,128)(2,1)} %constant.55.clone.low_ref, f32[64,128]{1,0:T(8,128)} %constant.56.clone.cos_ref, f32[64,128]{1,0:T(8,128)} %constant.57.clone.sin_ref, s16[16,2,2,128,128]{4,3,2,1,0:T(8,128)(2,1)} %all-to-all-done.in_ref), custom_call_target="tpu_custom_call" | custom-call | bytes 1024 | tf_op jit(solution)/shard_map/column_mix/pallas_call | solution.py:247
  256.6 7.2 %column_mix.6.refs_2_ = f32[16,2,256,128]{3,2,1,0:T(8,128)} custom-call(bf16[256,256]{1,0:T(8,128)(2,1)} %constant.54.clone.high_ref, bf16[256,256]{1,0:T(8,128)(2,1)} %constant.55.clone.low_ref, f32[64,128]{1,0:T(8,128)} %constant.56.clone.cos_ref, f32[64,128]{1,0:T(8,128)} %constant.57.clone.sin_ref, s16[16,2,2,128,128]{4,3,2,1,0:T(8,128)(2,1)} %all-to-all-done.1.in_ref), custom_call_target="tpu_custom_call" | custom-call | bytes 1024 | tf_op jit(solution)/shard_map/column_mix/pallas_call | solution.py:247
  263.8 7.1 %column_mix.7.refs_3_ = f32[16,2,256,128]{3,2,1,0:T(8,128)} custom-call(bf16[256,256]{1,0:T(8,128)(2,1)} %constant.54.clone.high_ref, bf16[256,256]{1,0:T(8,128)(2,1)} %constant.55.clone.low_ref, f32[64,128]{1,0:T(8,128)} %constant.56.clone.cos_ref, f32[64,128]{1,0:T(8,128)} %constant.57.clone.sin_ref, s16[16,2,2,128,128]{4,3,2,1,0:T(8,128)(2,1)} %all-to-all-done.2.in_ref), custom_call_target="tpu_custom_call" | custom-call | bytes 1024 | tf_op jit(solution)/shard_map/column_mix/pallas_call | solution.py:247
  270.9 5.3 %all-to-all-done.3.in_ref = s16[16,2,2,128,128]{4,3,2,1,0:T(8,128)(2,1)S(1)} async-done(((s16[16,2,2,128,128]{4,3,2,1,0:T(8,128)(2,1)}), s16[16,2,2,128,128]{4,3,2,1,0:T(8,128)(2,1)S(1)}, u32[]{:S(2)}, u32[]{:S(2)}) %all-to-all-start.3) | async-done | bytes 2097184 | tf_op jit(solution)/shard_map/all_to_all | solution.py:365
  276.2 1.3 copy-done.8
  277.5 7.1 %column_mix.4.refs_0_ = f32[16,2,256,128]{3,2,1,0:T(8,128)} custom-call(bf16[256,256]{1,0:T(8,128)(2,1)} %constant.54.clone.high_ref, bf16[256,256]{1,0:T(8,128)(2,1)} %constant.55.clone.low_ref, f32[64,128]{1,0:T(8,128)} %constant.56.clone.cos_ref, f32[64,128]{1,0:T(8,128)} %constant.57.clone.sin_ref, s16[16,2,2,128,128]{4,3,2,1,0:T(8,128)(2,1)} %copy-done.8), custom_call_target="tpu_custom_call" | custom-call | bytes 1024 | tf_op jit(solution)/shard_map/column_mix/pallas_call | solution.py:247
  284.6 2.2 copy-done.3
  286.8 15.3 %column_finish.1 = (f32[256,8192]{1,0:T(8,128)}, f32[256,8192]{1,0:T(8,128)}) custom-call(f32[16,2,256,128]{3,2,1,0:T(8,128)S(1)} %copy-done.3, f32[16,2,256,128]{3,2,1,0:T(8,128)} %column_mix.5.refs_1_, f32[16,2,256,128]{3,2,1,0:T(8,128)} %column_mix.6.refs_2_, f32[16,2,256,128]{3,2,1,0:T(8,128)} %column_mix.7.refs_3_), custom_call_target="tpu_custom_call" | custom-call | tf_op jit(solution)/shard_map/column_finish/pallas_call | solution.py:295
  (28 shorter events, 0.2 us)
Async XLA Ops:
  2.9 4.5 %collective-permute-start = (bf16[1,2048]{1,0:T(2,128)(2,1)S(1)}, bf16[1,2048]{1,0:T(2,128)(2,1)S(1)}, u32[]{:S(2)}, u32[]{:S(2)}) collective-permute-start(bf16[1,2048]{1,0:T(2,128)(2,1)S(1)} %slice.130), channel_id=1, source_target_pairs={{0,4},{4,8},{8,12},{12,16},{16,20},{20,24},{24,28},{1,5},{5,9},{9,... | collective-permute-start | bytes 12296 | tf_op jit(solution)/shard_map/ppermute | solution.py:348
  7.4 2.2 copy-start
  9.6 4.8 %copy-start.9 = (f32[2,64,128]{2,1,0:T(8,128)S(1)}, f32[2,64,128]{2,1,0:T(8,128)}, u32[]{:S(2)}) copy-start(f32[2,64,128]{2,1,0:T(8,128)} %constant.51.clone) | copy-start | bytes 196612
  9.6 4.8 %copy-start.10 = (f32[2,64,128]{2,1,0:T(8,128)S(1)}, f32[2,64,128]{2,1,0:T(8,128)}, u32[]{:S(2)}) copy-start(f32[2,64,128]{2,1,0:T(8,128)} %constant.50.clone) | copy-start | bytes 196612
  11.0 24.9 %collective-permute-start.9 = (s16[128,2048]{1,0:T(8,128)(2,1)S(1)}, s16[128,2048]{1,0:T(8,128)(2,1)S(1)}, u32[]{:S(2)}, u32[]{:S(2)}) collective-permute-start(s16[128,2048]{1,0:T(8,128)(2,1)S(1)} %get-tuple-element.24), channel_id=1, source_target_pairs={{0,3},{1,2},{2,1},{3,0},{4,7},{5,6},{6,5},{7,4},{8,11},{9,10},{10,... | collective-permute-start | bytes 1572872 | tf_op jit(solution)/shard_map/ppermute | solution.py:375
  11.2 25.8 %collective-permute-start.7 = (s16[128,2048]{1,0:T(8,128)(2,1)S(1)}, s16[128,2048]{1,0:T(8,128)(2,1)S(1)}, u32[]{:S(2)}, u32[]{:S(2)}) collective-permute-start(s16[128,2048]{1,0:T(8,128)(2,1)S(1)} %get-tuple-element.24), channel_id=1, source_target_pairs={{0,1},{1,0},{2,3},{3,2},{4,5},{5,4},{6,7},{7,6},{8,9},{9,8},{10,11... | collective-permute-start | bytes 1572872 | tf_op jit(solution)/shard_map/ppermute | solution.py:375
  12.4 55.8 %collective-permute-start.8 = (s16[128,2048]{1,0:T(8,128)(2,1)S(1)}, s16[128,2048]{1,0:T(8,128)(2,1)S(1)}, u32[]{:S(2)}, u32[]{:S(2)}) collective-permute-start(s16[128,2048]{1,0:T(8,128)(2,1)S(1)} %get-tuple-element.25.refs_0_), channel_id=1, source_target_pairs={{0,2},{1,3},{2,0},{3,1},{4,6},{5,7},{6,4},{7,5},{8,10},{9,11},{10,... | collective-permute-start | bytes 1572872 | tf_op jit(solution)/shard_map/ppermute | solution.py:375
  14.4 53.8 %copy-start.4 = (bf16[128,256]{1,0:T(8,128)(2,1)S(1)}, bf16[128,256]{1,0:T(8,128)(2,1)}, u32[]{:S(2)}) copy-start(bf16[128,256]{1,0:T(8,128)(2,1)} %constant.53.clone.low_ref) | copy-start | bytes 196612
  14.4 53.8 %copy-start.5 = (bf16[128,256]{1,0:T(8,128)(2,1)S(1)}, bf16[128,256]{1,0:T(8,128)(2,1)}, u32[]{:S(2)}) copy-start(bf16[128,256]{1,0:T(8,128)(2,1)} %constant.52.clone.high_ref) | copy-start | bytes 196612
  16.6 87.2 %collective-permute-start.3 = (s16[128,2048]{1,0:T(8,128)(2,1)}, s16[128,2048]{1,0:T(8,128)(2,1)S(1)}, u32[]{:S(2)}, u32[]{:S(2)}) collective-permute-start(s16[128,2048]{1,0:T(8,128)(2,1)} %get-tuple-element.28), channel_id=1, source_target_pairs={{0,3},{1,2},{2,1},{3,0},{4,7},{5,6},{6,5},{7,4},{8,11},{9,10},{10,... | collective-permute-start | bytes 1572872 | tf_op jit(solution)/shard_map/ppermute | solution.py:375
  16.9 86.9 %collective-permute-start.1 = (s16[128,2048]{1,0:T(8,128)(2,1)}, s16[128,2048]{1,0:T(8,128)(2,1)S(1)}, u32[]{:S(2)}, u32[]{:S(2)}) collective-permute-start(s16[128,2048]{1,0:T(8,128)(2,1)} %get-tuple-element.28), channel_id=1, source_target_pairs={{0,1},{1,0},{2,3},{3,2},{4,5},{5,4},{6,7},{7,6},{8,9},{9,8},{10,11... | collective-permute-start | bytes 1572872 | tf_op jit(solution)/shard_map/ppermute | solution.py:375
  35.9 76.9 %collective-permute-start.2 = (s16[128,2048]{1,0:T(8,128)(2,1)S(1)}, s16[128,2048]{1,0:T(8,128)(2,1)}, u32[]{:S(2)}, u32[]{:S(2)}) collective-permute-start(s16[128,2048]{1,0:T(8,128)(2,1)S(1)} %get-tuple-element.29.refs_0_), channel_id=1, source_target_pairs={{0,2},{1,3},{2,0},{3,1},{4,6},{5,7},{6,4},{7,5},{8,10},{9,11},{10,... | collective-permute-start | bytes 1572872 | tf_op jit(solution)/shard_map/ppermute | solution.py:375
  68.2 13.4 %copy-start.1 = (bf16[1024,2048]{1,0:T(8,128)(2,1)S(1)}, bf16[1024,2048]{1,0:T(8,128)(2,1)}, u32[]{:S(2)}) copy-start(bf16[1024,2048]{1,0:T(8,128)(2,1)} %param.10) | copy-start | bytes 12582916
  83.7 88.2 %collective-permute-start.12 = (s16[128,2048]{1,0:T(8,128)(2,1)}, s16[128,2048]{1,0:T(8,128)(2,1)S(1)}, u32[]{:S(2)}, u32[]{:S(2)}) collective-permute-start(s16[128,2048]{1,0:T(8,128)(2,1)} %get-tuple-element.22), channel_id=1, source_target_pairs={{0,3},{1,2},{2,1},{3,0},{4,7},{5,6},{6,5},{7,4},{8,11},{9,10},{10,... | collective-permute-start | bytes 1572872 | tf_op jit(solution)/shard_map/ppermute | solution.py:375
  84.7 89.6 %collective-permute-start.10 = (s16[128,2048]{1,0:T(8,128)(2,1)}, s16[128,2048]{1,0:T(8,128)(2,1)S(1)}, u32[]{:S(2)}, u32[]{:S(2)}) collective-permute-start(s16[128,2048]{1,0:T(8,128)(2,1)} %get-tuple-element.22), channel_id=1, source_target_pairs={{0,1},{1,0},{2,3},{3,2},{4,5},{5,4},{6,7},{7,6},{8,9},{9,8},{10,11... | collective-permute-start | bytes 1572872 | tf_op jit(solution)/shard_map/ppermute | solution.py:375
  88.2 79.2 %all-to-all-start = ((s16[16,2,2,128,128]{4,3,2,1,0:T(8,128)(2,1)}), s16[16,2,2,128,128]{4,3,2,1,0:T(8,128)(2,1)}, u32[]{:S(2)}, u32[]{:S(2)}) async-start(s16[16,2,2,128,128]{4,3,2,1,0:T(8,128)(2,1)} %bitcast.26), calls=%async_computation | async-start | bytes 4194304 | tf_op jit(solution)/shard_map/all_to_all | solution.py:365
  103.7 24.3 %copy-start.2 = (bf16[1024,2048]{1,0:T(8,128)(2,1)S(1)}, bf16[1024,2048]{1,0:T(8,128)(2,1)}, u32[]{:S(2)}) copy-start(bf16[1024,2048]{1,0:T(8,128)(2,1)} %param.10) | copy-start | bytes 12582916
  103.7 70.5 %collective-permute-start.11 = (s16[128,2048]{1,0:T(8,128)(2,1)S(1)}, s16[128,2048]{1,0:T(8,128)(2,1)}, u32[]{:S(2)}, u32[]{:S(2)}) collective-permute-start(s16[128,2048]{1,0:T(8,128)(2,1)S(1)} %get-tuple-element.23.refs_0_), channel_id=1, source_target_pairs={{0,2},{1,3},{2,0},{3,1},{4,6},{5,7},{6,4},{7,5},{8,10},{9,11},{10,... | collective-permute-start | bytes 1572872 | tf_op jit(solution)/shard_map/ppermute | solution.py:375
  112.7 0.8 copy-start.6
  129.2 45.0 %copy-start.7 = (bf16[128,256]{1,0:T(8,128)(2,1)S(1)}, bf16[128,256]{1,0:T(8,128)(2,1)}, u32[]{:S(2)}) copy-start(bf16[128,256]{1,0:T(8,128)(2,1)} %constant.52.clone.high_ref) | copy-start | bytes 196612
  130.1 87.1 %collective-permute-start.6 = (s16[128,2048]{1,0:T(8,128)(2,1)}, s16[128,2048]{1,0:T(8,128)(2,1)S(1)}, u32[]{:S(2)}, u32[]{:S(2)}) collective-permute-start(s16[128,2048]{1,0:T(8,128)(2,1)} %get-tuple-element.26), channel_id=1, source_target_pairs={{0,3},{1,2},{2,1},{3,0},{4,7},{5,6},{6,5},{7,4},{8,11},{9,10},{10,... | collective-permute-start | bytes 1572872 | tf_op jit(solution)/shard_map/ppermute | solution.py:375
  131.6 85.6 %collective-permute-start.4 = (s16[128,2048]{1,0:T(8,128)(2,1)}, s16[128,2048]{1,0:T(8,128)(2,1)S(1)}, u32[]{:S(2)}, u32[]{:S(2)}) collective-permute-start(s16[128,2048]{1,0:T(8,128)(2,1)} %get-tuple-element.26), channel_id=1, source_target_pairs={{0,1},{1,0},{2,3},{3,2},{4,5},{5,4},{6,7},{7,6},{8,9},{9,8},{10,11... | collective-permute-start | bytes 1572872 | tf_op jit(solution)/shard_map/ppermute | solution.py:375
  167.4 44.8 %all-to-all-start.1 = ((s16[16,2,2,128,128]{4,3,2,1,0:T(8,128)(2,1)}), s16[16,2,2,128,128]{4,3,2,1,0:T(8,128)(2,1)}, u32[]{:S(2)}, u32[]{:S(2)}) async-start(s16[16,2,2,128,128]{4,3,2,1,0:T(8,128)(2,1)} %bitcast.27), calls=%async_computation.1 | async-start | bytes 4194304 | tf_op jit(solution)/shard_map/all_to_all | solution.py:365
  171.9 45.3 %collective-permute-start.5 = (s16[128,2048]{1,0:T(8,128)(2,1)S(1)}, s16[128,2048]{1,0:T(8,128)(2,1)}, u32[]{:S(2)}, u32[]{:S(2)}) collective-permute-start(s16[128,2048]{1,0:T(8,128)(2,1)S(1)} %get-tuple-element.27.refs_0_), channel_id=1, source_target_pairs={{0,2},{1,3},{2,0},{3,1},{4,6},{5,7},{6,4},{7,5},{8,10},{9,11},{10,... | collective-permute-start | bytes 1572872 | tf_op jit(solution)/shard_map/ppermute | solution.py:375
  212.2 31.7 %all-to-all-start.2 = ((s16[16,2,2,128,128]{4,3,2,1,0:T(8,128)(2,1)}), s16[16,2,2,128,128]{4,3,2,1,0:T(8,128)(2,1)}, u32[]{:S(2)}, u32[]{:S(2)}) async-start(s16[16,2,2,128,128]{4,3,2,1,0:T(8,128)(2,1)} %bitcast.28), calls=%async_computation.2 | async-start | bytes 4194304 | tf_op jit(solution)/shard_map/all_to_all | solution.py:365
  243.9 32.2 %all-to-all-start.3 = ((s16[16,2,2,128,128]{4,3,2,1,0:T(8,128)(2,1)}), s16[16,2,2,128,128]{4,3,2,1,0:T(8,128)(2,1)S(1)}, u32[]{:S(2)}, u32[]{:S(2)}) async-start(s16[16,2,2,128,128]{4,3,2,1,0:T(8,128)(2,1)} %bitcast.29), calls=%async_computation.3 | async-start | bytes 4194304 | tf_op jit(solution)/shard_map/all_to_all | solution.py:365
  276.2 1.3 copy-start.8
  284.6 2.2 copy-start.3

commit v3 on v2

--- a/solution.py
+++ b/solution.py
@@ -73,9 +73,10 @@
     return (low + high)[:keep]
 
 
-def step_kernel(first, z_ref, scale_ref, before_scale_ref, halo_ref, now_ref, before_ref, out_ref):
+def step_kernel(first, offset, z_ref, scale_ref, before_scale_ref, halo_ref, now_ref, before_ref, out_ref):
     lines, _, segment, width = now_ref.shape[1:]
     groups = segment // BLOCK_ROWS
+    size = out_ref.shape[1] // lines
     starts = lax.broadcasted_iota(jnp.int32, (segment, LANES), 0) == 0
 
     def take(block, carry):
@@ -90,21 +91,22 @@
             above = last if first else ends
             last = ends
             change = value - jnp.where(starts, above, pltpu.roll(value, 1, 0))
-            out_ref[0, line * segment : (line + 1) * segment, here] = change.astype(jnp.int32).astype(jnp.int16)
+            change = change[offset : offset + size].astype(jnp.int32).astype(jnp.int16)
+            out_ref[0, line * size : (line + 1) * size, here] = change
         return carry
 
     lax.fori_loop(0, width // LANES, take, 0)
 
 
-def step_rows(z, by_kind, scales, halo, chunk):
+def step_rows(z, by_kind, scales, halo, chunk, offset, size):
     kinds, lines, chunks, segment, width = by_kind.shape
     before = (chunk - 1) % chunks
     kind = lambda k, z: lax.rem(lax.bitwise_xor(z[0], k), kinds)
     block = (1, lines, 1, segment, width)
     row_block = (1,) + scales.shape[2:]
     return pl.pallas_call(
-        functools.partial(step_kernel, chunk == 0),
-        out_shape=jax.ShapeDtypeStruct((kinds, lines * segment, width), jnp.int16),
+        functools.partial(step_kernel, chunk == 0, offset),
+        out_shape=jax.ShapeDtypeStruct((kinds, lines * size, width), jnp.int16),
         grid_spec=pltpu.PrefetchScalarGridSpec(
             num_scalar_prefetch=1,
             grid=(kinds,),
@@ -115,9 +117,9 @@
                 pl.BlockSpec(block, lambda k, z: (kind(k, z), 0, chunk, 0, 0)),
                 pl.BlockSpec(block, lambda k, z: (kind(k, z), 0, before, 0, 0)),
             ],
-            out_specs=pl.BlockSpec((1, lines * segment, width), lambda k, z: (k, 0, 0)),
+            out_specs=pl.BlockSpec((1, lines * size, width), lambda k, z: (k, 0, 0)),
         ),
-        compiler_params=pltpu.CompilerParams(vmem_limit_bytes=32 * 1024 * 1024),
+        compiler_params=pltpu.CompilerParams(vmem_limit_bytes=20 * 1024 * 1024),
         cost_estimate=pl.CostEstimate(
             flops=0, bytes_accessed=1024, transcendentals=0
         ),
@@ -142,13 +144,13 @@
     return jnp.where(code < 0, -value, value)
 
 
-def row_kernel(cols, z_ref, high_ref, low_ref, cos_ref, sin_ref, *refs):
+def row_kernel(cols, faces, z_ref, high_ref, low_ref, cos_ref, sin_ref, *refs):
     pieces, (out_ref, table, mixed, stage) = refs[:cols], refs[cols:]
     rows, piece_cols = pieces[0].shape
     outer = cos_ref.shape[0]
     slabs, kept = out_ref.shape[:2]
     pad = table.shape[0] - outer * LANES
-    z = z_ref[0]
+    z, first = z_ref[0], z_ref[1]
     table[0:pad, :] = jnp.zeros((pad, rows), f32)
 
     for step, piece in enumerate(pieces):
@@ -175,6 +177,7 @@
     lax.fori_loop(0, outer, mix, 0, unroll=8)
 
     inner = outer // slabs
+    planes = kept // faces
 
     def finish(tile, carry):
         here = pl.ds(pl.multiple_of(tile * 16, 16), 16)
@@ -186,20 +189,21 @@
             for k, value in enumerate(dft(values, kept)):
                 stage[k, low, 0], stage[k, low, 1] = times(value, low * k, outer)
         for k in range(kept):
+            place = lax.bitwise_xor(k // planes, first) * planes + k % planes if faces > 1 else k
             for slab, value in enumerate(dft([(stage[k, low, 0], stage[k, low, 1]) for low in range(slabs)])):
-                out_ref[slab, k, 0, here, :], out_ref[slab, k, 1, here, :] = encode(value[0]), encode(value[1])
+                out_ref[slab, place, 0, here, :], out_ref[slab, place, 1, here, :] = encode(value[0]), encode(value[1])
         return carry
 
     lax.fori_loop(0, rows // 16, finish, 0)
 
 
-def transform_rows(z, pieces, tables, slabs, kept, outer):
+def transform_rows(z, pieces, tables, slabs, kept, faces, outer):
     rows, piece_cols = pieces[0].shape
     cols = len(pieces)
     total = cols * piece_cols
     vmem = pl.BlockSpec(memory_space=pltpu.VMEM)
     return pl.pallas_call(
-        functools.partial(row_kernel, cols),
+        functools.partial(row_kernel, cols, faces),
         out_shape=jax.ShapeDtypeStruct((slabs, kept, 2, rows, LANES), jnp.int16),
         in_specs=[pl.BlockSpec(memory_space=pltpu.SMEM)] + [vmem] * (4 + cols),
         out_specs=vmem,
@@ -208,25 +212,28 @@
             pltpu.VMEM((outer, 2, rows, LANES), f32),
             pltpu.VMEM((kept, slabs, 2, 16, LANES), f32),
         ],
-        compiler_params=pltpu.CompilerParams(vmem_limit_bytes=48 * 1024 * 1024),
+        compiler_params=pltpu.CompilerParams(vmem_limit_bytes=24 * 1024 * 1024),
         cost_estimate=pl.CostEstimate(
-            flops=800 * rows * total * LANES, bytes_accessed=rows * total * 8, transcendentals=0
+            flops=300 * rows * total * LANES, bytes_accessed=rows * total * 8, transcendentals=0
         ),
         name="row_transform",
     )(z, *tables, *pieces)
 
 
-def column_kernel(first, high_ref, low_ref, cos_ref, sin_ref, in_ref, out_ref, real, imag):
-    sources, _, _, rows, width = in_ref.shape
+def column_kernel(first, faces, kind_ref, high_ref, low_ref, cos_ref, sin_ref, *refs):
+    in_refs, (out_ref, real, imag) = refs[:faces], refs[faces:]
+    sources, _, _, rows, width = in_refs[0].shape
     count = out_ref.shape[0]
-
-    def take(source, carry):
-        here = pl.ds(pl.multiple_of(source * rows, rows), rows)
-        real[here, :] = decode(in_ref[source, 0, 0])
-        imag[here, :] = decode(in_ref[source, 0, 1])
-        return carry
-
-    lax.fori_loop(0, sources, take, 0)
+    for face, in_ref in enumerate(in_refs):
+        slot = lax.bitwise_xor(kind_ref[2], face) if faces > 1 else 0
+
+        def take(source, carry, in_ref=in_ref, slot=slot):
+            here = pl.ds(pl.multiple_of((source * faces + slot) * rows, rows), rows)
+            real[here, :] = decode(in_ref[source, 0, 0])
+            imag[here, :] = decode(in_ref[source, 0, 1])
+            return carry
+
+        lax.fori_loop(0, sources, take, 0)
 
     def mix(index, carry):
         here = pl.ds(index, LANES, stride=count)
@@ -241,28 +248,28 @@
     lax.fori_loop(0, count, mix, 0, unroll=8)
 
 
-def mix_columns(gathered, tables, first, count):
-    sources, planes, _, rows, width = gathered.shape
+def mix_columns(word, gathered, tables, first, count, planes):
+    faces = len(gathered)
+    sources, _, _, rows, width = gathered[0].shape
     whole = lambda table: pl.BlockSpec(table.shape, lambda plane: (0, 0))
     return pl.pallas_call(
-        functools.partial(column_kernel, first),
+        functools.partial(column_kernel, first, faces),
         out_shape=jax.ShapeDtypeStruct((count, 2, planes * width, LANES), f32),
         grid=(planes,),
-        in_specs=[whole(table) for table in tables]
-        + [pl.BlockSpec((sources, 1, 2, rows, width), lambda plane: (0, plane, 0, 0, 0))],
+        in_specs=[pl.BlockSpec(memory_space=pltpu.SMEM)]
+        + [whole(table) for table in tables]
+        + [pl.BlockSpec((sources, 1, 2, rows, width), lambda plane: (0, plane, 0, 0, 0))] * faces,
         out_specs=pl.BlockSpec((count, 2, width, LANES), lambda plane: (0, 0, plane, 0)),
-        scratch_shapes=[pltpu.VMEM((sources * rows, width), f32)] * 2,
-        compiler_params=pltpu.CompilerParams(vmem_limit_bytes=56 * 1024 * 1024),
-        cost_estimate=pl.CostEstimate(
-            flops=0, bytes_accessed=1024, transcendentals=0
-        ),
+        scratch_shapes=[pltpu.VMEM((faces * sources * rows, width), f32)] * 2,
+        compiler_params=pltpu.CompilerParams(vmem_limit_bytes=20 * 1024 * 1024),
+        cost_estimate=pl.CostEstimate(flops=0, bytes_accessed=1024, transcendentals=0),
         name="column_mix",
-    )(*tables, gathered)
+    )(word, *tables, *gathered)
 
 
 def finish_kernel(outer, *refs):
     parts, (real_ref, imag_ref, stage) = refs[:-3], refs[-3:]
-    count = parts[0].shape[0]
+    residues = [(part, index) for part in parts for index in range(part.shape[0])]
     radix = 1 << ((outer.bit_length() - 1) // 2)
     rest = outer // radix
 
@@ -270,8 +277,8 @@
         here = pl.ds(pl.multiple_of(tile * 8, 8), 8)
 
         def load(index):
-            part = parts[index // count]
-            return part[index % count, 0, here, :], part[index % count, 1, here, :]
+            part, own = residues[index]
+            return part[own, 0, here, :], part[own, 1, here, :]
 
         for low in range(rest):
             values = dft([load(high * rest + low) for high in range(radix)])
@@ -301,7 +308,7 @@
         ],
         out_specs=(pl.BlockSpec((tile, outer * LANES), lambda step: (step, 0)),) * 2,
         scratch_shapes=[pltpu.VMEM((radix, outer // radix, 2, 8, LANES), f32)],
-        compiler_params=pltpu.CompilerParams(vmem_limit_bytes=48 * 1024 * 1024),
+        compiler_params=pltpu.CompilerParams(vmem_limit_bytes=24 * 1024 * 1024),
         name="column_finish",
     )(*parts)
 
@@ -321,7 +328,6 @@
     kind_lines = lines // half
     chunks = kind_lines * outer // LANES
     count = outer // chunks
-    chunk_rows = kind_lines * count
 
     index = np.arange(LANES)
     angle = 2 * np.pi * (index[:, None] * index[None, :] % LANES) / LANES
@@ -344,11 +350,8 @@
     scales = jnp.repeat(scales.reshape(chunks, half, kind_lines * (count // BLOCK_ROWS), -1), BLOCK_COLS, axis=-1)
 
     by_kind = mantissa.reshape(half, kind_lines, chunks, count, local_cols)
-    ends = by_kind[:, -1, -1, -1].astype(f32) * scales[-1, :, -1]
-    above = lax.ppermute(ends[-1:].astype(bf16), "rows", [(at, at + 1) for at in range(slabs - 1)])
-    halo = jnp.concatenate((above.astype(f32), ends[:-1]), axis=0).reshape(half, 1, local_cols)
-
-    word = jnp.full((1,), z, jnp.int32)
+    word = jnp.stack([z, jnp.zeros_like(z), kind])
+    word_face = jnp.stack([z, kind, kind])
     groups = [
         [row * cols + col for row in range(slabs) for col in range(part * half, (part + 1) * half)]
         for part in range(2)
@@ -357,42 +360,65 @@
     planes = slab // width
 
     def exchange(spectra):
+        rows = spectra.shape[3]
         if slab >= LANES:
-            spectra = spectra.reshape(slabs * half, planes, 2, chunk_rows, LANES)
+            spectra = spectra.reshape(slabs * half, planes, 2, rows, LANES)
         else:
-            spectra = spectra.reshape(slabs, kept, 2, chunk_rows, LANES // slab, slab)
-            spectra = spectra.transpose(0, 1, 4, 2, 3, 5).reshape(slabs * half, 1, 2, chunk_rows, slab)
+            spectra = spectra.reshape(slabs, kept, 2, rows, LANES // slab, slab)
+            spectra = spectra.transpose(0, 1, 4, 2, 3, 5).reshape(slabs * half, 1, 2, rows, slab)
         return lax.all_to_all(
             spectra, ("rows", "cols"), split_axis=0, concat_axis=0, tiled=True, axis_index_groups=groups
         )
 
-    order = [*range(1, chunks), 0]
-    raw, gathered, parts = {}, {}, {}
+    order = [(c, 0, count) for c in (*range(1, chunks), 0)] if chunks > 1 else [(0, 0, count)]
+    places = len(order)
+    twice = [False] * places
+    raw, sent, gathered, parts = {}, {}, {}, {}
 
     def send(place, source):
-        steps = step_rows(source, by_kind, scales, halo, order[place])
+        steps = step_rows(source, by_kind, scales, halo, *order[place])
         raw[place] = [
             lax.ppermute(steps[step % half], "cols", [(at, at ^ step) for at in range(cols)]) if step else steps[0]
             for step in range(cols)
         ]
 
     def mix(place):
-        chunk = order[place]
-        parts[chunk] = mix_columns(gathered[place], column_tables, chunk * count, count)
-
-    for place in range(min(2, chunks)):
+        chunk, offset, size = order[place]
+        first = chunk * count + offset
+        parts[first] = mix_columns(word, gathered[place], column_tables, first, size, planes)
+
+    halo = jnp.zeros((half, 1, local_cols), f32)
+    if places > 1:
+        send(0, word)
+    last, _ = lax.optimization_barrier((by_kind[:, -1, -1, -1], raw[0][0] if raw else word))
+    ends = last.astype(f32) * scales[-1, :, -1]
+    above = lax.ppermute(ends[-1:].astype(bf16), "rows", [(at, at + 1) for at in range(slabs - 1)])
+    halo = jnp.concatenate((above.astype(f32), ends[:-1]), axis=0).reshape(half, 1, local_cols)
+
+    for place in range(places > 1, min(2, places)):
         send(place, word)
-    for place in range(chunks):
-        spectra = transform_rows(word, raw[place], row_tables, slabs, kept, outer)
-        if place + 2 < chunks:
-            source, spectra = lax.optimization_barrier((word, spectra))
-            send(place + 2, source)
-        if place >= 1:
-            spectra, gathered[place - 1] = lax.optimization_barrier((spectra, gathered[place - 1]))
-            mix(place - 1)
-        gathered[place] = exchange(spectra)
-    mix(chunks - 1)
-    return tuple(finish_columns([parts[chunk] for chunk in range(chunks)], outer))
+    for place in range(places):
+        if 0 < place < places - 1:
+            source, *_ = lax.optimization_barrier((word, raw[place][3 % cols]))
+            send(place + 1, source)
+        spectra = transform_rows(
+            word_face if twice[place] else word, raw[place], row_tables, slabs, kept, half if twice[place] else 1, outer
+        )
+        for before in (place - 1, place - 2):
+            if before >= 0 and before == place - (2 if twice[before] else 1):
+                spectra, gathered[before] = lax.optimization_barrier((spectra, gathered[before]))
+                mix(before)
+        if twice[place]:
+            over_rows = lax.all_to_all(spectra, "rows", split_axis=0, concat_axis=0, tiled=True)
+            other = lax.ppermute(over_rows[:, planes:], "cols", [(at, at ^ 1) for at in range(cols)])
+            gathered[place] = [over_rows, other]
+        else:
+            gathered[place] = [exchange(spectra)]
+    for place in range(places):
+        first = order[place][0] * count + order[place][1]
+        if first not in parts:
+            mix(place)
+    return tuple(finish_columns([parts[first] for first in sorted(parts)], outer))
 
 
 def solution(mesh):

time: 307 us -> 282 us (0.919)
  waiting for transfers between devices: 142 us -> 95.3 us
  local copies, waits for them, and re-layouts: 10.4 us -> 29.2 us
  starting transfers between devices: 41.2 us -> 56.2 us
  Pallas kernels: 106 us -> 94.7 us
    all_to_all x4, waiting for transfers between devices: 74.2 us -> 45 us  [exchange(): lax.all_to_all(spectra, ('rows', 'cols'), split_axis=0, concat_axis=0, ti...]
    all_to_all x4, starting transfers between devices: 21.7 us -> 39.9 us  [exchange(): lax.all_to_all(spectra, ('rows', 'cols'), split_axis=0, concat_axis=0, ti...]
    ppermute x12, waiting for transfers between devices: 67.8 us -> 49.9 us  [send(): lax.ppermute(steps[step % half], 'cols', [(at, at ^ step) for at in range...]
    unnamed x22 -> x53, local copies, waits for them, and re-layouts: 6.56 us -> 23.1 us
    pallas_call x12, Pallas kernels: 90.4 us -> 84 us  [the longest x4 53.1 us: transform_rows(): pl.pallas_call(functools.partial(row_kernel, cols, faces), out_shape=jax....]
    pallas_call x1, Pallas kernels: 15.3 us -> 10.7 us  [finish_columns(): pl.pallas_call(functools.partial(finish_kernel, outer), out_shape=(shape,...]
    ppermute x12, starting transfers between devices: 15.9 us -> 12.1 us  [send(): lax.ppermute(steps[step % half], 'cols', [(at, at ^ step) for at in range...]
  transfers between devices with their start and end apart: 17 -> 17, of which waited for: 10 -> 11; matrix products, arithmetic and copies ran while one was open for 1% -> 2% of each run, Pallas kernels for 27% -> 27%
where the time goes in v3:
time: 282 us; the launch traced here: 278 us
  waiting for transfers between devices  95.3 us (34%)
  Pallas kernels  94.7 us (34%)
  starting transfers between devices  56.2 us (20%)
  local copies, waits for them, and re-layouts  29.2 us (10%)
    pallas_call x4, Pallas kernels, transform_rows(): pl.pallas_call(functools.partial(row_kernel, cols, faces), out_shape=jax....  53.1 us
    ppermute x12, waiting for transfers between devices, send(): lax.ppermute(steps[step % half], 'cols', [(at, at ^ step) for at in range...  49.9 us
    all_to_all x4, waiting for transfers between devices, exchange(): lax.all_to_all(spectra, ('rows', 'cols'), split_axis=0, concat_axis=0, ti...  45 us
    all_to_all x4, starting transfers between devices, exchange(): lax.all_to_all(spectra, ('rows', 'cols'), split_axis=0, concat_axis=0, ti...  39.9 us
    pallas_call x4, Pallas kernels, mix_columns(): pl.pallas_call(functools.partial(column_kernel, first, faces), out_shape=...  23.8 us
    unnamed x53, local copies, waits for them, and re-layouts  23.1 us
    ppermute x12, starting transfers between devices, send(): lax.ppermute(steps[step % half], 'cols', [(at, at ^ step) for at in range...  12.1 us
    pallas_call x1, Pallas kernels, finish_columns(): pl.pallas_call(functools.partial(finish_kernel, outer), out_shape=(shape,...  10.7 us
  transfers between devices with their start and end apart: 17, of which 11 were waited for; matrix products, arithmetic and copies ran while one was open for 2% of the time, Pallas kernels for 27%

profile of v3, /device:TPU:17, one launch (start us, length us, event | category | flops | bytes accessed | tf_op | source)
XLA Modules:
  0.0 278.2 jit_solution(16807846888872820196)
XLA Ops:
  0.6 0.8 fusion.2
  1.5 0.1 copy.21
  1.7 0.1 broadcast_bitcast_fusion.1
  1.8 0.1 pad_add_fusion.z_ref.kind_ref
  1.9 2.2 copy-done
  4.1 1.8 step_rows.4
  5.9 0.9 slice_bitcast_fusion
  6.8 0.2 collective-permute-start.12
  6.9 1.1 collective-permute-start.10
  8.1 2.1 collective-permute-start.11
  10.2 0.2 broadcast_in_dim.29
  10.4 1.1 reshape.58
  11.5 0.7 fusion.3
  12.3 4.2 %collective-permute-start = (bf16[1,2048]{1,0:T(2,128)(2,1)S(1)}, bf16[1,2048]{1,0:T(2,128)(2,1)S(1)}, u32[]{:S(2)}, u32[]{:S(2)}) collective-permute-start(bf16[1,2048]{1,0:T(2,128)(2,1)S(1)} %slice.129), channel_id=1, source_target_pairs={{0,4},{4,8},{8,12},{12,16},{16,20},{20,24},{24,28},{1,5},{5,9},{9,... | collective-permute-start | bytes 12296 | tf_op jit(solution)/shard_map/ppermute | solution.py:395
  16.5 0.1 copy.23
  16.7 0.1 broadcast_bitcast_fusion
  16.9 0.4 collective-permute-done
  17.3 2.2 copy-done.1
  19.5 1.8 step_rows.5
  21.3 1.1 slice_bitcast_fusion.1
  22.4 1.7 collective-permute-start.8
  24.2 6.8 %collective-permute-done.12.refs_3_ = s16[128,2048]{1,0:T(8,128)(2,1)S(1)} collective-permute-done((s16[128,2048]{1,0:T(8,128)(2,1)}, s16[128,2048]{1,0:T(8,128)(2,1)S(1)}, u32[]{:S(2)}, u32[]{:S(2)}) %collective-permute-start.12) | collective-permute-done | bytes 524320 | tf_op jit(solution)/shard_map/ppermute | solution.py:381
  31.0 0.2 collective-permute-done.10.refs_1_
  31.3 20.4 %collective-permute-done.11.refs_2_ = s16[128,2048]{1,0:T(8,128)(2,1)S(1)} collective-permute-done((s16[128,2048]{1,0:T(8,128)(2,1)S(1)}, s16[128,2048]{1,0:T(8,128)(2,1)S(1)}, u32[]{:S(2)}, u32[]{:S(2)}) %collective-permute-start.11) | collective-permute-done | bytes 524320 | tf_op jit(solution)/shard_map/ppermute | solution.py:381
  51.7 12.6 %row_transform.7 = s16[8,4,2,128,128]{4,3,2,1,0:T(8,128)(2,1)S(1)} custom-call(s32[3]{0:T(128)S(1)} %pad_add_fusion.z_ref.kind_ref, bf16[128,256]{1,0:T(8,128)(2,1)S(1)} %copy-done.22, bf16[128,256]{1,0:T(8,128)(2,1)S(1)} %copy-done.20, f32[64,128]{1,0:T(8,128)S(1)} %get-tuple-element.33.cos_ref, f32[64,128]{1,0:T(8,128)S(1)} %get-tuple-element.32.sin_ref, ...), custom_call_target="tpu_custom_call" | custom-call | flops 40265318400 | bytes 8388608 | tf_op jit(solution)/shard_map/row_transform/pallas_call | solution.py:205
  64.3 1.3 copy-done.10
  65.6 9.5 %all-to-all-start = ((s16[16,2,2,128,128]{4,3,2,1,0:T(8,128)(2,1)}), s16[16,2,2,128,128]{4,3,2,1,0:T(8,128)(2,1)S(1)}, u32[]{:S(2)}, u32[]{:S(2)}) async-start(s16[16,2,2,128,128]{4,3,2,1,0:T(8,128)(2,1)} %bitcast.64), calls=%async_computation | async-start | bytes 4194304 | tf_op jit(solution)/shard_map/all_to_all | solution.py:369
  75.1 12.2 %collective-permute-done.1.refs_3_ = s16[128,2048]{1,0:T(8,128)(2,1)} collective-permute-done((s16[128,2048]{1,0:T(8,128)(2,1)}, s16[128,2048]{1,0:T(8,128)(2,1)}, u32[]{:S(2)}, u32[]{:S(2)}) %collective-permute-start.1) | collective-permute-done | bytes 524320 | tf_op jit(solution)/shard_map/ppermute | solution.py:381
  87.3 2.2 copy-done.2
  89.5 1.8 step_rows.6
  91.3 1.1 slice_bitcast_fusion.2
  92.4 0.4 collective-permute-start.2
  92.8 3.2 %collective-permute-start.7 = (s16[128,2048]{1,0:T(8,128)(2,1)}, s16[128,2048]{1,0:T(8,128)(2,1)}, u32[]{:S(2)}, u32[]{:S(2)}) collective-permute-start(s16[128,2048]{1,0:T(8,128)(2,1)} %get-tuple-element.24.refs_0_), channel_id=1, source_target_pairs={{0,2},{1,3},{2,0},{3,1},{4,6},{5,7},{6,4},{7,5},{8,10},{9,11},{10,... | collective-permute-start | bytes 1572872 | tf_op jit(solution)/shard_map/ppermute | solution.py:381
  96.0 0.8 collective-permute-done.9.refs_2_
  96.7 13.8 %row_transform.6 = s16[8,4,2,128,128]{4,3,2,1,0:T(8,128)(2,1)S(1)} custom-call(s32[3]{0:T(128)S(1)} %pad_add_fusion.z_ref.kind_ref, bf16[128,256]{1,0:T(8,128)(2,1)S(1)} %copy-done.22, bf16[128,256]{1,0:T(8,128)(2,1)S(1)} %copy-done.20, f32[64,128]{1,0:T(8,128)S(1)} %get-tuple-element.33.cos_ref, f32[64,128]{1,0:T(8,128)S(1)} %get-tuple-element.32.sin_ref, ...), custom_call_target="tpu_custom_call" | custom-call | flops 40265318400 | bytes 8388608 | tf_op jit(solution)/shard_map/row_transform/pallas_call | solution.py:205
  110.5 1.3 copy-done.11
  111.8 0.8 copy-done.18
  112.6 1.8 step_rows.7
  114.4 18.5 %all-to-all-start.1 = ((s16[16,2,2,128,128]{4,3,2,1,0:T(8,128)(2,1)}), s16[16,2,2,128,128]{4,3,2,1,0:T(8,128)(2,1)}, u32[]{:S(2)}, u32[]{:S(2)}) async-start(s16[16,2,2,128,128]{4,3,2,1,0:T(8,128)(2,1)} %bitcast.65), calls=%async_computation.1 | async-start | bytes 4194304 | tf_op jit(solution)/shard_map/all_to_all | solution.py:369
  133.0 1.1 slice_bitcast_fusion.3
  134.0 2.0 collective-permute-start.5
  136.0 1.0 collective-permute-start.3
  137.0 0.5 collective-permute-start.4
  137.5 4.3 %collective-permute-done.7.refs_2_ = s16[128,2048]{1,0:T(8,128)(2,1)} collective-permute-done((s16[128,2048]{1,0:T(8,128)(2,1)}, s16[128,2048]{1,0:T(8,128)(2,1)}, u32[]{:S(2)}, u32[]{:S(2)}) %collective-permute-start.7) | collective-permute-done | bytes 524320 | tf_op jit(solution)/shard_map/ppermute | solution.py:381
  141.8 13.5 %row_transform.5 = s16[8,4,2,128,128]{4,3,2,1,0:T(8,128)(2,1)S(1)} custom-call(s32[3]{0:T(128)S(1)} %pad_add_fusion.z_ref.kind_ref, bf16[128,256]{1,0:T(8,128)(2,1)S(1)} %copy-done.23, bf16[128,256]{1,0:T(8,128)(2,1)S(1)} %copy-done.21, f32[64,128]{1,0:T(8,128)S(1)} %get-tuple-element.33.cos_ref, f32[64,128]{1,0:T(8,128)S(1)} %get-tuple-element.32.sin_ref, ...), custom_call_target="tpu_custom_call" | custom-call | flops 40265318400 | bytes 8388608 | tf_op jit(solution)/shard_map/row_transform/pallas_call | solution.py:205
  155.3 1.3 copy-done.12
  156.6 31.7 %all-to-all-done.1.refs_0_ = s16[16,2,2,128,128]{4,3,2,1,0:T(8,128)(2,1)} async-done(((s16[16,2,2,128,128]{4,3,2,1,0:T(8,128)(2,1)}), s16[16,2,2,128,128]{4,3,2,1,0:T(8,128)(2,1)}, u32[]{:S(2)}, u32[]{:S(2)}) %all-to-all-start.1) | async-done | bytes 2097184 | tf_op jit(solution)/shard_map/all_to_all | solution.py:369
  188.3 6.1 %all-to-all-start.2 = ((s16[16,2,2,128,128]{4,3,2,1,0:T(8,128)(2,1)}), s16[16,2,2,128,128]{4,3,2,1,0:T(8,128)(2,1)}, u32[]{:S(2)}, u32[]{:S(2)}) async-start(s16[16,2,2,128,128]{4,3,2,1,0:T(8,128)(2,1)} %bitcast.66), calls=%async_computation.2 | async-start | bytes 4194304 | tf_op jit(solution)/shard_map/all_to_all | solution.py:369
  194.4 5.1 %collective-permute-done.3.refs_1_ = s16[128,2048]{1,0:T(8,128)(2,1)S(1)} collective-permute-done((s16[128,2048]{1,0:T(8,128)(2,1)}, s16[128,2048]{1,0:T(8,128)(2,1)S(1)}, u32[]{:S(2)}, u32[]{:S(2)}) %collective-permute-start.3) | collective-permute-done | bytes 524320 | tf_op jit(solution)/shard_map/ppermute | solution.py:381
  199.5 13.3 %row_transform.4 = s16[8,4,2,128,128]{4,3,2,1,0:T(8,128)(2,1)S(1)} custom-call(s32[3]{0:T(128)S(1)} %pad_add_fusion.z_ref.kind_ref, bf16[128,256]{1,0:T(8,128)(2,1)S(1)} %copy-done.23, bf16[128,256]{1,0:T(8,128)(2,1)S(1)} %copy-done.21, f32[64,128]{1,0:T(8,128)S(1)} %get-tuple-element.33.cos_ref, f32[64,128]{1,0:T(8,128)S(1)} %get-tuple-element.32.sin_ref, ...), custom_call_target="tpu_custom_call" | custom-call | flops 40265318400 | bytes 8388608 | tf_op jit(solution)/shard_map/row_transform/pallas_call | solution.py:205
  212.8 1.4 copy-done.13
  214.2 9.9 %all-to-all-done.2.refs_0_ = s16[16,2,2,128,128]{4,3,2,1,0:T(8,128)(2,1)} async-done(((s16[16,2,2,128,128]{4,3,2,1,0:T(8,128)(2,1)}), s16[16,2,2,128,128]{4,3,2,1,0:T(8,128)(2,1)}, u32[]{:S(2)}, u32[]{:S(2)}) %all-to-all-start.2) | async-done | bytes 2097184 | tf_op jit(solution)/shard_map/all_to_all | solution.py:369
  224.1 5.7 %all-to-all-start.3 = ((s16[16,2,2,128,128]{4,3,2,1,0:T(8,128)(2,1)}), s16[16,2,2,128,128]{4,3,2,1,0:T(8,128)(2,1)}, u32[]{:S(2)}, u32[]{:S(2)}) async-start(s16[16,2,2,128,128]{4,3,2,1,0:T(8,128)(2,1)} %bitcast.67), calls=%async_computation.3 | async-start | bytes 4194304 | tf_op jit(solution)/shard_map/all_to_all | solution.py:369
  229.9 5.5 %column_mix.5.refs_1_ = f32[16,2,256,128]{3,2,1,0:T(8,128)S(1)} custom-call(s32[3]{0:T(128)S(1)} %pad_add_fusion.z_ref.kind_ref, bf16[256,256]{1,0:T(8,128)(2,1)S(1)} %copy-done.15, bf16[256,256]{1,0:T(8,128)(2,1)S(1)} %copy-done.14, f32[64,128]{1,0:T(8,128)S(1)} %copy-done.17, f32[64,128]{1,0:T(8,128)S(1)} %copy-done.16, ...), custom_call_target="tpu_custom_call" | custom-call | bytes 1024 | tf_op jit(solution)/shard_map/column_mix/pallas_call | solution.py:255
  235.4 2.0 copy-done.4
  237.4 6.1 %column_mix.6.refs_2_ = f32[16,2,256,128]{3,2,1,0:T(8,128)S(1)} custom-call(s32[3]{0:T(128)S(1)} %pad_add_fusion.z_ref.kind_ref, bf16[256,256]{1,0:T(8,128)(2,1)S(1)} %copy-done.15, bf16[256,256]{1,0:T(8,128)(2,1)S(1)} %copy-done.14, f32[64,128]{1,0:T(8,128)S(1)} %copy-done.17, f32[64,128]{1,0:T(8,128)S(1)} %copy-done.16, ...), custom_call_target="tpu_custom_call" | custom-call | bytes 1024 | tf_op jit(solution)/shard_map/column_mix/pallas_call | solution.py:255
  243.5 2.0 copy-done.6
  245.5 6.1 %column_mix.7.refs_3_ = f32[16,2,256,128]{3,2,1,0:T(8,128)S(1)} custom-call(s32[3]{0:T(128)S(1)} %pad_add_fusion.z_ref.kind_ref, bf16[256,256]{1,0:T(8,128)(2,1)S(1)} %copy-done.15, bf16[256,256]{1,0:T(8,128)(2,1)S(1)} %copy-done.14, f32[64,128]{1,0:T(8,128)S(1)} %copy-done.17, f32[64,128]{1,0:T(8,128)S(1)} %copy-done.16, ...), custom_call_target="tpu_custom_call" | custom-call | bytes 1024 | tf_op jit(solution)/shard_map/column_mix/pallas_call | solution.py:255
  251.6 2.0 copy-done.8
  253.6 3.4 %all-to-all-done.3.refs_0_ = s16[16,2,2,128,128]{4,3,2,1,0:T(8,128)(2,1)} async-done(((s16[16,2,2,128,128]{4,3,2,1,0:T(8,128)(2,1)}), s16[16,2,2,128,128]{4,3,2,1,0:T(8,128)(2,1)}, u32[]{:S(2)}, u32[]{:S(2)}) %all-to-all-start.3) | async-done | bytes 2097184 | tf_op jit(solution)/shard_map/all_to_all | solution.py:369
  257.0 6.2 %column_mix.4.refs_0_ = f32[16,2,256,128]{3,2,1,0:T(8,128)S(1)} custom-call(s32[3]{0:T(128)S(1)} %pad_add_fusion.z_ref.kind_ref, bf16[256,256]{1,0:T(8,128)(2,1)S(1)} %copy-done.15, bf16[256,256]{1,0:T(8,128)(2,1)S(1)} %copy-done.14, f32[64,128]{1,0:T(8,128)S(1)} %copy-done.17, f32[64,128]{1,0:T(8,128)S(1)} %copy-done.16, ...), custom_call_target="tpu_custom_call" | custom-call | bytes 1024 | tf_op jit(solution)/shard_map/column_mix/pallas_call | solution.py:255
  263.2 2.2 copy-done.7
  265.4 2.2 copy-done.9
  267.6 10.7 %column_finish.1 = (f32[256,8192]{1,0:T(8,128)}, f32[256,8192]{1,0:T(8,128)}) custom-call(f32[16,2,256,128]{3,2,1,0:T(8,128)S(1)} %column_mix.4.refs_0_, f32[16,2,256,128]{3,2,1,0:T(8,128)S(1)} %copy-done.5, f32[16,2,256,128]{3,2,1,0:T(8,128)S(1)} %copy-done.7, f32[16,2,256,128]{3,2,1,0:T(8,128)S(1)} %copy-done.9), custom_call_target="tpu_custom_call" | custom-call | tf_op jit(solution)/shard_map/column_finish/pallas_call | solution.py:302
  (61 shorter events, 0.4 us)
Async XLA Ops:
  1.9 2.2 copy-start
  5.9 10.9 %copy-start.24 = (f32[2,64,128]{2,1,0:T(8,128)S(1)}, f32[2,64,128]{2,1,0:T(8,128)}, u32[]{:S(2)}) copy-start(f32[2,64,128]{2,1,0:T(8,128)} %constant.64.clone) | copy-start | bytes 196612
  5.9 10.9 %copy-start.25 = (f32[2,64,128]{2,1,0:T(8,128)S(1)}, f32[2,64,128]{2,1,0:T(8,128)}, u32[]{:S(2)}) copy-start(f32[2,64,128]{2,1,0:T(8,128)} %constant.63.clone) | copy-start | bytes 196612
  6.8 24.2 %collective-permute-start.12 = (s16[128,2048]{1,0:T(8,128)(2,1)}, s16[128,2048]{1,0:T(8,128)(2,1)S(1)}, u32[]{:S(2)}, u32[]{:S(2)}) collective-permute-start(s16[128,2048]{1,0:T(8,128)(2,1)} %get-tuple-element.20), channel_id=1, source_target_pairs={{0,3},{1,2},{2,1},{3,0},{4,7},{5,6},{6,5},{7,4},{8,11},{9,10},{10,... | collective-permute-start | bytes 1572872 | tf_op jit(solution)/shard_map/ppermute | solution.py:381
  6.9 24.3 %collective-permute-start.10 = (s16[128,2048]{1,0:T(8,128)(2,1)}, s16[128,2048]{1,0:T(8,128)(2,1)S(1)}, u32[]{:S(2)}, u32[]{:S(2)}) collective-permute-start(s16[128,2048]{1,0:T(8,128)(2,1)} %get-tuple-element.20), channel_id=1, source_target_pairs={{0,1},{1,0},{2,3},{3,2},{4,5},{5,4},{6,7},{7,6},{8,9},{9,8},{10,11... | collective-permute-start | bytes 1572872 | tf_op jit(solution)/shard_map/ppermute | solution.py:381
  8.1 43.6 %collective-permute-start.11 = (s16[128,2048]{1,0:T(8,128)(2,1)S(1)}, s16[128,2048]{1,0:T(8,128)(2,1)S(1)}, u32[]{:S(2)}, u32[]{:S(2)}) collective-permute-start(s16[128,2048]{1,0:T(8,128)(2,1)S(1)} %get-tuple-element.21.refs_0_), channel_id=1, source_target_pairs={{0,2},{1,3},{2,0},{3,1},{4,6},{5,7},{6,4},{7,5},{8,10},{9,11},{10,... | collective-permute-start | bytes 1572872 | tf_op jit(solution)/shard_map/ppermute | solution.py:381
  12.3 5.0 %collective-permute-start = (bf16[1,2048]{1,0:T(2,128)(2,1)S(1)}, bf16[1,2048]{1,0:T(2,128)(2,1)S(1)}, u32[]{:S(2)}, u32[]{:S(2)}) collective-permute-start(bf16[1,2048]{1,0:T(2,128)(2,1)S(1)} %slice.129), channel_id=1, source_target_pairs={{0,4},{4,8},{8,12},{12,16},{16,20},{20,24},{24,28},{1,5},{5,9},{9,... | collective-permute-start | bytes 12296 | tf_op jit(solution)/shard_map/ppermute | solution.py:395
  17.3 2.2 copy-start.1
  21.3 30.4 %copy-start.20 = (bf16[128,256]{1,0:T(8,128)(2,1)S(1)}, bf16[128,256]{1,0:T(8,128)(2,1)}, u32[]{:S(2)}) copy-start(bf16[128,256]{1,0:T(8,128)(2,1)} %constant.66.clone.low_ref) | copy-start | bytes 196612
  21.3 30.4 %copy-start.22 = (bf16[128,256]{1,0:T(8,128)(2,1)S(1)}, bf16[128,256]{1,0:T(8,128)(2,1)}, u32[]{:S(2)}) copy-start(bf16[128,256]{1,0:T(8,128)(2,1)} %constant.65.clone.high_ref) | copy-start | bytes 196612
  22.4 74.3 %collective-permute-start.8 = (s16[128,2048]{1,0:T(8,128)(2,1)}, s16[128,2048]{1,0:T(8,128)(2,1)}, u32[]{:S(2)}, u32[]{:S(2)}) collective-permute-start(s16[128,2048]{1,0:T(8,128)(2,1)} %get-tuple-element.23), channel_id=1, source_target_pairs={{0,1},{1,0},{2,3},{3,2},{4,5},{5,4},{6,7},{7,6},{8,9},{9,8},{10,11... | collective-permute-start | bytes 1572872 | tf_op jit(solution)/shard_map/ppermute | solution.py:381
  24.2 63.2 %collective-permute-start.1 = (s16[128,2048]{1,0:T(8,128)(2,1)}, s16[128,2048]{1,0:T(8,128)(2,1)}, u32[]{:S(2)}, u32[]{:S(2)}) collective-permute-start(s16[128,2048]{1,0:T(8,128)(2,1)} %get-tuple-element.23), channel_id=1, source_target_pairs={{0,3},{1,2},{2,1},{3,0},{4,7},{5,6},{6,5},{7,4},{8,11},{9,10},{10,... | collective-permute-start | bytes 1572872 | tf_op jit(solution)/shard_map/ppermute | solution.py:381
  31.0 65.7 %collective-permute-start.9 = (s16[128,2048]{1,0:T(8,128)(2,1)}, s16[128,2048]{1,0:T(8,128)(2,1)}, u32[]{:S(2)}, u32[]{:S(2)}) collective-permute-start(s16[128,2048]{1,0:T(8,128)(2,1)} %get-tuple-element.22.refs_0_), channel_id=1, source_target_pairs={{0,2},{1,3},{2,0},{3,1},{4,6},{5,7},{6,4},{7,5},{8,10},{9,11},{10,... | collective-permute-start | bytes 1572872 | tf_op jit(solution)/shard_map/ppermute | solution.py:381
  64.3 1.3 copy-start.10
  65.6 48.8 %all-to-all-start = ((s16[16,2,2,128,128]{4,3,2,1,0:T(8,128)(2,1)}), s16[16,2,2,128,128]{4,3,2,1,0:T(8,128)(2,1)S(1)}, u32[]{:S(2)}, u32[]{:S(2)}) async-start(s16[16,2,2,128,128]{4,3,2,1,0:T(8,128)(2,1)} %bitcast.64), calls=%async_computation | async-start | bytes 4194304 | tf_op jit(solution)/shard_map/all_to_all | solution.py:369
  87.3 2.2 copy-start.2
  92.4 49.3 %collective-permute-start.6 = (s16[128,2048]{1,0:T(8,128)(2,1)}, s16[128,2048]{1,0:T(8,128)(2,1)}, u32[]{:S(2)}, u32[]{:S(2)}) collective-permute-start(s16[128,2048]{1,0:T(8,128)(2,1)} %get-tuple-element.25), channel_id=1, source_target_pairs={{0,1},{1,0},{2,3},{3,2},{4,5},{5,4},{6,7},{7,6},{8,9},{9,8},{10,11... | collective-permute-start | bytes 1572872 | tf_op jit(solution)/shard_map/ppermute | solution.py:381
  92.4 19.4 %collective-permute-start.2 = (s16[128,2048]{1,0:T(8,128)(2,1)}, s16[128,2048]{1,0:T(8,128)(2,1)S(1)}, u32[]{:S(2)}, u32[]{:S(2)}) collective-permute-start(s16[128,2048]{1,0:T(8,128)(2,1)} %get-tuple-element.25), channel_id=1, source_target_pairs={{0,3},{1,2},{2,1},{3,0},{4,7},{5,6},{6,5},{7,4},{8,11},{9,10},{10,... | collective-permute-start | bytes 1572872 | tf_op jit(solution)/shard_map/ppermute | solution.py:381
  92.8 49.0 %collective-permute-start.7 = (s16[128,2048]{1,0:T(8,128)(2,1)}, s16[128,2048]{1,0:T(8,128)(2,1)}, u32[]{:S(2)}, u32[]{:S(2)}) collective-permute-start(s16[128,2048]{1,0:T(8,128)(2,1)} %get-tuple-element.24.refs_0_), channel_id=1, source_target_pairs={{0,2},{1,3},{2,0},{3,1},{4,6},{5,7},{6,4},{7,5},{8,10},{9,11},{10,... | collective-permute-start | bytes 1572872 | tf_op jit(solution)/shard_map/ppermute | solution.py:381
  96.7 15.9 %copy-start.3 = (bf16[1024,2048]{1,0:T(8,128)(2,1)S(1)}, bf16[1024,2048]{1,0:T(8,128)(2,1)}, u32[]{:S(2)}) copy-start(bf16[1024,2048]{1,0:T(8,128)(2,1)} %param.10) | copy-start | bytes 12582916
  110.5 1.3 copy-start.11
  111.8 0.8 copy-start.18
  114.4 73.8 %all-to-all-start.1 = ((s16[16,2,2,128,128]{4,3,2,1,0:T(8,128)(2,1)}), s16[16,2,2,128,128]{4,3,2,1,0:T(8,128)(2,1)}, u32[]{:S(2)}, u32[]{:S(2)}) async-start(s16[16,2,2,128,128]{4,3,2,1,0:T(8,128)(2,1)} %bitcast.65), calls=%async_computation.1 | async-start | bytes 4194304 | tf_op jit(solution)/shard_map/all_to_all | solution.py:369
  132.9 8.8 %copy-start.19 = (s16[128,2048]{1,0:T(8,128)(2,1)S(1)}, s16[128,2048]{1,0:T(8,128)(2,1)}, u32[]{:S(2)}) copy-start(s16[128,2048]{1,0:T(8,128)(2,1)} %copy-done.18) | copy-start | bytes 1572868
  132.9 8.8 %copy-start.21 = (bf16[128,256]{1,0:T(8,128)(2,1)S(1)}, bf16[128,256]{1,0:T(8,128)(2,1)}, u32[]{:S(2)}) copy-start(bf16[128,256]{1,0:T(8,128)(2,1)} %constant.66.clone.low_ref) | copy-start | bytes 196612
  132.9 8.8 %copy-start.23 = (bf16[128,256]{1,0:T(8,128)(2,1)S(1)}, bf16[128,256]{1,0:T(8,128)(2,1)}, u32[]{:S(2)}) copy-start(bf16[128,256]{1,0:T(8,128)(2,1)} %constant.65.clone.high_ref) | copy-start | bytes 196612
  134.0 60.4 %collective-permute-start.5 = (s16[128,2048]{1,0:T(8,128)(2,1)}, s16[128,2048]{1,0:T(8,128)(2,1)S(1)}, u32[]{:S(2)}, u32[]{:S(2)}) collective-permute-start(s16[128,2048]{1,0:T(8,128)(2,1)} %get-tuple-element.26), channel_id=1, source_target_pairs={{0,3},{1,2},{2,1},{3,0},{4,7},{5,6},{6,5},{7,4},{8,11},{9,10},{10,... | collective-permute-start | bytes 1572872 | tf_op jit(solution)/shard_map/ppermute | solution.py:381
  136.0 63.5 %collective-permute-start.3 = (s16[128,2048]{1,0:T(8,128)(2,1)}, s16[128,2048]{1,0:T(8,128)(2,1)S(1)}, u32[]{:S(2)}, u32[]{:S(2)}) collective-permute-start(s16[128,2048]{1,0:T(8,128)(2,1)} %get-tuple-element.26), channel_id=1, source_target_pairs={{0,1},{1,0},{2,3},{3,2},{4,5},{5,4},{6,7},{7,6},{8,9},{9,8},{10,11... | collective-permute-start | bytes 1572872 | tf_op jit(solution)/shard_map/ppermute | solution.py:381
  137.0 62.5 %collective-permute-start.4 = (s16[128,2048]{1,0:T(8,128)(2,1)}, s16[128,2048]{1,0:T(8,128)(2,1)}, u32[]{:S(2)}, u32[]{:S(2)}) collective-permute-start(s16[128,2048]{1,0:T(8,128)(2,1)} %get-tuple-element.27.refs_0_), channel_id=1, source_target_pairs={{0,2},{1,3},{2,0},{3,1},{4,6},{5,7},{6,4},{7,5},{8,10},{9,11},{10,... | collective-permute-start | bytes 1572872 | tf_op jit(solution)/shard_map/ppermute | solution.py:381
  155.2 1.3 copy-start.12
  188.3 35.9 %all-to-all-start.2 = ((s16[16,2,2,128,128]{4,3,2,1,0:T(8,128)(2,1)}), s16[16,2,2,128,128]{4,3,2,1,0:T(8,128)(2,1)}, u32[]{:S(2)}, u32[]{:S(2)}) async-start(s16[16,2,2,128,128]{4,3,2,1,0:T(8,128)(2,1)} %bitcast.66), calls=%async_computation.2 | async-start | bytes 4194304 | tf_op jit(solution)/shard_map/all_to_all | solution.py:369
  212.8 1.4 copy-start.13
  224.1 5.8 %copy-start.14 = (bf16[256,256]{1,0:T(8,128)(2,1)S(1)}, bf16[256,256]{1,0:T(8,128)(2,1)}, u32[]{:S(2)}) copy-start(bf16[256,256]{1,0:T(8,128)(2,1)} %constant.68.clone.low_ref) | copy-start | bytes 393220
  224.1 5.8 %copy-start.15 = (bf16[256,256]{1,0:T(8,128)(2,1)S(1)}, bf16[256,256]{1,0:T(8,128)(2,1)}, u32[]{:S(2)}) copy-start(bf16[256,256]{1,0:T(8,128)(2,1)} %constant.67.clone.high_ref) | copy-start | bytes 393220
  224.1 5.8 %copy-start.16 = (f32[64,128]{1,0:T(8,128)S(1)}, f32[64,128]{1,0:T(8,128)}, u32[]{:S(2)}) copy-start(f32[64,128]{1,0:T(8,128)} %constant.70.clone.sin_ref) | copy-start | bytes 98308
  224.1 5.8 %copy-start.17 = (f32[64,128]{1,0:T(8,128)S(1)}, f32[64,128]{1,0:T(8,128)}, u32[]{:S(2)}) copy-start(f32[64,128]{1,0:T(8,128)} %constant.69.clone.cos_ref) | copy-start | bytes 98308
  224.1 32.8 %all-to-all-start.3 = ((s16[16,2,2,128,128]{4,3,2,1,0:T(8,128)(2,1)}), s16[16,2,2,128,128]{4,3,2,1,0:T(8,128)(2,1)}, u32[]{:S(2)}, u32[]{:S(2)}) async-start(s16[16,2,2,128,128]{4,3,2,1,0:T(8,128)(2,1)} %bitcast.67), calls=%async_computation.3 | async-start | bytes 4194304 | tf_op jit(solution)/shard_map/all_to_all | solution.py:369
  235.4 2.0 copy-start.4
  243.5 2.0 copy-start.6
  251.6 2.0 copy-start.8
  257.0 6.2 %copy-start.5 = (f32[16,2,256,128]{3,2,1,0:T(8,128)S(1)}, f32[16,2,256,128]{3,2,1,0:T(8,128)}, u32[]{:S(2)}) copy-start(f32[16,2,256,128]{3,2,1,0:T(8,128)} %copy-done.4) | copy-start | bytes 12582916
  263.2 2.2 copy-start.7
  265.4 2.2 copy-start.9

commit v4 on v2

--- a/solution.py
+++ b/solution.py
@@ -13,6 +13,7 @@
 BLOCK_ROWS = 16
 BLOCK_COLS = 128
 UNITS = 2048
+PAD = 8
 f32 = jnp.float32
 bf16 = jnp.bfloat16
 
@@ -73,12 +74,13 @@
     return (low + high)[:keep]
 
 
-def step_kernel(first, z_ref, scale_ref, before_scale_ref, halo_ref, now_ref, before_ref, out_ref):
+def step_kernel(first, offset, z_ref, scale_ref, before_scale_ref, halo_ref, now_ref, before_ref, *out_refs):
     lines, _, segment, width = now_ref.shape[1:]
     groups = segment // BLOCK_ROWS
+    size = out_refs[0].shape[0] // lines
     starts = lax.broadcasted_iota(jnp.int32, (segment, LANES), 0) == 0
 
-    def take(block, carry):
+    def take(block, carry, out_ref):
         here = pl.ds(pl.multiple_of(block * LANES, LANES), LANES)
         last = halo_ref[0, :, here]
         for line in range(lines):
@@ -90,21 +92,26 @@
             above = last if first else ends
             last = ends
             change = value - jnp.where(starts, above, pltpu.roll(value, 1, 0))
-            out_ref[0, line * segment : (line + 1) * segment, here] = change.astype(jnp.int32).astype(jnp.int16)
-        return carry
-
-    lax.fori_loop(0, width // LANES, take, 0)
-
-
-def step_rows(z, by_kind, scales, halo, chunk):
+            change = change[offset : offset + size].astype(jnp.int32).astype(jnp.int16)
+            out_ref[line * size : (line + 1) * size, here] = change
+        return carry
+
+    for k, out_ref in enumerate(out_refs):
+
+        @pl.when(pl.program_id(0) == k)
+        def _(out_ref=out_ref):
+            lax.fori_loop(0, width // LANES, functools.partial(take, out_ref=out_ref), 0)
+
+
+def step_rows(z, by_kind, scales, halo, chunk, offset, size):
     kinds, lines, chunks, segment, width = by_kind.shape
     before = (chunk - 1) % chunks
     kind = lambda k, z: lax.rem(lax.bitwise_xor(z[0], k), kinds)
     block = (1, lines, 1, segment, width)
     row_block = (1,) + scales.shape[2:]
     return pl.pallas_call(
-        functools.partial(step_kernel, chunk == 0),
-        out_shape=jax.ShapeDtypeStruct((kinds, lines * segment, width), jnp.int16),
+        functools.partial(step_kernel, chunk == 0, offset),
+        out_shape=[jax.ShapeDtypeStruct((lines * size, width), jnp.int16)] * kinds,
         grid_spec=pltpu.PrefetchScalarGridSpec(
             num_scalar_prefetch=1,
             grid=(kinds,),
@@ -115,9 +122,9 @@
                 pl.BlockSpec(block, lambda k, z: (kind(k, z), 0, chunk, 0, 0)),
                 pl.BlockSpec(block, lambda k, z: (kind(k, z), 0, before, 0, 0)),
             ],
-            out_specs=pl.BlockSpec((1, lines * segment, width), lambda k, z: (k, 0, 0)),
+            out_specs=[pl.BlockSpec((lines * size, width), lambda k, z: (0, 0))] * kinds,
         ),
-        compiler_params=pltpu.CompilerParams(vmem_limit_bytes=32 * 1024 * 1024),
+        compiler_params=pltpu.CompilerParams(vmem_limit_bytes=20 * 1024 * 1024),
         cost_estimate=pl.CostEstimate(
             flops=0, bytes_accessed=1024, transcendentals=0
         ),
@@ -147,7 +154,7 @@
     rows, piece_cols = pieces[0].shape
     outer = cos_ref.shape[0]
     slabs, kept = out_ref.shape[:2]
-    pad = table.shape[0] - outer * LANES
+    pad = PAD
     z = z_ref[0]
     table[0:pad, :] = jnp.zeros((pad, rows), f32)
 
@@ -204,19 +211,19 @@
         in_specs=[pl.BlockSpec(memory_space=pltpu.SMEM)] + [vmem] * (4 + cols),
         out_specs=vmem,
         scratch_shapes=[
-            pltpu.VMEM((8 + total, rows), f32),
+            pltpu.VMEM((PAD + total + outer, rows), f32),
             pltpu.VMEM((outer, 2, rows, LANES), f32),
             pltpu.VMEM((kept, slabs, 2, 16, LANES), f32),
         ],
-        compiler_params=pltpu.CompilerParams(vmem_limit_bytes=48 * 1024 * 1024),
+        compiler_params=pltpu.CompilerParams(vmem_limit_bytes=24 * 1024 * 1024),
         cost_estimate=pl.CostEstimate(
-            flops=800 * rows * total * LANES, bytes_accessed=rows * total * 8, transcendentals=0
+            flops=300 * rows * total * LANES, bytes_accessed=rows * total * 8, transcendentals=0
         ),
         name="row_transform",
     )(z, *tables, *pieces)
 
 
-def column_kernel(first, high_ref, low_ref, cos_ref, sin_ref, in_ref, out_ref, real, imag):
+def mix_chunk(first, high_ref, low_ref, cos_ref, sin_ref, in_ref, out_ref, real, imag):
     sources, _, _, rows, width = in_ref.shape
     count = out_ref.shape[0]
 
@@ -225,8 +232,6 @@
         real[here, :] = decode(in_ref[source, 0, 0])
         imag[here, :] = decode(in_ref[source, 0, 1])
         return carry
-
-    lax.fori_loop(0, sources, take, 0)
 
     def mix(index, carry):
         here = pl.ds(index, LANES, stride=count)
@@ -238,6 +243,7 @@
         out_ref[index, 1] = spun_imag * cos - spun_real * sin
         return carry
 
+    lax.fori_loop(0, sources, take, 0)
     lax.fori_loop(0, count, mix, 0, unroll=8)
 
 
@@ -245,33 +251,41 @@
     sources, planes, _, rows, width = gathered.shape
     whole = lambda table: pl.BlockSpec(table.shape, lambda plane: (0, 0))
     return pl.pallas_call(
-        functools.partial(column_kernel, first),
+        functools.partial(mix_chunk, first),
         out_shape=jax.ShapeDtypeStruct((count, 2, planes * width, LANES), f32),
         grid=(planes,),
         in_specs=[whole(table) for table in tables]
         + [pl.BlockSpec((sources, 1, 2, rows, width), lambda plane: (0, plane, 0, 0, 0))],
         out_specs=pl.BlockSpec((count, 2, width, LANES), lambda plane: (0, 0, plane, 0)),
-        scratch_shapes=[pltpu.VMEM((sources * rows, width), f32)] * 2,
-        compiler_params=pltpu.CompilerParams(vmem_limit_bytes=56 * 1024 * 1024),
-        cost_estimate=pl.CostEstimate(
-            flops=0, bytes_accessed=1024, transcendentals=0
-        ),
+        scratch_shapes=[pltpu.VMEM((sources * rows + count, width), f32)] * 2,
+        compiler_params=pltpu.CompilerParams(vmem_limit_bytes=20 * 1024 * 1024),
+        cost_estimate=pl.CostEstimate(flops=0, bytes_accessed=1024, transcendentals=0),
         name="column_mix",
     )(*tables, gathered)
 
 
-def finish_kernel(outer, *refs):
-    parts, (real_ref, imag_ref, stage) = refs[:-3], refs[-3:]
-    count = parts[0].shape[0]
+def finish_kernel(outer, first, high_ref, low_ref, cos_ref, sin_ref, in_ref, *refs):
+    parts, (real_ref, imag_ref, stage, mixed, real, imag) = refs[:-6], refs[-6:]
+    count = mixed.shape[0]
+    size = real_ref.shape[0]
     radix = 1 << ((outer.bit_length() - 1) // 2)
     rest = outer // radix
 
+    @pl.when(pl.program_id(1) == 0)
+    def _():
+        mix_chunk(first, high_ref, low_ref, cos_ref, sin_ref, in_ref, mixed, real, imag)
+
+    places = [(part, index) for part in parts for index in range(part.shape[0])]
+    places[first:first] = [(mixed, index) for index in range(count)]
+
     def finish(tile, carry):
         here = pl.ds(pl.multiple_of(tile * 8, 8), 8)
+        there = pl.ds(pl.multiple_of(pl.program_id(1) * size + tile * 8, 8), 8)
 
         def load(index):
-            part = parts[index // count]
-            return part[index % count, 0, here, :], part[index % count, 1, here, :]
+            part, own = places[index]
+            lines = there if part is mixed else here
+            return part[own, 0, lines, :], part[own, 1, lines, :]
 
         for low in range(rest):
             values = dft([load(high * rest + low) for high in range(radix)])
@@ -284,26 +298,35 @@
                 real_ref[here, column : column + LANES], imag_ref[here, column : column + LANES] = value
         return carry
 
-    lax.fori_loop(0, real_ref.shape[0] // 8, finish, 0)
-
-
-def finish_columns(parts, outer):
-    slab = parts[0].shape[2]
-    tile = min(32, slab)
+    lax.fori_loop(0, size // 8, finish, 0)
+
+
+def finish_columns(gathered, tables, first, count, parts, outer):
+    sources, planes, _, rows, width = gathered.shape
+    tile = min(32, width)
+    steps = width // tile
     radix = 1 << ((outer.bit_length() - 1) // 2)
-    shape = jax.ShapeDtypeStruct((slab, outer * LANES), f32)
+    shape = jax.ShapeDtypeStruct((planes * width, outer * LANES), f32)
+    whole = lambda table: pl.BlockSpec(table.shape, lambda plane, step: (0, 0))
     return pl.pallas_call(
-        functools.partial(finish_kernel, outer),
+        functools.partial(finish_kernel, outer, first),
         out_shape=(shape, shape),
-        grid=(slab // tile,),
-        in_specs=[
-            pl.BlockSpec((part.shape[0], 2, tile, LANES), lambda step: (0, 0, step, 0)) for part in parts
+        grid=(planes, steps),
+        in_specs=[whole(table) for table in tables]
+        + [pl.BlockSpec((sources, 1, 2, rows, width), lambda plane, step: (0, plane, 0, 0, 0))]
+        + [
+            pl.BlockSpec((part.shape[0], 2, tile, LANES), lambda plane, step: (0, 0, plane * steps + step, 0))
+            for part in parts
         ],
-        out_specs=(pl.BlockSpec((tile, outer * LANES), lambda step: (step, 0)),) * 2,
-        scratch_shapes=[pltpu.VMEM((radix, outer // radix, 2, 8, LANES), f32)],
-        compiler_params=pltpu.CompilerParams(vmem_limit_bytes=48 * 1024 * 1024),
+        out_specs=(pl.BlockSpec((tile, outer * LANES), lambda plane, step: (plane * steps + step, 0)),) * 2,
+        scratch_shapes=[
+            pltpu.VMEM((radix, outer // radix, 2, 8, LANES), f32),
+            pltpu.VMEM((count, 2, width, LANES), f32),
+        ]
+        + [pltpu.VMEM((sources * rows + count, width), f32)] * 2,
+        compiler_params=pltpu.CompilerParams(vmem_limit_bytes=60 * 1024 * 1024),
         name="column_finish",
-    )(*parts)
+    )(*tables, gathered, *parts)
 
 
 def local(mantissa, exponents):
@@ -321,7 +344,6 @@
     kind_lines = lines // half
     chunks = kind_lines * outer // LANES
     count = outer // chunks
-    chunk_rows = kind_lines * count
 
     index = np.arange(LANES)
     angle = 2 * np.pi * (index[:, None] * index[None, :] % LANES) / LANES
@@ -344,10 +366,6 @@
     scales = jnp.repeat(scales.reshape(chunks, half, kind_lines * (count // BLOCK_ROWS), -1), BLOCK_COLS, axis=-1)
 
     by_kind = mantissa.reshape(half, kind_lines, chunks, count, local_cols)
-    ends = by_kind[:, -1, -1, -1].astype(f32) * scales[-1, :, -1]
-    above = lax.ppermute(ends[-1:].astype(bf16), "rows", [(at, at + 1) for at in range(slabs - 1)])
-    halo = jnp.concatenate((above.astype(f32), ends[:-1]), axis=0).reshape(half, 1, local_cols)
-
     word = jnp.full((1,), z, jnp.int32)
     groups = [
         [row * cols + col for row in range(slabs) for col in range(part * half, (part + 1) * half)]
@@ -357,42 +375,54 @@
     planes = slab // width
 
     def exchange(spectra):
+        rows = spectra.shape[3]
         if slab >= LANES:
-            spectra = spectra.reshape(slabs * half, planes, 2, chunk_rows, LANES)
+            spectra = spectra.reshape(slabs * half, planes, 2, rows, LANES)
         else:
-            spectra = spectra.reshape(slabs, kept, 2, chunk_rows, LANES // slab, slab)
-            spectra = spectra.transpose(0, 1, 4, 2, 3, 5).reshape(slabs * half, 1, 2, chunk_rows, slab)
+            spectra = spectra.reshape(slabs, kept, 2, rows, LANES // slab, slab)
+            spectra = spectra.transpose(0, 1, 4, 2, 3, 5).reshape(slabs * half, 1, 2, rows, slab)
         return lax.all_to_all(
             spectra, ("rows", "cols"), split_axis=0, concat_axis=0, tiled=True, axis_index_groups=groups
         )
 
-    order = [*range(1, chunks), 0]
+    order = [(chunk, 0, count) for chunk in (*range(1, chunks), 0)]
+    places = len(order)
     raw, gathered, parts = {}, {}, {}
 
     def send(place, source):
-        steps = step_rows(source, by_kind, scales, halo, order[place])
+        steps = step_rows(source, by_kind, scales, halo, *order[place])
         raw[place] = [
             lax.ppermute(steps[step % half], "cols", [(at, at ^ step) for at in range(cols)]) if step else steps[0]
             for step in range(cols)
         ]
 
     def mix(place):
-        chunk = order[place]
-        parts[chunk] = mix_columns(gathered[place], column_tables, chunk * count, count)
-
-    for place in range(min(2, chunks)):
+        chunk, offset, size = order[place]
+        first = chunk * count + offset
+        parts[first] = mix_columns(gathered[place], column_tables, first, size)
+
+    halo = jnp.zeros((half, 1, local_cols), f32)
+    if places > 1:
+        send(0, word)
+    last, _ = lax.optimization_barrier((by_kind[:, -1, -1, -1], raw[0][0] if raw else word))
+    ends = last.astype(f32) * scales[-1, :, -1]
+    above = lax.ppermute(ends[-1:].astype(bf16), "rows", [(at, at + 1) for at in range(slabs - 1)])
+    halo = jnp.concatenate((above.astype(f32), ends[:-1]), axis=0).reshape(half, 1, local_cols)
+
+    for place in range(places > 1, min(2, places)):
         send(place, word)
-    for place in range(chunks):
+    for place in range(places):
+        if 0 < place < places - 1:
+            source, *_ = lax.optimization_barrier((word, raw[place][3 % cols]))
+            send(place + 1, source)
         spectra = transform_rows(word, raw[place], row_tables, slabs, kept, outer)
-        if place + 2 < chunks:
-            source, spectra = lax.optimization_barrier((word, spectra))
-            send(place + 2, source)
         if place >= 1:
             spectra, gathered[place - 1] = lax.optimization_barrier((spectra, gathered[place - 1]))
             mix(place - 1)
         gathered[place] = exchange(spectra)
-    mix(chunks - 1)
-    return tuple(finish_columns([parts[chunk] for chunk in range(chunks)], outer))
+    last = order[-1][0] * count
+    parts = [parts[first] for first in sorted(parts)]
+    return tuple(finish_columns(gathered[places - 1], column_tables, last, count, parts, outer))
 
 
 def solution(mesh):

time: 307 us -> 281 us (0.915)
  waiting for transfers between devices: 142 us -> 93.2 us
  starting transfers between devices: 41.2 us -> 58 us
  local copies, waits for them, and re-layouts: 10.4 us -> 23.9 us
  Pallas kernels: 106 us -> 99.2 us
    all_to_all x4, waiting for transfers between devices: 74.2 us -> 46.3 us  [exchange(): lax.all_to_all(spectra, ('rows', 'cols'), split_axis=0, concat_axis=0, ti...]
    ppermute x12, waiting for transfers between devices: 67.8 us -> 46.6 us  [send(): lax.ppermute(steps[step % half], 'cols', [(at, at ^ step) for at in range...]
    all_to_all x4, starting transfers between devices: 21.7 us -> 39.5 us  [exchange(): lax.all_to_all(spectra, ('rows', 'cols'), split_axis=0, concat_axis=0, ti...]
    unnamed x22 -> x39, local copies, waits for them, and re-layouts: 6.56 us -> 20.1 us
    pallas_call x9 -> x8, Pallas kernels: 48.8 us -> 45.4 us  [the longest x1 20.7 us: finish_columns(): pl.pallas_call(functools.partial(finish_kernel, outer, first), out_shape=...]
    pallas_call x4, Pallas kernels: 56.8 us -> 53.8 us  [transform_rows(): pl.pallas_call(functools.partial(row_kernel, cols), out_shape=jax.ShapeDt...]
  transfers between devices with their start and end apart: 17 -> 17, of which waited for: 10 -> 11; matrix products, arithmetic and copies ran while one was open for 1% -> 2% of each run, Pallas kernels for 27% -> 28%
where the time goes in v4:
time: 281 us; the launch traced here: 277 us
  Pallas kernels  99.2 us (35%)
  waiting for transfers between devices  93.2 us (33%)
  starting transfers between devices  58 us (21%)
  local copies, waits for them, and re-layouts  23.9 us (9%)
    pallas_call x4, Pallas kernels, transform_rows(): pl.pallas_call(functools.partial(row_kernel, cols), out_shape=jax.ShapeDt...  53.8 us
    ppermute x12, waiting for transfers between devices, send(): lax.ppermute(steps[step % half], 'cols', [(at, at ^ step) for at in range...  46.6 us
    all_to_all x4, waiting for transfers between devices, exchange(): lax.all_to_all(spectra, ('rows', 'cols'), split_axis=0, concat_axis=0, ti...  46.3 us
    all_to_all x4, starting transfers between devices, exchange(): lax.all_to_all(spectra, ('rows', 'cols'), split_axis=0, concat_axis=0, ti...  39.5 us
    pallas_call x1, Pallas kernels, finish_columns(): pl.pallas_call(functools.partial(finish_kernel, outer, first), out_shape=...  20.7 us
    unnamed x39, local copies, waits for them, and re-layouts  20.1 us
    pallas_call x3, Pallas kernels, mix_columns(): pl.pallas_call(functools.partial(mix_chunk, first), out_shape=jax.ShapeDt...  17.1 us
    ppermute x12, starting transfers between devices, send(): lax.ppermute(steps[step % half], 'cols', [(at, at ^ step) for at in range...  14.3 us
  transfers between devices with their start and end apart: 17, of which 11 were waited for; matrix products, arithmetic and copies ran while one was open for 2% of the time, Pallas kernels for 28%

profile of v4, /device:TPU:17, one launch (start us, length us, event | category | flops | bytes accessed | tf_op | source)
XLA Modules:
  0.0 277.0 jit_solution(7648326231876493701)
XLA Ops:
  0.6 0.8 fusion.2
  1.5 0.1 copy.21
  1.6 0.1 copy.20
  1.7 0.1 broadcast_bitcast_fusion.1
  1.8 0.0 copy-start
  1.8 2.2 copy-done
  4.0 1.2 step_rows.4
  5.2 0.0 copy-start.17
  5.2 0.0 copy-start.18
  5.3 0.2 collective-permute-start.12
  5.5 1.2 collective-permute-start.10
  6.7 2.0 collective-permute-start.11
  8.8 1.0 broadcast_in_dim.33
  9.8 2.1 reshape.58
  11.9 0.7 fusion.3
  12.6 4.2 %collective-permute-start = (bf16[1,2048]{1,0:T(2,128)(2,1)S(1)}, bf16[1,2048]{1,0:T(2,128)(2,1)S(1)}, u32[]{:S(2)}, u32[]{:S(2)}) collective-permute-start(bf16[1,2048]{1,0:T(2,128)(2,1)S(1)} %slice.73), channel_id=1, source_target_pairs={{0,4},{4,8},{8,12},{12,16},{16,20},{20,24},{24,28},{1,5},{5,9},{9,... | collective-permute-start | bytes 12296 | tf_op jit(solution)/shard_map/ppermute | solution.py:409
  16.9 0.1 copy.23
  17.0 0.1 copy.19
  17.0 0.1 broadcast_bitcast_fusion
  17.2 0.4 collective-permute-done
  17.7 0.0 copy-start.1
  17.7 2.2 copy-done.1
  19.9 2.2 step_rows.5
  22.1 1.7 collective-permute-start.8
  23.9 5.5 %collective-permute-done.12.refs_3_ = s16[128,2048]{1,0:T(8,128)(2,1)S(1)} collective-permute-done((s16[128,2048]{1,0:T(8,128)(2,1)S(1)}, s16[128,2048]{1,0:T(8,128)(2,1)S(1)}, u32[]{:S(2)}, u32[]{:S(2)}) %collective-permute-start.12) | collective-permute-done | bytes 524320 | tf_op jit(solution)/shard_map/ppermute | solution.py:395
  29.4 0.2 collective-permute-done.10.refs_1_
  29.6 20.4 %collective-permute-done.11.refs_2_ = s16[128,2048]{1,0:T(8,128)(2,1)} collective-permute-done((s16[128,2048]{1,0:T(8,128)(2,1)S(1)}, s16[128,2048]{1,0:T(8,128)(2,1)}, u32[]{:S(2)}, u32[]{:S(2)}) %collective-permute-start.11) | collective-permute-done | bytes 524320 | tf_op jit(solution)/shard_map/ppermute | solution.py:395
  50.0 13.1 %row_transform.7 = s16[8,4,2,128,128]{4,3,2,1,0:T(8,128)(2,1)S(1)} custom-call(s32[1]{0:T(128)} %bitcast.z_ref, bf16[128,256]{1,0:T(8,128)(2,1)S(1)} %copy-done.16, bf16[128,256]{1,0:T(8,128)(2,1)S(1)} %copy-done.15, f32[64,128]{1,0:T(8,128)S(1)} %get-tuple-element.41.cos_ref, f32[64,128]{1,0:T(8,128)S(1)} %get-tuple-element.40.sin_ref, ...), custom_call_target="tpu_custom_call" | custom-call | flops 40265318400 | bytes 8388608 | tf_op jit(solution)/shard_map/row_transform/pallas_call | solution.py:208
  63.2 0.0 copy-start.10
  63.2 1.3 copy-done.10
  64.5 9.6 %all-to-all-start = ((s16[16,2,2,128,128]{4,3,2,1,0:T(8,128)(2,1)}), s16[16,2,2,128,128]{4,3,2,1,0:T(8,128)(2,1)S(1)}, u32[]{:S(2)}, u32[]{:S(2)}) async-start(s16[16,2,2,128,128]{4,3,2,1,0:T(8,128)(2,1)} %bitcast.48), calls=%async_computation | async-start | bytes 4194304 | tf_op jit(solution)/shard_map/all_to_all | solution.py:384
  74.0 11.6 %collective-permute-done.1.refs_3_ = s16[128,2048]{1,0:T(8,128)(2,1)} collective-permute-done((s16[128,2048]{1,0:T(8,128)(2,1)}, s16[128,2048]{1,0:T(8,128)(2,1)}, u32[]{:S(2)}, u32[]{:S(2)}) %collective-permute-start.1) | collective-permute-done | bytes 524320 | tf_op jit(solution)/shard_map/ppermute | solution.py:395
  85.7 2.2 copy-done.2
  87.9 2.0 step_rows.6
  89.9 0.4 collective-permute-start.2
  90.2 3.2 %collective-permute-start.7 = (s16[128,2048]{1,0:T(8,128)(2,1)S(1)}, s16[128,2048]{1,0:T(8,128)(2,1)}, u32[]{:S(2)}, u32[]{:S(2)}) collective-permute-start(s16[128,2048]{1,0:T(8,128)(2,1)S(1)} %get-tuple-element.27.refs_0_), channel_id=1, source_target_pairs={{0,2},{1,3},{2,0},{3,1},{4,6},{5,7},{6,4},{7,5},{8,10},{9,11},{10,... | collective-permute-start | bytes 1572872 | tf_op jit(solution)/shard_map/ppermute | solution.py:395
  93.4 1.6 collective-permute-done.9.refs_2_
  95.1 13.6 %row_transform.6 = s16[8,4,2,128,128]{4,3,2,1,0:T(8,128)(2,1)S(1)} custom-call(s32[1]{0:T(128)} %bitcast.z_ref, bf16[128,256]{1,0:T(8,128)(2,1)S(1)} %copy-done.16, bf16[128,256]{1,0:T(8,128)(2,1)S(1)} %copy-done.15, f32[64,128]{1,0:T(8,128)S(1)} %get-tuple-element.41.cos_ref, f32[64,128]{1,0:T(8,128)S(1)} %get-tuple-element.40.sin_ref, ...), custom_call_target="tpu_custom_call" | custom-call | flops 40265318400 | bytes 8388608 | tf_op jit(solution)/shard_map/row_transform/pallas_call | solution.py:208
  108.7 1.3 copy-done.9
  110.0 18.1 %all-to-all-start.1 = ((s16[16,2,2,128,128]{4,3,2,1,0:T(8,128)(2,1)}), s16[16,2,2,128,128]{4,3,2,1,0:T(8,128)(2,1)}, u32[]{:S(2)}, u32[]{:S(2)}) async-start(s16[16,2,2,128,128]{4,3,2,1,0:T(8,128)(2,1)} %bitcast.47), calls=%async_computation.1 | async-start | bytes 4194304 | tf_op jit(solution)/shard_map/all_to_all | solution.py:384
  128.1 2.2 copy-done.3
  130.3 2.2 step_rows.7
  132.4 4.3 %collective-permute-start.5 = (s16[128,2048]{1,0:T(8,128)(2,1)}, s16[128,2048]{1,0:T(8,128)(2,1)}, u32[]{:S(2)}, u32[]{:S(2)}) collective-permute-start(s16[128,2048]{1,0:T(8,128)(2,1)} %get-tuple-element.26), channel_id=1, source_target_pairs={{0,3},{1,2},{2,1},{3,0},{4,7},{5,6},{6,5},{7,4},{8,11},{9,10},{10,... | collective-permute-start | bytes 1572872 | tf_op jit(solution)/shard_map/ppermute | solution.py:395
  136.7 1.0 collective-permute-start.3
  137.7 0.2 collective-permute-start.4
  137.9 2.1 collective-permute-done.7.refs_2_
  140.0 13.4 %row_transform.5 = s16[8,4,2,128,128]{4,3,2,1,0:T(8,128)(2,1)S(1)} custom-call(s32[1]{0:T(128)} %bitcast.z_ref, bf16[128,256]{1,0:T(8,128)(2,1)S(1)} %copy-done.16, bf16[128,256]{1,0:T(8,128)(2,1)S(1)} %copy-done.15, f32[64,128]{1,0:T(8,128)S(1)} %get-tuple-element.41.cos_ref, f32[64,128]{1,0:T(8,128)S(1)} %get-tuple-element.40.sin_ref, ...), custom_call_target="tpu_custom_call" | custom-call | flops 40265318400 | bytes 8388608 | tf_op jit(solution)/shard_map/row_transform/pallas_call | solution.py:208
  153.4 1.4 copy-done.11
  154.8 32.7 %all-to-all-done.1.in_ref = s16[16,2,2,128,128]{4,3,2,1,0:T(8,128)(2,1)} async-done(((s16[16,2,2,128,128]{4,3,2,1,0:T(8,128)(2,1)}), s16[16,2,2,128,128]{4,3,2,1,0:T(8,128)(2,1)}, u32[]{:S(2)}, u32[]{:S(2)}) %all-to-all-start.1) | async-done | bytes 2097184 | tf_op jit(solution)/shard_map/all_to_all | solution.py:384
  187.6 6.1 %all-to-all-start.2 = ((s16[16,2,2,128,128]{4,3,2,1,0:T(8,128)(2,1)}), s16[16,2,2,128,128]{4,3,2,1,0:T(8,128)(2,1)}, u32[]{:S(2)}, u32[]{:S(2)}) async-start(s16[16,2,2,128,128]{4,3,2,1,0:T(8,128)(2,1)} %bitcast.49), calls=%async_computation.2 | async-start | bytes 4194304 | tf_op jit(solution)/shard_map/all_to_all | solution.py:384
  193.7 5.1 %collective-permute-done.3.refs_1_ = s16[128,2048]{1,0:T(8,128)(2,1)} collective-permute-done((s16[128,2048]{1,0:T(8,128)(2,1)}, s16[128,2048]{1,0:T(8,128)(2,1)}, u32[]{:S(2)}, u32[]{:S(2)}) %collective-permute-start.3) | collective-permute-done | bytes 524320 | tf_op jit(solution)/shard_map/ppermute | solution.py:395
  198.8 13.6 %row_transform.4 = s16[8,4,2,128,128]{4,3,2,1,0:T(8,128)(2,1)S(1)} custom-call(s32[1]{0:T(128)} %bitcast.z_ref, bf16[128,256]{1,0:T(8,128)(2,1)S(1)} %copy-done.16, bf16[128,256]{1,0:T(8,128)(2,1)S(1)} %copy-done.15, f32[64,128]{1,0:T(8,128)S(1)} %get-tuple-element.41.cos_ref, f32[64,128]{1,0:T(8,128)S(1)} %get-tuple-element.40.sin_ref, ...), custom_call_target="tpu_custom_call" | custom-call | flops 40265318400 | bytes 8388608 | tf_op jit(solution)/shard_map/row_transform/pallas_call | solution.py:208
  212.4 0.0 copy-start.12
  212.4 1.3 copy-done.12
  213.7 9.6 %all-to-all-done.2.in_ref = s16[16,2,2,128,128]{4,3,2,1,0:T(8,128)(2,1)} async-done(((s16[16,2,2,128,128]{4,3,2,1,0:T(8,128)(2,1)}), s16[16,2,2,128,128]{4,3,2,1,0:T(8,128)(2,1)}, u32[]{:S(2)}, u32[]{:S(2)}) %all-to-all-start.2) | async-done | bytes 2097184 | tf_op jit(solution)/shard_map/all_to_all | solution.py:384
  223.4 5.7 %all-to-all-start.3 = ((s16[16,2,2,128,128]{4,3,2,1,0:T(8,128)(2,1)}), s16[16,2,2,128,128]{4,3,2,1,0:T(8,128)(2,1)}, u32[]{:S(2)}, u32[]{:S(2)}) async-start(s16[16,2,2,128,128]{4,3,2,1,0:T(8,128)(2,1)} %bitcast.50), calls=%async_computation.3 | async-start | bytes 4194304 | tf_op jit(solution)/shard_map/all_to_all | solution.py:384
  229.1 5.0 %column_mix.3.refs_0_ = f32[16,2,256,128]{3,2,1,0:T(8,128)S(1)} custom-call(bf16[256,256]{1,0:T(8,128)(2,1)S(1)} %copy-done.8, bf16[256,256]{1,0:T(8,128)(2,1)S(1)} %copy-done.7, f32[64,128]{1,0:T(8,128)S(1)} %copy-done.14, f32[64,128]{1,0:T(8,128)S(1)} %copy-done.13, s16[16,2,2,128,128]{4,3,2,1,0:T(8,128)(2,1)S(1)} %all-to-all-done.in_ref), custom_call_target="tpu_custom_call" | custom-call | bytes 1024 | tf_op jit(solution)/shard_map/column_mix/pallas_call | solution.py:253
  234.2 2.0 copy-done.4
  236.1 6.1 %column_mix.4.refs_1_ = f32[16,2,256,128]{3,2,1,0:T(8,128)S(1)} custom-call(bf16[256,256]{1,0:T(8,128)(2,1)S(1)} %copy-done.8, bf16[256,256]{1,0:T(8,128)(2,1)S(1)} %copy-done.7, f32[64,128]{1,0:T(8,128)S(1)} %copy-done.14, f32[64,128]{1,0:T(8,128)S(1)} %copy-done.13, s16[16,2,2,128,128]{4,3,2,1,0:T(8,128)(2,1)} %all-to-all-done.1.in_ref), custom_call_target="tpu_custom_call" | custom-call | bytes 1024 | tf_op jit(solution)/shard_map/column_mix/pallas_call | solution.py:253
  242.2 2.0 copy-done.5
  244.2 6.1 %column_mix.5.refs_2_ = f32[16,2,256,128]{3,2,1,0:T(8,128)S(1)} custom-call(bf16[256,256]{1,0:T(8,128)(2,1)S(1)} %copy-done.8, bf16[256,256]{1,0:T(8,128)(2,1)S(1)} %copy-done.7, f32[64,128]{1,0:T(8,128)S(1)} %copy-done.14, f32[64,128]{1,0:T(8,128)S(1)} %copy-done.13, s16[16,2,2,128,128]{4,3,2,1,0:T(8,128)(2,1)} %all-to-all-done.2.in_ref), custom_call_target="tpu_custom_call" | custom-call | bytes 1024 | tf_op jit(solution)/shard_map/column_mix/pallas_call | solution.py:253
  250.3 2.0 copy-done.6
  252.3 3.9 %all-to-all-done.3.in_ref = s16[16,2,2,128,128]{4,3,2,1,0:T(8,128)(2,1)} async-done(((s16[16,2,2,128,128]{4,3,2,1,0:T(8,128)(2,1)}), s16[16,2,2,128,128]{4,3,2,1,0:T(8,128)(2,1)}, u32[]{:S(2)}, u32[]{:S(2)}) %all-to-all-start.3) | async-done | bytes 2097184 | tf_op jit(solution)/shard_map/all_to_all | solution.py:384
  256.2 20.7 %column_finish.1 = (f32[256,8192]{1,0:T(8,128)}, f32[256,8192]{1,0:T(8,128)}) custom-call(bf16[256,256]{1,0:T(8,128)(2,1)} %constant.56.clone.high_ref, bf16[256,256]{1,0:T(8,128)(2,1)} %constant.57.clone.low_ref, f32[64,128]{1,0:T(8,128)} %constant.58.clone.cos_ref, f32[64,128]{1,0:T(8,128)} %constant.59.clone.sin_ref, ...), custom_call_target="tpu_custom_call" | custom-call | tf_op jit(solution)/shard_map/column_finish/pallas_call | solution.py:311
  (41 shorter events, 0.2 us)
Async XLA Ops:
  1.8 2.2 copy-start
  5.2 11.9 %copy-start.17 = (f32[2,64,128]{2,1,0:T(8,128)S(1)}, f32[2,64,128]{2,1,0:T(8,128)}, u32[]{:S(2)}) copy-start(f32[2,64,128]{2,1,0:T(8,128)} %constant.53.clone) | copy-start | bytes 196612
  5.2 11.9 %copy-start.18 = (f32[2,64,128]{2,1,0:T(8,128)S(1)}, f32[2,64,128]{2,1,0:T(8,128)}, u32[]{:S(2)}) copy-start(f32[2,64,128]{2,1,0:T(8,128)} %constant.52.clone) | copy-start | bytes 196612
  5.3 24.1 %collective-permute-start.12 = (s16[128,2048]{1,0:T(8,128)(2,1)S(1)}, s16[128,2048]{1,0:T(8,128)(2,1)S(1)}, u32[]{:S(2)}, u32[]{:S(2)}) collective-permute-start(s16[128,2048]{1,0:T(8,128)(2,1)S(1)} %get-tuple-element.29), channel_id=1, source_target_pairs={{0,3},{1,2},{2,1},{3,0},{4,7},{5,6},{6,5},{7,4},{8,11},{9,10},{10,... | collective-permute-start | bytes 1572872 | tf_op jit(solution)/shard_map/ppermute | solution.py:395
  5.5 24.1 %collective-permute-start.10 = (s16[128,2048]{1,0:T(8,128)(2,1)S(1)}, s16[128,2048]{1,0:T(8,128)(2,1)S(1)}, u32[]{:S(2)}, u32[]{:S(2)}) collective-permute-start(s16[128,2048]{1,0:T(8,128)(2,1)S(1)} %get-tuple-element.29), channel_id=1, source_target_pairs={{0,1},{1,0},{2,3},{3,2},{4,5},{5,4},{6,7},{7,6},{8,9},{9,8},{10,11... | collective-permute-start | bytes 1572872 | tf_op jit(solution)/shard_map/ppermute | solution.py:395
  6.7 43.3 %collective-permute-start.11 = (s16[128,2048]{1,0:T(8,128)(2,1)S(1)}, s16[128,2048]{1,0:T(8,128)(2,1)}, u32[]{:S(2)}, u32[]{:S(2)}) collective-permute-start(s16[128,2048]{1,0:T(8,128)(2,1)S(1)} %get-tuple-element.19.refs_0_), channel_id=1, source_target_pairs={{0,2},{1,3},{2,0},{3,1},{4,6},{5,7},{6,4},{7,5},{8,10},{9,11},{10,... | collective-permute-start | bytes 1572872 | tf_op jit(solution)/shard_map/ppermute | solution.py:395
  12.6 5.0 %collective-permute-start = (bf16[1,2048]{1,0:T(2,128)(2,1)S(1)}, bf16[1,2048]{1,0:T(2,128)(2,1)S(1)}, u32[]{:S(2)}, u32[]{:S(2)}) collective-permute-start(bf16[1,2048]{1,0:T(2,128)(2,1)S(1)} %slice.73), channel_id=1, source_target_pairs={{0,4},{4,8},{8,12},{12,16},{16,20},{20,24},{24,28},{1,5},{5,9},{9,... | collective-permute-start | bytes 12296 | tf_op jit(solution)/shard_map/ppermute | solution.py:409
  17.7 2.2 copy-start.1
  19.9 30.1 %copy-start.15 = (bf16[128,256]{1,0:T(8,128)(2,1)S(1)}, bf16[128,256]{1,0:T(8,128)(2,1)}, u32[]{:S(2)}) copy-start(bf16[128,256]{1,0:T(8,128)(2,1)} %constant.55.clone.low_ref) | copy-start | bytes 196612
  19.9 30.1 %copy-start.16 = (bf16[128,256]{1,0:T(8,128)(2,1)S(1)}, bf16[128,256]{1,0:T(8,128)(2,1)}, u32[]{:S(2)}) copy-start(bf16[128,256]{1,0:T(8,128)(2,1)} %constant.54.clone.high_ref) | copy-start | bytes 196612
  22.1 71.3 %collective-permute-start.8 = (s16[128,2048]{1,0:T(8,128)(2,1)}, s16[128,2048]{1,0:T(8,128)(2,1)}, u32[]{:S(2)}, u32[]{:S(2)}) collective-permute-start(s16[128,2048]{1,0:T(8,128)(2,1)} %get-tuple-element.21), channel_id=1, source_target_pairs={{0,1},{1,0},{2,3},{3,2},{4,5},{5,4},{6,7},{7,6},{8,9},{9,8},{10,11... | collective-permute-start | bytes 1572872 | tf_op jit(solution)/shard_map/ppermute | solution.py:395
  23.9 61.8 %collective-permute-start.1 = (s16[128,2048]{1,0:T(8,128)(2,1)}, s16[128,2048]{1,0:T(8,128)(2,1)}, u32[]{:S(2)}, u32[]{:S(2)}) collective-permute-start(s16[128,2048]{1,0:T(8,128)(2,1)} %get-tuple-element.21), channel_id=1, source_target_pairs={{0,3},{1,2},{2,1},{3,0},{4,7},{5,6},{6,5},{7,4},{8,11},{9,10},{10,... | collective-permute-start | bytes 1572872 | tf_op jit(solution)/shard_map/ppermute | solution.py:395
  29.3 65.7 %collective-permute-start.9 = (s16[128,2048]{1,0:T(8,128)(2,1)}, s16[128,2048]{1,0:T(8,128)(2,1)}, u32[]{:S(2)}, u32[]{:S(2)}) collective-permute-start(s16[128,2048]{1,0:T(8,128)(2,1)} %get-tuple-element.28.refs_0_), channel_id=1, source_target_pairs={{0,2},{1,3},{2,0},{3,1},{4,6},{5,7},{6,4},{7,5},{8,10},{9,11},{10,... | collective-permute-start | bytes 1572872 | tf_op jit(solution)/shard_map/ppermute | solution.py:395
  63.2 1.3 copy-start.10
  64.5 45.5 %all-to-all-start = ((s16[16,2,2,128,128]{4,3,2,1,0:T(8,128)(2,1)}), s16[16,2,2,128,128]{4,3,2,1,0:T(8,128)(2,1)S(1)}, u32[]{:S(2)}, u32[]{:S(2)}) async-start(s16[16,2,2,128,128]{4,3,2,1,0:T(8,128)(2,1)} %bitcast.48), calls=%async_computation | async-start | bytes 4194304 | tf_op jit(solution)/shard_map/all_to_all | solution.py:384
  85.7 2.2 copy-start.2
  89.9 48.1 %collective-permute-start.6 = (s16[128,2048]{1,0:T(8,128)(2,1)}, s16[128,2048]{1,0:T(8,128)(2,1)}, u32[]{:S(2)}, u32[]{:S(2)}) collective-permute-start(s16[128,2048]{1,0:T(8,128)(2,1)} %get-tuple-element.23), channel_id=1, source_target_pairs={{0,1},{1,0},{2,3},{3,2},{4,5},{5,4},{6,7},{7,6},{8,9},{9,8},{10,11... | collective-permute-start | bytes 1572872 | tf_op jit(solution)/shard_map/ppermute | solution.py:395
  89.9 38.2 %collective-permute-start.2 = (s16[128,2048]{1,0:T(8,128)(2,1)}, s16[128,2048]{1,0:T(8,128)(2,1)}, u32[]{:S(2)}, u32[]{:S(2)}) collective-permute-start(s16[128,2048]{1,0:T(8,128)(2,1)} %get-tuple-element.23), channel_id=1, source_target_pairs={{0,3},{1,2},{2,1},{3,0},{4,7},{5,6},{6,5},{7,4},{8,11},{9,10},{10,... | collective-permute-start | bytes 1572872 | tf_op jit(solution)/shard_map/ppermute | solution.py:395
  90.2 49.8 %collective-permute-start.7 = (s16[128,2048]{1,0:T(8,128)(2,1)S(1)}, s16[128,2048]{1,0:T(8,128)(2,1)}, u32[]{:S(2)}, u32[]{:S(2)}) collective-permute-start(s16[128,2048]{1,0:T(8,128)(2,1)S(1)} %get-tuple-element.27.refs_0_), channel_id=1, source_target_pairs={{0,2},{1,3},{2,0},{3,1},{4,6},{5,7},{6,4},{7,5},{8,10},{9,11},{10,... | collective-permute-start | bytes 1572872 | tf_op jit(solution)/shard_map/ppermute | solution.py:395
  108.7 1.3 copy-start.9
  110.0 77.6 %all-to-all-start.1 = ((s16[16,2,2,128,128]{4,3,2,1,0:T(8,128)(2,1)}), s16[16,2,2,128,128]{4,3,2,1,0:T(8,128)(2,1)}, u32[]{:S(2)}, u32[]{:S(2)}) async-start(s16[16,2,2,128,128]{4,3,2,1,0:T(8,128)(2,1)} %bitcast.47), calls=%async_computation.1 | async-start | bytes 4194304 | tf_op jit(solution)/shard_map/all_to_all | solution.py:384
  128.1 2.2 copy-start.3
  132.4 61.3 %collective-permute-start.5 = (s16[128,2048]{1,0:T(8,128)(2,1)}, s16[128,2048]{1,0:T(8,128)(2,1)}, u32[]{:S(2)}, u32[]{:S(2)}) collective-permute-start(s16[128,2048]{1,0:T(8,128)(2,1)} %get-tuple-element.26), channel_id=1, source_target_pairs={{0,3},{1,2},{2,1},{3,0},{4,7},{5,6},{6,5},{7,4},{8,11},{9,10},{10,... | collective-permute-start | bytes 1572872 | tf_op jit(solution)/shard_map/ppermute | solution.py:395
  136.7 62.0 %collective-permute-start.3 = (s16[128,2048]{1,0:T(8,128)(2,1)}, s16[128,2048]{1,0:T(8,128)(2,1)}, u32[]{:S(2)}, u32[]{:S(2)}) collective-permute-start(s16[128,2048]{1,0:T(8,128)(2,1)} %get-tuple-element.26), channel_id=1, source_target_pairs={{0,1},{1,0},{2,3},{3,2},{4,5},{5,4},{6,7},{7,6},{8,9},{9,8},{10,11... | collective-permute-start | bytes 1572872 | tf_op jit(solution)/shard_map/ppermute | solution.py:395
  137.7 56.0 %collective-permute-start.4 = (s16[128,2048]{1,0:T(8,128)(2,1)}, s16[128,2048]{1,0:T(8,128)(2,1)}, u32[]{:S(2)}, u32[]{:S(2)}) collective-permute-start(s16[128,2048]{1,0:T(8,128)(2,1)} %get-tuple-element.25.refs_0_), channel_id=1, source_target_pairs={{0,2},{1,3},{2,0},{3,1},{4,6},{5,7},{6,4},{7,5},{8,10},{9,11},{10,... | collective-permute-start | bytes 1572872 | tf_op jit(solution)/shard_map/ppermute | solution.py:395
  153.4 1.4 copy-start.11
  187.6 35.8 %all-to-all-start.2 = ((s16[16,2,2,128,128]{4,3,2,1,0:T(8,128)(2,1)}), s16[16,2,2,128,128]{4,3,2,1,0:T(8,128)(2,1)}, u32[]{:S(2)}, u32[]{:S(2)}) async-start(s16[16,2,2,128,128]{4,3,2,1,0:T(8,128)(2,1)} %bitcast.49), calls=%async_computation.2 | async-start | bytes 4194304 | tf_op jit(solution)/shard_map/all_to_all | solution.py:384
  212.4 1.3 copy-start.12
  223.4 5.8 %copy-start.7 = (bf16[256,256]{1,0:T(8,128)(2,1)S(1)}, bf16[256,256]{1,0:T(8,128)(2,1)}, u32[]{:S(2)}) copy-start(bf16[256,256]{1,0:T(8,128)(2,1)} %constant.57.clone.low_ref) | copy-start | bytes 393220
  223.4 5.8 %copy-start.8 = (bf16[256,256]{1,0:T(8,128)(2,1)S(1)}, bf16[256,256]{1,0:T(8,128)(2,1)}, u32[]{:S(2)}) copy-start(bf16[256,256]{1,0:T(8,128)(2,1)} %constant.56.clone.high_ref) | copy-start | bytes 393220
  223.4 5.8 %copy-start.13 = (f32[64,128]{1,0:T(8,128)S(1)}, f32[64,128]{1,0:T(8,128)}, u32[]{:S(2)}) copy-start(f32[64,128]{1,0:T(8,128)} %constant.59.clone.sin_ref) | copy-start | bytes 98308
  223.4 5.8 %copy-start.14 = (f32[64,128]{1,0:T(8,128)S(1)}, f32[64,128]{1,0:T(8,128)}, u32[]{:S(2)}) copy-start(f32[64,128]{1,0:T(8,128)} %constant.58.clone.cos_ref) | copy-start | bytes 98308
  223.4 32.9 %all-to-all-start.3 = ((s16[16,2,2,128,128]{4,3,2,1,0:T(8,128)(2,1)}), s16[16,2,2,128,128]{4,3,2,1,0:T(8,128)(2,1)}, u32[]{:S(2)}, u32[]{:S(2)}) async-start(s16[16,2,2,128,128]{4,3,2,1,0:T(8,128)(2,1)} %bitcast.50), calls=%async_computation.3 | async-start | bytes 4194304 | tf_op jit(solution)/shard_map/all_to_all | solution.py:384
  234.1 2.0 copy-start.4
  242.2 2.0 copy-start.5
  250.3 2.0 copy-start.6

commit v5 on v4

--- a/solution.py
+++ b/solution.py
@@ -150,10 +150,11 @@
 
 
 def row_kernel(cols, z_ref, high_ref, low_ref, cos_ref, sin_ref, *refs):
-    pieces, (out_ref, table, mixed, stage) = refs[:cols], refs[cols:]
+    pieces, out_refs, (table, mixed, stage) = refs[:cols], refs[cols:-3], refs[-3:]
     rows, piece_cols = pieces[0].shape
     outer = cos_ref.shape[0]
-    slabs, kept = out_ref.shape[:2]
+    split_by = len(out_refs)
+    slabs, kept = out_refs[0].shape[0], out_refs[0].shape[1] * split_by
     pad = PAD
     z = z_ref[0]
     table[0:pad, :] = jnp.zeros((pad, rows), f32)
@@ -193,23 +194,24 @@
             for k, value in enumerate(dft(values, kept)):
                 stage[k, low, 0], stage[k, low, 1] = times(value, low * k, outer)
         for k in range(kept):
+            out_ref, place = out_refs[k % split_by], k // split_by
             for slab, value in enumerate(dft([(stage[k, low, 0], stage[k, low, 1]) for low in range(slabs)])):
-                out_ref[slab, k, 0, here, :], out_ref[slab, k, 1, here, :] = encode(value[0]), encode(value[1])
+                out_ref[slab, place, 0, here, :], out_ref[slab, place, 1, here, :] = encode(value[0]), encode(value[1])
         return carry
 
     lax.fori_loop(0, rows // 16, finish, 0)
 
 
-def transform_rows(z, pieces, tables, slabs, kept, outer):
+def transform_rows(z, pieces, tables, slabs, kept, outer, split_by=1):
     rows, piece_cols = pieces[0].shape
     cols = len(pieces)
     total = cols * piece_cols
     vmem = pl.BlockSpec(memory_space=pltpu.VMEM)
     return pl.pallas_call(
         functools.partial(row_kernel, cols),
-        out_shape=jax.ShapeDtypeStruct((slabs, kept, 2, rows, LANES), jnp.int16),
+        out_shape=[jax.ShapeDtypeStruct((slabs, kept // split_by, 2, rows, LANES), jnp.int16)] * split_by,
         in_specs=[pl.BlockSpec(memory_space=pltpu.SMEM)] + [vmem] * (4 + cols),
-        out_specs=vmem,
+        out_specs=[vmem] * split_by,
         scratch_shapes=[
             pltpu.VMEM((PAD + total + outer, rows), f32),
             pltpu.VMEM((outer, 2, rows, LANES), f32),
@@ -264,14 +266,13 @@
     )(*tables, gathered)
 
 
-def finish_kernel(outer, first, high_ref, low_ref, cos_ref, sin_ref, in_ref, *refs):
-    parts, (real_ref, imag_ref, stage, mixed, real, imag) = refs[:-6], refs[-6:]
-    count = mixed.shape[0]
+def finish_kernel(outer, first, count, filled, high_ref, low_ref, cos_ref, sin_ref, in_ref, *refs):
+    parts, (real_ref, imag_ref, stage, mixed, real, imag) = refs[: -6 - filled], refs[-6:]
     size = real_ref.shape[0]
     radix = 1 << ((outer.bit_length() - 1) // 2)
     rest = outer // radix
 
-    @pl.when(pl.program_id(1) == 0)
+    @pl.when(pl.program_id(0) == 0)
     def _():
         mix_chunk(first, high_ref, low_ref, cos_ref, sin_ref, in_ref, mixed, real, imag)
 
@@ -280,7 +281,7 @@
 
     def finish(tile, carry):
         here = pl.ds(pl.multiple_of(tile * 8, 8), 8)
-        there = pl.ds(pl.multiple_of(pl.program_id(1) * size + tile * 8, 8), 8)
+        there = pl.ds(pl.multiple_of(pl.program_id(0) * size + tile * 8, 8), 8)
 
         def load(index):
             part, own = places[index]
@@ -301,32 +302,35 @@
     lax.fori_loop(0, size // 8, finish, 0)
 
 
-def finish_columns(gathered, tables, first, count, parts, outer):
-    sources, planes, _, rows, width = gathered.shape
-    tile = min(32, width)
+def finish_columns(gathered, tables, first, count, parts, outer, plane, planes, filled):
+    sources, _, _, rows, width = gathered.shape
+    tile = min(64, width)
     steps = width // tile
     radix = 1 << ((outer.bit_length() - 1) // 2)
     shape = jax.ShapeDtypeStruct((planes * width, outer * LANES), f32)
-    whole = lambda table: pl.BlockSpec(table.shape, lambda plane, step: (0, 0))
+    whole = lambda table: pl.BlockSpec(table.shape, lambda step: (0,) * table.ndim)
+    arguments = (*tables, gathered, *parts, *filled)
     return pl.pallas_call(
-        functools.partial(finish_kernel, outer, first),
+        functools.partial(finish_kernel, outer, first, count, len(filled)),
         out_shape=(shape, shape),
-        grid=(planes, steps),
-        in_specs=[whole(table) for table in tables]
-        + [pl.BlockSpec((sources, 1, 2, rows, width), lambda plane, step: (0, plane, 0, 0, 0))]
+        grid=(steps,),
+        in_specs=[whole(table) for table in (*tables, gathered)]
         + [
-            pl.BlockSpec((part.shape[0], 2, tile, LANES), lambda plane, step: (0, 0, plane * steps + step, 0))
+            pl.BlockSpec((part.shape[0], 2, tile, LANES), lambda step: (0, 0, plane * steps + step, 0))
             for part in parts
-        ],
-        out_specs=(pl.BlockSpec((tile, outer * LANES), lambda plane, step: (plane * steps + step, 0)),) * 2,
+        ]
+        + [pl.BlockSpec(memory_space=pl.ANY)] * len(filled),
+        out_specs=(pl.BlockSpec((tile, outer * LANES), lambda step: (plane * steps + step, 0)),) * 2,
         scratch_shapes=[
             pltpu.VMEM((radix, outer // radix, 2, 8, LANES), f32),
             pltpu.VMEM((count, 2, width, LANES), f32),
         ]
         + [pltpu.VMEM((sources * rows + count, width), f32)] * 2,
+        input_output_aliases={len(arguments) - len(filled) + at: at for at in range(len(filled))},
         compiler_params=pltpu.CompilerParams(vmem_limit_bytes=60 * 1024 * 1024),
+        cost_estimate=pl.CostEstimate(flops=0, bytes_accessed=1024, transcendentals=0),
         name="column_finish",
-    )(*tables, gathered, *parts)
+    )(*arguments)
 
 
 def local(mantissa, exponents):
@@ -377,7 +381,7 @@
     def exchange(spectra):
         rows = spectra.shape[3]
         if slab >= LANES:
-            spectra = spectra.reshape(slabs * half, planes, 2, rows, LANES)
+            spectra = spectra.reshape(slabs * half, -1, 2, rows, LANES)
         else:
             spectra = spectra.reshape(slabs, kept, 2, rows, LANES // slab, slab)
             spectra = spectra.transpose(0, 1, 4, 2, 3, 5).reshape(slabs * half, 1, 2, rows, slab)
@@ -415,14 +419,27 @@
         if 0 < place < places - 1:
             source, *_ = lax.optimization_barrier((word, raw[place][3 % cols]))
             send(place + 1, source)
-        spectra = transform_rows(word, raw[place], row_tables, slabs, kept, outer)
+        spectra = transform_rows(
+            word, raw[place], row_tables, slabs, kept, outer, planes if place == places - 1 else 1
+        )
         if place >= 1:
-            spectra, gathered[place - 1] = lax.optimization_barrier((spectra, gathered[place - 1]))
+            *spectra, gathered[place - 1] = lax.optimization_barrier((*spectra, gathered[place - 1]))
             mix(place - 1)
-        gathered[place] = exchange(spectra)
-    last = order[-1][0] * count
-    parts = [parts[first] for first in sorted(parts)]
-    return tuple(finish_columns(gathered[places - 1], column_tables, last, count, parts, outer))
+        if place < places - 1:
+            if len(parts) >= 2:
+                at = next(iter(parts))
+                spectra[0], parts[at] = lax.optimization_barrier((spectra[0], parts[at]))
+            gathered[place] = exchange(spectra[0])
+    for plane in range(1, len(spectra)):
+        spectra[plane], *done = lax.optimization_barrier((spectra[plane], *parts.values()))
+        parts = dict(zip(parts, done))
+    gathered[places - 1] = [exchange(part) for part in spectra]
+    first = order[-1][0] * count
+    parts = [parts[at] for at in sorted(parts)]
+    filled = ()
+    for plane, last in enumerate(gathered[places - 1]):
+        filled = finish_columns(last, column_tables, first, count, parts, outer, plane, planes, filled)
+    return tuple(filled)
 
 
 def solution(mesh):

time: 281 us -> 278 us (0.989)
  waiting for transfers between devices: 93.2 us -> 85.9 us
  starting transfers between devices: 58 us -> 62.3 us
    all_to_all x4 -> x5, waiting for transfers between devices: 46.3 us -> 39.5 us  [exchange(): lax.all_to_all(spectra, ('rows', 'cols'), split_axis=0, concat_axis=0, ti...]
    all_to_all x4 -> x5, starting transfers between devices: 39.5 us -> 44.4 us  [exchange(): lax.all_to_all(spectra, ('rows', 'cols'), split_axis=0, concat_axis=0, ti...]
    pallas_call x5 -> x6, Pallas kernels: 74.5 us -> 75.4 us  [the longest x4 55 us: transform_rows(): pl.pallas_call(functools.partial(row_kernel, cols), out_shape=[jax.ShapeD...]
    unnamed x39 -> x45, local copies, waits for them, and re-layouts: 20.1 us -> 21.1 us
  transfers between devices with their start and end apart: 17 -> 18, of which waited for: 11 -> 11; matrix products, arithmetic and copies ran while one was open for 2% -> 2% of each run, Pallas kernels for 28% -> 32%
where the time goes in v5:
time: 278 us; the launch traced here: 275 us
  Pallas kernels  99.1 us (36%)
  waiting for transfers between devices  85.9 us (31%)
  starting transfers between devices  62.3 us (22%)
  local copies, waits for them, and re-layouts  24.9 us (9%)
    pallas_call x4, Pallas kernels, transform_rows(): pl.pallas_call(functools.partial(row_kernel, cols), out_shape=[jax.ShapeD...  55 us
    ppermute x12, waiting for transfers between devices, send(): lax.ppermute(steps[step % half], 'cols', [(at, at ^ step) for at in range...  45.9 us
    all_to_all x5, starting transfers between devices, exchange(): lax.all_to_all(spectra, ('rows', 'cols'), split_axis=0, concat_axis=0, ti...  44.4 us
    all_to_all x5, waiting for transfers between devices, exchange(): lax.all_to_all(spectra, ('rows', 'cols'), split_axis=0, concat_axis=0, ti...  39.5 us
    unnamed x45, local copies, waits for them, and re-layouts  21.1 us
    pallas_call x2, Pallas kernels, finish_columns(): pl.pallas_call(functools.partial(finish_kernel, outer, first, count, len(...  20.5 us
    pallas_call x3, Pallas kernels, mix_columns(): pl.pallas_call(functools.partial(mix_chunk, first), out_shape=jax.ShapeDt...  16 us
    ppermute x12, starting transfers between devices, send(): lax.ppermute(steps[step % half], 'cols', [(at, at ^ step) for at in range...  13.6 us
  transfers between devices with their start and end apart: 18, of which 11 were waited for; matrix products, arithmetic and copies ran while one was open for 2% of the time, Pallas kernels for 32%

profile of v5, /device:TPU:17, one launch (start us, length us, event | category | flops | bytes accessed | tf_op | source)
XLA Modules:
  0.0 274.7 jit_solution(13509645869014750672)
XLA Ops:
  0.6 0.8 fusion.2
  1.5 0.1 copy.23
  1.6 0.1 copy.22
  1.7 0.1 broadcast_bitcast_fusion.1
  1.8 0.0 copy-start
  1.8 2.2 copy-done
  4.0 1.2 step_rows.4
  5.2 0.2 collective-permute-start.12
  5.5 1.2 collective-permute-start.10
  6.7 2.0 collective-permute-start.11
  8.8 1.0 broadcast_in_dim.33
  9.8 2.1 reshape.61
  11.9 0.7 fusion.3
  12.6 4.2 %collective-permute-start = (bf16[1,2048]{1,0:T(2,128)(2,1)S(1)}, bf16[1,2048]{1,0:T(2,128)(2,1)S(1)}, u32[]{:S(2)}, u32[]{:S(2)}) collective-permute-start(bf16[1,2048]{1,0:T(2,128)(2,1)S(1)} %slice.73), channel_id=1, source_target_pairs={{0,4},{4,8},{8,12},{12,16},{16,20},{20,24},{24,28},{1,5},{5,9},{9,... | collective-permute-start | bytes 12296 | tf_op jit(solution)/shard_map/ppermute | solution.py:413
  16.9 0.1 copy.25
  16.9 0.1 copy.21
  17.0 0.1 broadcast_bitcast_fusion
  17.2 0.4 collective-permute-done
  17.7 0.0 copy-start.1
  17.7 2.2 copy-done.1
  19.9 2.2 step_rows.5
  22.1 1.7 collective-permute-start.8
  23.8 5.5 %collective-permute-done.12.refs_3_ = s16[128,2048]{1,0:T(8,128)(2,1)S(1)} collective-permute-done((s16[128,2048]{1,0:T(8,128)(2,1)S(1)}, s16[128,2048]{1,0:T(8,128)(2,1)S(1)}, u32[]{:S(2)}, u32[]{:S(2)}) %collective-permute-start.12) | collective-permute-done | bytes 524320 | tf_op jit(solution)/shard_map/ppermute | solution.py:399
  29.3 0.2 collective-permute-done.10.refs_1_
  29.6 20.4 %collective-permute-done.11.refs_2_ = s16[128,2048]{1,0:T(8,128)(2,1)} collective-permute-done((s16[128,2048]{1,0:T(8,128)(2,1)S(1)}, s16[128,2048]{1,0:T(8,128)(2,1)}, u32[]{:S(2)}, u32[]{:S(2)}) %collective-permute-start.11) | collective-permute-done | bytes 524320 | tf_op jit(solution)/shard_map/ppermute | solution.py:399
  50.0 13.1 %row_transform.7 = s16[8,4,2,128,128]{4,3,2,1,0:T(8,128)(2,1)S(1)} custom-call(s32[1]{0:T(128)} %bitcast.z_ref, bf16[128,256]{1,0:T(8,128)(2,1)S(1)} %copy-done.17, bf16[128,256]{1,0:T(8,128)(2,1)S(1)} %copy-done.16, f32[64,128]{1,0:T(8,128)S(1)} %get-tuple-element.63.cos_ref, f32[64,128]{1,0:T(8,128)S(1)} %get-tuple-element.62.sin_ref, ...), custom_call_target="tpu_custom_call" | custom-call | flops 40265318400 | bytes 8388608 | tf_op jit(solution)/shard_map/row_transform/pallas_call | solution.py:210
  63.2 1.3 copy-done.12
  64.5 9.6 %all-to-all-start = ((s16[16,2,2,128,128]{4,3,2,1,0:T(8,128)(2,1)}), s16[16,2,2,128,128]{4,3,2,1,0:T(8,128)(2,1)S(1)}, u32[]{:S(2)}, u32[]{:S(2)}) async-start(s16[16,2,2,128,128]{4,3,2,1,0:T(8,128)(2,1)} %bitcast.49), calls=%async_computation | async-start | bytes 4194304 | tf_op jit(solution)/shard_map/all_to_all | solution.py:388
  74.0 11.6 %collective-permute-done.1.refs_3_ = s16[128,2048]{1,0:T(8,128)(2,1)} collective-permute-done((s16[128,2048]{1,0:T(8,128)(2,1)}, s16[128,2048]{1,0:T(8,128)(2,1)}, u32[]{:S(2)}, u32[]{:S(2)}) %collective-permute-start.1) | collective-permute-done | bytes 524320 | tf_op jit(solution)/shard_map/ppermute | solution.py:399
  85.7 2.2 copy-done.2
  87.8 2.0 step_rows.6
  89.9 0.4 collective-permute-start.2
  90.2 3.2 %collective-permute-start.7 = (s16[128,2048]{1,0:T(8,128)(2,1)S(1)}, s16[128,2048]{1,0:T(8,128)(2,1)}, u32[]{:S(2)}, u32[]{:S(2)}) collective-permute-start(s16[128,2048]{1,0:T(8,128)(2,1)S(1)} %get-tuple-element.40.refs_0_), channel_id=1, source_target_pairs={{0,2},{1,3},{2,0},{3,1},{4,6},{5,7},{6,4},{7,5},{8,10},{9,11},{10,... | collective-permute-start | bytes 1572872 | tf_op jit(solution)/shard_map/ppermute | solution.py:399
  93.4 1.6 collective-permute-done.9.refs_2_
  95.0 13.6 %row_transform.6 = s16[8,4,2,128,128]{4,3,2,1,0:T(8,128)(2,1)S(1)} custom-call(s32[1]{0:T(128)} %bitcast.z_ref, bf16[128,256]{1,0:T(8,128)(2,1)S(1)} %copy-done.17, bf16[128,256]{1,0:T(8,128)(2,1)S(1)} %copy-done.16, f32[64,128]{1,0:T(8,128)S(1)} %get-tuple-element.63.cos_ref, f32[64,128]{1,0:T(8,128)S(1)} %get-tuple-element.62.sin_ref, ...), custom_call_target="tpu_custom_call" | custom-call | flops 40265318400 | bytes 8388608 | tf_op jit(solution)/shard_map/row_transform/pallas_call | solution.py:210
  108.7 1.3 copy-done.11
  110.0 1.3 copy-done.7
  111.3 18.1 %all-to-all-start.1 = ((s16[16,2,2,128,128]{4,3,2,1,0:T(8,128)(2,1)}), s16[16,2,2,128,128]{4,3,2,1,0:T(8,128)(2,1)S(1)}, u32[]{:S(2)}, u32[]{:S(2)}) async-start(s16[16,2,2,128,128]{4,3,2,1,0:T(8,128)(2,1)} %bitcast.48), calls=%async_computation.1 | async-start | bytes 4194304 | tf_op jit(solution)/shard_map/all_to_all | solution.py:388
  129.4 2.2 copy-done.3
  131.6 2.2 step_rows.7
  133.8 3.6 %collective-permute-start.5 = (s16[128,2048]{1,0:T(8,128)(2,1)}, s16[128,2048]{1,0:T(8,128)(2,1)}, u32[]{:S(2)}, u32[]{:S(2)}) collective-permute-start(s16[128,2048]{1,0:T(8,128)(2,1)} %get-tuple-element.37), channel_id=1, source_target_pairs={{0,3},{1,2},{2,1},{3,0},{4,7},{5,6},{6,5},{7,4},{8,11},{9,10},{10,... | collective-permute-start | bytes 1572872 | tf_op jit(solution)/shard_map/ppermute | solution.py:399
  137.4 1.0 collective-permute-start.3
  138.4 0.0 copy-start.15
  138.4 0.3 collective-permute-start.4
  138.7 1.3 collective-permute-done.7.refs_2_
  140.0 13.4 %row_transform.5 = s16[8,4,2,128,128]{4,3,2,1,0:T(8,128)(2,1)S(1)} custom-call(s32[1]{0:T(128)} %bitcast.z_ref, bf16[128,256]{1,0:T(8,128)(2,1)S(1)} %copy-done.17, bf16[128,256]{1,0:T(8,128)(2,1)S(1)} %copy-done.16, f32[64,128]{1,0:T(8,128)S(1)} %get-tuple-element.63.cos_ref, f32[64,128]{1,0:T(8,128)S(1)} %get-tuple-element.62.sin_ref, ...), custom_call_target="tpu_custom_call" | custom-call | flops 40265318400 | bytes 8388608 | tf_op jit(solution)/shard_map/row_transform/pallas_call | solution.py:210
  153.4 1.3 copy-done.13
  154.8 5.0 %column_mix.3.refs_0_ = f32[16,2,256,128]{3,2,1,0:T(8,128)S(1)} custom-call(bf16[256,256]{1,0:T(8,128)(2,1)S(1)} %copy-done.10, bf16[256,256]{1,0:T(8,128)(2,1)S(1)} %copy-done.9, f32[64,128]{1,0:T(8,128)S(1)} %copy-done.15, f32[64,128]{1,0:T(8,128)S(1)} %copy-done.14, s16[16,2,2,128,128]{4,3,2,1,0:T(8,128)(2,1)S(1)} %copy-done.8), custom_call_target="tpu_custom_call" | custom-call | bytes 1024 | tf_op jit(solution)/shard_map/column_mix/pallas_call | solution.py:255
  159.8 2.0 copy-done.4
  161.8 25.7 %all-to-all-done.1.in_ref = s16[16,2,2,128,128]{4,3,2,1,0:T(8,128)(2,1)S(1)} async-done(((s16[16,2,2,128,128]{4,3,2,1,0:T(8,128)(2,1)}), s16[16,2,2,128,128]{4,3,2,1,0:T(8,128)(2,1)S(1)}, u32[]{:S(2)}, u32[]{:S(2)}) %all-to-all-start.1) | async-done | bytes 2097184 | tf_op jit(solution)/shard_map/all_to_all | solution.py:388
  187.5 6.0 %all-to-all-start.2 = ((s16[16,2,2,128,128]{4,3,2,1,0:T(8,128)(2,1)}), s16[16,2,2,128,128]{4,3,2,1,0:T(8,128)(2,1)}, u32[]{:S(2)}, u32[]{:S(2)}) async-start(s16[16,2,2,128,128]{4,3,2,1,0:T(8,128)(2,1)} %bitcast.50), calls=%async_computation.2 | async-start | bytes 4194304 | tf_op jit(solution)/shard_map/all_to_all | solution.py:388
  193.6 5.2 %collective-permute-done.3.refs_1_ = s16[128,2048]{1,0:T(8,128)(2,1)} collective-permute-done((s16[128,2048]{1,0:T(8,128)(2,1)}, s16[128,2048]{1,0:T(8,128)(2,1)}, u32[]{:S(2)}, u32[]{:S(2)}) %collective-permute-start.3) | collective-permute-done | bytes 524320 | tf_op jit(solution)/shard_map/ppermute | solution.py:399
  198.8 14.8 %row_transform.4 = (s16[8,2,2,128,128]{4,3,2,1,0:T(8,128)(2,1)}, s16[8,2,2,128,128]{4,3,2,1,0:T(8,128)(2,1)}) custom-call(s32[1]{0:T(128)} %bitcast.z_ref, bf16[128,256]{1,0:T(8,128)(2,1)S(1)} %copy-done.17, bf16[128,256]{1,0:T(8,128)(2,1)S(1)} %copy-done.16, f32[64,128]{1,0:T(8,128)S(1)} %get-tuple-element.63.cos_ref, ...), custom_call_target="tpu_custom_call" | custom-call | flops 40265318400 | bytes 8388608 | tf_op jit(solution)/shard_map/row_transform/pallas_call | solution.py:210
  213.6 9.7 %all-to-all-done.2.in_ref = s16[16,2,2,128,128]{4,3,2,1,0:T(8,128)(2,1)} async-done(((s16[16,2,2,128,128]{4,3,2,1,0:T(8,128)(2,1)}), s16[16,2,2,128,128]{4,3,2,1,0:T(8,128)(2,1)}, u32[]{:S(2)}, u32[]{:S(2)}) %all-to-all-start.2) | async-done | bytes 2097184 | tf_op jit(solution)/shard_map/all_to_all | solution.py:388
  223.3 5.6 %all-to-all-start.4 = ((s16[16,1,2,128,128]{4,3,2,1,0:T(8,128)(2,1)}), s16[16,1,2,128,128]{4,3,2,1,0:T(8,128)(2,1)S(1)}, u32[]{:S(2)}, u32[]{:S(2)}) async-start(s16[16,1,2,128,128]{4,3,2,1,0:T(8,128)(2,1)} %bitcast.21), calls=%async_computation.4 | async-start | bytes 2097152 | tf_op jit(solution)/shard_map/all_to_all | solution.py:388
  228.9 5.0 %column_mix.4.refs_1_ = f32[16,2,256,128]{3,2,1,0:T(8,128)S(1)} custom-call(bf16[256,256]{1,0:T(8,128)(2,1)S(1)} %copy-done.10, bf16[256,256]{1,0:T(8,128)(2,1)S(1)} %copy-done.9, f32[64,128]{1,0:T(8,128)S(1)} %copy-done.15, f32[64,128]{1,0:T(8,128)S(1)} %copy-done.14, s16[16,2,2,128,128]{4,3,2,1,0:T(8,128)(2,1)S(1)} %all-to-all-done.1.in_ref), custom_call_target="tpu_custom_call" | custom-call | bytes 1024 | tf_op jit(solution)/shard_map/column_mix/pallas_call | solution.py:255
  233.9 2.0 copy-done.5
  235.9 6.1 %column_mix.5.refs_2_ = f32[16,2,256,128]{3,2,1,0:T(8,128)S(1)} custom-call(bf16[256,256]{1,0:T(8,128)(2,1)S(1)} %copy-done.10, bf16[256,256]{1,0:T(8,128)(2,1)S(1)} %copy-done.9, f32[64,128]{1,0:T(8,128)S(1)} %copy-done.15, f32[64,128]{1,0:T(8,128)S(1)} %copy-done.14, s16[16,2,2,128,128]{4,3,2,1,0:T(8,128)(2,1)} %all-to-all-done.2.in_ref), custom_call_target="tpu_custom_call" | custom-call | bytes 1024 | tf_op jit(solution)/shard_map/column_mix/pallas_call | solution.py:255
  241.9 2.1 copy-done.6
  244.0 5.1 %all-to-all-start.3 = ((s16[16,1,2,128,128]{4,3,2,1,0:T(8,128)(2,1)}), s16[16,1,2,128,128]{4,3,2,1,0:T(8,128)(2,1)S(1)}, u32[]{:S(2)}, u32[]{:S(2)}) async-start(s16[16,1,2,128,128]{4,3,2,1,0:T(8,128)(2,1)} %bitcast.20), calls=%async_computation.3 | async-start | bytes 2097152 | tf_op jit(solution)/shard_map/all_to_all | solution.py:388
  249.1 10.2 %column_finish.2 = (f32[256,8192]{1,0:T(8,128)}, f32[256,8192]{1,0:T(8,128)}) custom-call(bf16[256,256]{1,0:T(8,128)(2,1)} %constant.56.clone.high_ref, bf16[256,256]{1,0:T(8,128)(2,1)} %constant.57.clone.low_ref, f32[64,128]{1,0:T(8,128)} %constant.58.clone.cos_ref, f32[64,128]{1,0:T(8,128)} %constant.59.clone.sin_ref, ...), custom_call_target="tpu_custom_call" | custom-call | bytes 1024 | tf_op jit(solution)/shard_map/column_finish/pallas_call | solution.py:313
  259.3 4.1 %all-to-all-done.3.in_ref = s16[16,1,2,128,128]{4,3,2,1,0:T(8,128)(2,1)S(1)} async-done(((s16[16,1,2,128,128]{4,3,2,1,0:T(8,128)(2,1)}), s16[16,1,2,128,128]{4,3,2,1,0:T(8,128)(2,1)S(1)}, u32[]{:S(2)}, u32[]{:S(2)}) %all-to-all-start.3) | async-done | bytes 1048608 | tf_op jit(solution)/shard_map/all_to_all | solution.py:388
  263.5 1.0 copy-done.19
  264.4 10.2 %column_finish.3 = (f32[256,8192]{1,0:T(8,128)}, f32[256,8192]{1,0:T(8,128)}) custom-call(bf16[256,256]{1,0:T(8,128)(2,1)} %constant.56.clone.high_ref, bf16[256,256]{1,0:T(8,128)(2,1)} %constant.57.clone.low_ref, f32[64,128]{1,0:T(8,128)} %constant.58.clone.cos_ref, ...), custom_call_target="tpu_custom_call", output_to_operand_aliasing={{0}: (8, {}), {1}: (9, {})} | custom-call | bytes 1024 | tf_op jit(solution)/shard_map/column_finish/pallas_call | solution.py:313
  (50 shorter events, 0.3 us)
Async XLA Ops:
  1.8 2.2 copy-start
  4.0 13.1 %copy-start.20 = (f32[2,64,128]{2,1,0:T(8,128)S(1)}, f32[2,64,128]{2,1,0:T(8,128)}, u32[]{:S(2)}) copy-start(f32[2,64,128]{2,1,0:T(8,128)} %constant.53.clone) | copy-start | bytes 196612
  4.0 13.2 %copy-start.21 = (f32[2,64,128]{2,1,0:T(8,128)S(1)}, f32[2,64,128]{2,1,0:T(8,128)}, u32[]{:S(2)}) copy-start(f32[2,64,128]{2,1,0:T(8,128)} %constant.52.clone) | copy-start | bytes 196612
  5.2 24.1 %collective-permute-start.12 = (s16[128,2048]{1,0:T(8,128)(2,1)S(1)}, s16[128,2048]{1,0:T(8,128)(2,1)S(1)}, u32[]{:S(2)}, u32[]{:S(2)}) collective-permute-start(s16[128,2048]{1,0:T(8,128)(2,1)S(1)} %get-tuple-element.42), channel_id=1, source_target_pairs={{0,3},{1,2},{2,1},{3,0},{4,7},{5,6},{6,5},{7,4},{8,11},{9,10},{10,... | collective-permute-start | bytes 1572872 | tf_op jit(solution)/shard_map/ppermute | solution.py:399
  5.5 24.1 %collective-permute-start.10 = (s16[128,2048]{1,0:T(8,128)(2,1)S(1)}, s16[128,2048]{1,0:T(8,128)(2,1)S(1)}, u32[]{:S(2)}, u32[]{:S(2)}) collective-permute-start(s16[128,2048]{1,0:T(8,128)(2,1)S(1)} %get-tuple-element.42), channel_id=1, source_target_pairs={{0,1},{1,0},{2,3},{3,2},{4,5},{5,4},{6,7},{7,6},{8,9},{9,8},{10,11... | collective-permute-start | bytes 1572872 | tf_op jit(solution)/shard_map/ppermute | solution.py:399
  6.7 43.3 %collective-permute-start.11 = (s16[128,2048]{1,0:T(8,128)(2,1)S(1)}, s16[128,2048]{1,0:T(8,128)(2,1)}, u32[]{:S(2)}, u32[]{:S(2)}) collective-permute-start(s16[128,2048]{1,0:T(8,128)(2,1)S(1)} %get-tuple-element.30.refs_0_), channel_id=1, source_target_pairs={{0,2},{1,3},{2,0},{3,1},{4,6},{5,7},{6,4},{7,5},{8,10},{9,11},{10,... | collective-permute-start | bytes 1572872 | tf_op jit(solution)/shard_map/ppermute | solution.py:399
  12.6 5.0 %collective-permute-start = (bf16[1,2048]{1,0:T(2,128)(2,1)S(1)}, bf16[1,2048]{1,0:T(2,128)(2,1)S(1)}, u32[]{:S(2)}, u32[]{:S(2)}) collective-permute-start(bf16[1,2048]{1,0:T(2,128)(2,1)S(1)} %slice.73), channel_id=1, source_target_pairs={{0,4},{4,8},{8,12},{12,16},{16,20},{20,24},{24,28},{1,5},{5,9},{9,... | collective-permute-start | bytes 12296 | tf_op jit(solution)/shard_map/ppermute | solution.py:413
  17.7 2.2 copy-start.1
  19.9 30.1 %copy-start.16 = (bf16[128,256]{1,0:T(8,128)(2,1)S(1)}, bf16[128,256]{1,0:T(8,128)(2,1)}, u32[]{:S(2)}) copy-start(bf16[128,256]{1,0:T(8,128)(2,1)} %constant.55.clone.low_ref) | copy-start | bytes 196612
  19.9 30.1 %copy-start.17 = (bf16[128,256]{1,0:T(8,128)(2,1)S(1)}, bf16[128,256]{1,0:T(8,128)(2,1)}, u32[]{:S(2)}) copy-start(bf16[128,256]{1,0:T(8,128)(2,1)} %constant.54.clone.high_ref) | copy-start | bytes 196612
  22.1 71.3 %collective-permute-start.8 = (s16[128,2048]{1,0:T(8,128)(2,1)}, s16[128,2048]{1,0:T(8,128)(2,1)}, u32[]{:S(2)}, u32[]{:S(2)}) collective-permute-start(s16[128,2048]{1,0:T(8,128)(2,1)} %get-tuple-element.32), channel_id=1, source_target_pairs={{0,1},{1,0},{2,3},{3,2},{4,5},{5,4},{6,7},{7,6},{8,9},{9,8},{10,11... | collective-permute-start | bytes 1572872 | tf_op jit(solution)/shard_map/ppermute | solution.py:399
  23.8 61.8 %collective-permute-start.1 = (s16[128,2048]{1,0:T(8,128)(2,1)}, s16[128,2048]{1,0:T(8,128)(2,1)}, u32[]{:S(2)}, u32[]{:S(2)}) collective-permute-start(s16[128,2048]{1,0:T(8,128)(2,1)} %get-tuple-element.32), channel_id=1, source_target_pairs={{0,3},{1,2},{2,1},{3,0},{4,7},{5,6},{6,5},{7,4},{8,11},{9,10},{10,... | collective-permute-start | bytes 1572872 | tf_op jit(solution)/shard_map/ppermute | solution.py:399
  29.3 65.7 %collective-permute-start.9 = (s16[128,2048]{1,0:T(8,128)(2,1)}, s16[128,2048]{1,0:T(8,128)(2,1)}, u32[]{:S(2)}, u32[]{:S(2)}) collective-permute-start(s16[128,2048]{1,0:T(8,128)(2,1)} %get-tuple-element.41.refs_0_), channel_id=1, source_target_pairs={{0,2},{1,3},{2,0},{3,1},{4,6},{5,7},{6,4},{7,5},{8,10},{9,11},{10,... | collective-permute-start | bytes 1572872 | tf_op jit(solution)/shard_map/ppermute | solution.py:399
  63.1 1.3 copy-start.12
  64.5 45.5 %all-to-all-start = ((s16[16,2,2,128,128]{4,3,2,1,0:T(8,128)(2,1)}), s16[16,2,2,128,128]{4,3,2,1,0:T(8,128)(2,1)S(1)}, u32[]{:S(2)}, u32[]{:S(2)}) async-start(s16[16,2,2,128,128]{4,3,2,1,0:T(8,128)(2,1)} %bitcast.49), calls=%async_computation | async-start | bytes 4194304 | tf_op jit(solution)/shard_map/all_to_all | solution.py:388
  85.7 2.2 copy-start.2
  89.8 48.8 %collective-permute-start.6 = (s16[128,2048]{1,0:T(8,128)(2,1)}, s16[128,2048]{1,0:T(8,128)(2,1)}, u32[]{:S(2)}, u32[]{:S(2)}) collective-permute-start(s16[128,2048]{1,0:T(8,128)(2,1)} %get-tuple-element.34), channel_id=1, source_target_pairs={{0,1},{1,0},{2,3},{3,2},{4,5},{5,4},{6,7},{7,6},{8,9},{9,8},{10,11... | collective-permute-start | bytes 1572872 | tf_op jit(solution)/shard_map/ppermute | solution.py:399
  89.9 39.6 %collective-permute-start.2 = (s16[128,2048]{1,0:T(8,128)(2,1)}, s16[128,2048]{1,0:T(8,128)(2,1)}, u32[]{:S(2)}, u32[]{:S(2)}) collective-permute-start(s16[128,2048]{1,0:T(8,128)(2,1)} %get-tuple-element.34), channel_id=1, source_target_pairs={{0,3},{1,2},{2,1},{3,0},{4,7},{5,6},{6,5},{7,4},{8,11},{9,10},{10,... | collective-permute-start | bytes 1572872 | tf_op jit(solution)/shard_map/ppermute | solution.py:399
  90.2 49.8 %collective-permute-start.7 = (s16[128,2048]{1,0:T(8,128)(2,1)S(1)}, s16[128,2048]{1,0:T(8,128)(2,1)}, u32[]{:S(2)}, u32[]{:S(2)}) collective-permute-start(s16[128,2048]{1,0:T(8,128)(2,1)S(1)} %get-tuple-element.40.refs_0_), channel_id=1, source_target_pairs={{0,2},{1,3},{2,0},{3,1},{4,6},{5,7},{6,4},{7,5},{8,10},{9,11},{10,... | collective-permute-start | bytes 1572872 | tf_op jit(solution)/shard_map/ppermute | solution.py:399
  108.6 1.3 copy-start.11
  110.0 1.3 copy-start.7
  111.3 76.2 %all-to-all-start.1 = ((s16[16,2,2,128,128]{4,3,2,1,0:T(8,128)(2,1)}), s16[16,2,2,128,128]{4,3,2,1,0:T(8,128)(2,1)S(1)}, u32[]{:S(2)}, u32[]{:S(2)}) async-start(s16[16,2,2,128,128]{4,3,2,1,0:T(8,128)(2,1)} %bitcast.48), calls=%async_computation.1 | async-start | bytes 4194304 | tf_op jit(solution)/shard_map/all_to_all | solution.py:388
  129.4 2.2 copy-start.3
  133.8 59.8 %collective-permute-start.5 = (s16[128,2048]{1,0:T(8,128)(2,1)}, s16[128,2048]{1,0:T(8,128)(2,1)}, u32[]{:S(2)}, u32[]{:S(2)}) collective-permute-start(s16[128,2048]{1,0:T(8,128)(2,1)} %get-tuple-element.37), channel_id=1, source_target_pairs={{0,3},{1,2},{2,1},{3,0},{4,7},{5,6},{6,5},{7,4},{8,11},{9,10},{10,... | collective-permute-start | bytes 1572872 | tf_op jit(solution)/shard_map/ppermute | solution.py:399
  137.4 61.4 %collective-permute-start.3 = (s16[128,2048]{1,0:T(8,128)(2,1)}, s16[128,2048]{1,0:T(8,128)(2,1)}, u32[]{:S(2)}, u32[]{:S(2)}) collective-permute-start(s16[128,2048]{1,0:T(8,128)(2,1)} %get-tuple-element.37), channel_id=1, source_target_pairs={{0,1},{1,0},{2,3},{3,2},{4,5},{5,4},{6,7},{7,6},{8,9},{9,8},{10,11... | collective-permute-start | bytes 1572872 | tf_op jit(solution)/shard_map/ppermute | solution.py:399
  138.4 16.4 %copy-start.8 = (s16[16,2,2,128,128]{4,3,2,1,0:T(8,128)(2,1)S(1)}, s16[16,2,2,128,128]{4,3,2,1,0:T(8,128)(2,1)}, u32[]{:S(2)}) copy-start(s16[16,2,2,128,128]{4,3,2,1,0:T(8,128)(2,1)} %copy-done.7) | copy-start | bytes 6291460
  138.4 16.4 %copy-start.9 = (bf16[256,256]{1,0:T(8,128)(2,1)S(1)}, bf16[256,256]{1,0:T(8,128)(2,1)}, u32[]{:S(2)}) copy-start(bf16[256,256]{1,0:T(8,128)(2,1)} %constant.57.clone.low_ref) | copy-start | bytes 393220
  138.4 16.4 %copy-start.10 = (bf16[256,256]{1,0:T(8,128)(2,1)S(1)}, bf16[256,256]{1,0:T(8,128)(2,1)}, u32[]{:S(2)}) copy-start(bf16[256,256]{1,0:T(8,128)(2,1)} %constant.56.clone.high_ref) | copy-start | bytes 393220
  138.4 16.4 %copy-start.14 = (f32[64,128]{1,0:T(8,128)S(1)}, f32[64,128]{1,0:T(8,128)}, u32[]{:S(2)}) copy-start(f32[64,128]{1,0:T(8,128)} %constant.59.clone.sin_ref) | copy-start | bytes 98308
  138.4 16.4 %copy-start.15 = (f32[64,128]{1,0:T(8,128)S(1)}, f32[64,128]{1,0:T(8,128)}, u32[]{:S(2)}) copy-start(f32[64,128]{1,0:T(8,128)} %constant.58.clone.cos_ref) | copy-start | bytes 98308
  138.4 55.2 %collective-permute-start.4 = (s16[128,2048]{1,0:T(8,128)(2,1)}, s16[128,2048]{1,0:T(8,128)(2,1)}, u32[]{:S(2)}, u32[]{:S(2)}) collective-permute-start(s16[128,2048]{1,0:T(8,128)(2,1)} %get-tuple-element.36.refs_0_), channel_id=1, source_target_pairs={{0,2},{1,3},{2,0},{3,1},{4,6},{5,7},{6,4},{7,5},{8,10},{9,11},{10,... | collective-permute-start | bytes 1572872 | tf_op jit(solution)/shard_map/ppermute | solution.py:399
  153.4 1.4 copy-start.13
  159.8 2.0 copy-start.4
  187.5 35.7 %all-to-all-start.2 = ((s16[16,2,2,128,128]{4,3,2,1,0:T(8,128)(2,1)}), s16[16,2,2,128,128]{4,3,2,1,0:T(8,128)(2,1)}, u32[]{:S(2)}, u32[]{:S(2)}) async-start(s16[16,2,2,128,128]{4,3,2,1,0:T(8,128)(2,1)} %bitcast.50), calls=%async_computation.2 | async-start | bytes 4194304 | tf_op jit(solution)/shard_map/all_to_all | solution.py:388
  223.3 20.7 %all-to-all-start.4 = ((s16[16,1,2,128,128]{4,3,2,1,0:T(8,128)(2,1)}), s16[16,1,2,128,128]{4,3,2,1,0:T(8,128)(2,1)S(1)}, u32[]{:S(2)}, u32[]{:S(2)}) async-start(s16[16,1,2,128,128]{4,3,2,1,0:T(8,128)(2,1)} %bitcast.21), calls=%async_computation.4 | async-start | bytes 2097152 | tf_op jit(solution)/shard_map/all_to_all | solution.py:388
  233.8 2.0 copy-start.5
  241.9 2.1 copy-start.6
  244.0 5.1 %copy-start.18 = (s16[16,1,2,128,128]{4,3,2,1,0:T(8,128)(2,1)}, s16[16,1,2,128,128]{4,3,2,1,0:T(8,128)(2,1)S(1)}, u32[]{:S(2)}) copy-start(s16[16,1,2,128,128]{4,3,2,1,0:T(8,128)(2,1)S(1)} %all-to-all-done.4.in_ref) | copy-start | bytes 3145732
  244.0 19.5 %all-to-all-start.3 = ((s16[16,1,2,128,128]{4,3,2,1,0:T(8,128)(2,1)}), s16[16,1,2,128,128]{4,3,2,1,0:T(8,128)(2,1)S(1)}, u32[]{:S(2)}, u32[]{:S(2)}) async-start(s16[16,1,2,128,128]{4,3,2,1,0:T(8,128)(2,1)} %bitcast.20), calls=%async_computation.3 | async-start | bytes 2097152 | tf_op jit(solution)/shard_map/all_to_all | solution.py:388
  263.5 1.0 copy-start.19

commit v6 on v5

--- a/solution.py
+++ b/solution.py
@@ -260,7 +260,7 @@
         + [pl.BlockSpec((sources, 1, 2, rows, width), lambda plane: (0, plane, 0, 0, 0))],
         out_specs=pl.BlockSpec((count, 2, width, LANES), lambda plane: (0, 0, plane, 0)),
         scratch_shapes=[pltpu.VMEM((sources * rows + count, width), f32)] * 2,
-        compiler_params=pltpu.CompilerParams(vmem_limit_bytes=20 * 1024 * 1024),
+        compiler_params=pltpu.CompilerParams(vmem_limit_bytes=60 * 1024 * 1024),
         cost_estimate=pl.CostEstimate(flops=0, bytes_accessed=1024, transcendentals=0),
         name="column_mix",
     )(*tables, gathered)

time: 278 us -> 277 us (level)
  local copies, waits for them, and re-layouts: 24.9 us -> 13.5 us
  Pallas kernels: 99.1 us -> 106 us
  waiting for transfers between devices: 85.9 us -> 89.3 us
    unnamed x45 -> x21, local copies, waits for them, and re-layouts: 21.1 us -> 9.74 us
    all_to_all x5, starting transfers between devices: 44.4 us -> 35.5 us  [exchange(): lax.all_to_all(spectra, ('rows', 'cols'), split_axis=0, concat_axis=0, ti...]
    ppermute x12, starting transfers between devices: 13.6 us -> 21.6 us  [send(): lax.ppermute(steps[step % half], 'cols', [(at, at ^ step) for at in range...]
    pallas_call x3, Pallas kernels: 16 us -> 21.5 us  [mix_columns(): pl.pallas_call(functools.partial(mix_chunk, first), out_shape=jax.ShapeDt...]
    ppermute x12, waiting for transfers between devices: 45.9 us -> 50.1 us  [send(): lax.ppermute(steps[step % half], 'cols', [(at, at ^ step) for at in range...]
  transfers between devices with their start and end apart: 18 -> 18, of which waited for: 11 -> 12; matrix products, arithmetic and copies ran while one was open for 2% -> 2% of each run, Pallas kernels for 32% -> 35%
where the time goes in v6:
time: 277 us; the launch traced here: 273 us
  Pallas kernels  106 us (38%)
  waiting for transfers between devices  89.3 us (32%)
  starting transfers between devices  61.4 us (22%)
  local copies, waits for them, and re-layouts  13.5 us (5%)
    pallas_call x4, Pallas kernels, transform_rows(): pl.pallas_call(functools.partial(row_kernel, cols), out_shape=[jax.ShapeD...  57.3 us
    ppermute x12, waiting for transfers between devices, send(): lax.ppermute(steps[step % half], 'cols', [(at, at ^ step) for at in range...  50.1 us
    all_to_all x5, waiting for transfers between devices, exchange(): lax.all_to_all(spectra, ('rows', 'cols'), split_axis=0, concat_axis=0, ti...  38.8 us
    all_to_all x5, starting transfers between devices, exchange(): lax.all_to_all(spectra, ('rows', 'cols'), split_axis=0, concat_axis=0, ti...  35.5 us
    ppermute x12, starting transfers between devices, send(): lax.ppermute(steps[step % half], 'cols', [(at, at ^ step) for at in range...  21.6 us
    pallas_call x3, Pallas kernels, mix_columns(): pl.pallas_call(functools.partial(mix_chunk, first), out_shape=jax.ShapeDt...  21.5 us
    pallas_call x2, Pallas kernels, finish_columns(): pl.pallas_call(functools.partial(finish_kernel, outer, first, count, len(...  20.4 us
    unnamed x21, local copies, waits for them, and re-layouts  9.74 us
  transfers between devices with their start and end apart: 18, of which 12 were waited for; matrix products, arithmetic and copies ran while one was open for 2% of the time, Pallas kernels for 35%

profile of v6, /device:TPU:17, one launch (start us, length us, event | category | flops | bytes accessed | tf_op | source)
XLA Modules:
  0.0 272.5 jit_solution(6293049054368174291)
XLA Ops:
  0.6 0.8 fusion.2
  1.5 0.1 copy.23
  1.6 0.1 copy.22
  1.7 0.1 broadcast_bitcast_fusion.1
  1.8 0.0 copy-start
  1.8 2.2 copy-done
  4.0 1.2 step_rows.4
  5.2 0.2 collective-permute-start.12
  5.5 1.2 collective-permute-start.10
  6.7 2.0 collective-permute-start.11
  8.8 1.0 broadcast_in_dim.33
  9.8 2.1 reshape.61
  11.9 0.7 fusion.3
  12.6 4.2 %collective-permute-start = (bf16[1,2048]{1,0:T(2,128)(2,1)S(1)}, bf16[1,2048]{1,0:T(2,128)(2,1)S(1)}, u32[]{:S(2)}, u32[]{:S(2)}) collective-permute-start(bf16[1,2048]{1,0:T(2,128)(2,1)S(1)} %slice.73), channel_id=1, source_target_pairs={{0,4},{4,8},{8,12},{12,16},{16,20},{20,24},{24,28},{1,5},{5,9},{9,... | collective-permute-start | bytes 12296 | tf_op jit(solution)/shard_map/ppermute | solution.py:413
  16.9 0.1 copy.25
  16.9 0.1 copy.21
  17.0 0.1 broadcast_bitcast_fusion
  17.2 0.4 collective-permute-done
  17.7 0.0 copy-start.1
  17.7 2.2 copy-done.1
  19.9 2.2 step_rows.5
  22.1 1.7 collective-permute-start.8
  23.8 0.0 collective-permute-start.1
  23.8 5.5 %collective-permute-done.12.refs_3_ = s16[128,2048]{1,0:T(8,128)(2,1)S(1)} collective-permute-done((s16[128,2048]{1,0:T(8,128)(2,1)S(1)}, s16[128,2048]{1,0:T(8,128)(2,1)S(1)}, u32[]{:S(2)}, u32[]{:S(2)}) %collective-permute-start.12) | collective-permute-done | bytes 524320 | tf_op jit(solution)/shard_map/ppermute | solution.py:399
  29.3 0.2 collective-permute-done.10.refs_1_
  29.6 20.4 %collective-permute-done.11.refs_2_ = s16[128,2048]{1,0:T(8,128)(2,1)S(1)} collective-permute-done((s16[128,2048]{1,0:T(8,128)(2,1)S(1)}, s16[128,2048]{1,0:T(8,128)(2,1)S(1)}, u32[]{:S(2)}, u32[]{:S(2)}) %collective-permute-start.11) | collective-permute-done | bytes 524320 | tf_op jit(solution)/shard_map/ppermute | solution.py:399
  50.0 13.4 %row_transform.7 = s16[8,4,2,128,128]{4,3,2,1,0:T(8,128)(2,1)} custom-call(s32[1]{0:T(128)} %bitcast.z_ref, bf16[128,256]{1,0:T(8,128)(2,1)S(1)} %copy-done.5, bf16[128,256]{1,0:T(8,128)(2,1)S(1)} %copy-done.4, f32[64,128]{1,0:T(8,128)S(1)} %get-tuple-element.63.cos_ref, f32[64,128]{1,0:T(8,128)S(1)} %get-tuple-element.62.sin_ref, ...), custom_call_target="tpu_custom_call" | custom-call | flops 40265318400 | bytes 8388608 | tf_op jit(solution)/shard_map/row_transform/pallas_call | solution.py:210
  63.4 9.5 %all-to-all-start = ((s16[16,2,2,128,128]{4,3,2,1,0:T(8,128)(2,1)}), s16[16,2,2,128,128]{4,3,2,1,0:T(8,128)(2,1)}, u32[]{:S(2)}, u32[]{:S(2)}) async-start(s16[16,2,2,128,128]{4,3,2,1,0:T(8,128)(2,1)} %bitcast.17), calls=%async_computation | async-start | bytes 4194304 | tf_op jit(solution)/shard_map/all_to_all | solution.py:388
  72.9 12.8 %collective-permute-done.1.refs_3_ = s16[128,2048]{1,0:T(8,128)(2,1)} collective-permute-done((s16[128,2048]{1,0:T(8,128)(2,1)}, s16[128,2048]{1,0:T(8,128)(2,1)}, u32[]{:S(2)}, u32[]{:S(2)}) %collective-permute-start.1) | collective-permute-done | bytes 524320 | tf_op jit(solution)/shard_map/ppermute | solution.py:399
  85.7 2.2 copy-done.2
  87.8 1.2 step_rows.6
  89.1 0.1 collective-permute-start.6
  89.1 0.4 collective-permute-start.2
  89.6 3.1 %collective-permute-start.7 = (s16[128,2048]{1,0:T(8,128)(2,1)S(1)}, s16[128,2048]{1,0:T(8,128)(2,1)}, u32[]{:S(2)}, u32[]{:S(2)}) collective-permute-start(s16[128,2048]{1,0:T(8,128)(2,1)S(1)} %get-tuple-element.40.refs_0_), channel_id=1, source_target_pairs={{0,2},{1,3},{2,0},{3,1},{4,6},{5,7},{6,4},{7,5},{8,10},{9,11},{10,... | collective-permute-start | bytes 1572872 | tf_op jit(solution)/shard_map/ppermute | solution.py:399
  92.7 2.4 collective-permute-done.9.refs_2_
  95.0 14.9 %row_transform.6 = s16[8,4,2,128,128]{4,3,2,1,0:T(8,128)(2,1)} custom-call(s32[1]{0:T(128)} %bitcast.z_ref, bf16[128,256]{1,0:T(8,128)(2,1)S(1)} %copy-done.5, bf16[128,256]{1,0:T(8,128)(2,1)S(1)} %copy-done.4, f32[64,128]{1,0:T(8,128)S(1)} %get-tuple-element.63.cos_ref, f32[64,128]{1,0:T(8,128)S(1)} %get-tuple-element.62.sin_ref, ...), custom_call_target="tpu_custom_call" | custom-call | flops 40265318400 | bytes 8388608 | tf_op jit(solution)/shard_map/row_transform/pallas_call | solution.py:210
  110.0 0.0 all-to-all-done.in_ref
  110.0 9.2 %all-to-all-start.1 = ((s16[16,2,2,128,128]{4,3,2,1,0:T(8,128)(2,1)}), s16[16,2,2,128,128]{4,3,2,1,0:T(8,128)(2,1)}, u32[]{:S(2)}, u32[]{:S(2)}) async-start(s16[16,2,2,128,128]{4,3,2,1,0:T(8,128)(2,1)} %bitcast.18), calls=%async_computation.1 | async-start | bytes 4194304 | tf_op jit(solution)/shard_map/all_to_all | solution.py:388
  119.2 0.0 collective-permute-done.2.refs_3_
  119.2 0.0 copy-start.3
  119.2 2.2 copy-done.3
  121.4 2.0 step_rows.7
  123.4 11.7 %collective-permute-start.5 = (s16[128,2048]{1,0:T(8,128)(2,1)}, s16[128,2048]{1,0:T(8,128)(2,1)S(1)}, u32[]{:S(2)}, u32[]{:S(2)}) collective-permute-start(s16[128,2048]{1,0:T(8,128)(2,1)} %get-tuple-element.37), channel_id=1, source_target_pairs={{0,3},{1,2},{2,1},{3,0},{4,7},{5,6},{6,5},{7,4},{8,11},{9,10},{10,... | collective-permute-start | bytes 1572872 | tf_op jit(solution)/shard_map/ppermute | solution.py:399
  135.1 1.0 collective-permute-start.3
  136.1 0.2 collective-permute-start.4
  136.3 0.0 collective-permute-done.6.refs_1_
  136.3 3.7 %collective-permute-done.7.refs_2_ = s16[128,2048]{1,0:T(8,128)(2,1)} collective-permute-done((s16[128,2048]{1,0:T(8,128)(2,1)S(1)}, s16[128,2048]{1,0:T(8,128)(2,1)}, u32[]{:S(2)}, u32[]{:S(2)}) %collective-permute-start.7) | collective-permute-done | bytes 524320 | tf_op jit(solution)/shard_map/ppermute | solution.py:399
  140.0 14.4 %row_transform.5 = s16[8,4,2,128,128]{4,3,2,1,0:T(8,128)(2,1)} custom-call(s32[1]{0:T(128)} %bitcast.z_ref, bf16[128,256]{1,0:T(8,128)(2,1)S(1)} %copy-done.5, bf16[128,256]{1,0:T(8,128)(2,1)S(1)} %copy-done.4, f32[64,128]{1,0:T(8,128)S(1)} %get-tuple-element.63.cos_ref, f32[64,128]{1,0:T(8,128)S(1)} %get-tuple-element.62.sin_ref, ...), custom_call_target="tpu_custom_call" | custom-call | flops 40265318400 | bytes 8388608 | tf_op jit(solution)/shard_map/row_transform/pallas_call | solution.py:210
  154.4 7.2 %column_mix.3.refs_0_ = f32[16,2,256,128]{3,2,1,0:T(8,128)} custom-call(bf16[256,256]{1,0:T(8,128)(2,1)} %constant.56.clone.high_ref, bf16[256,256]{1,0:T(8,128)(2,1)} %constant.57.clone.low_ref, f32[64,128]{1,0:T(8,128)} %constant.58.clone.cos_ref, f32[64,128]{1,0:T(8,128)} %constant.59.clone.sin_ref, s16[16,2,2,128,128]{4,3,2,1,0:T(8,128)(2,1)} %all-to-all-done.in_ref), custom_call_target="tpu_custom_call" | custom-call | bytes 1024 | tf_op jit(solution)/shard_map/column_mix/pallas_call | solution.py:255
  161.6 24.5 %all-to-all-done.1.in_ref = s16[16,2,2,128,128]{4,3,2,1,0:T(8,128)(2,1)} async-done(((s16[16,2,2,128,128]{4,3,2,1,0:T(8,128)(2,1)}), s16[16,2,2,128,128]{4,3,2,1,0:T(8,128)(2,1)}, u32[]{:S(2)}, u32[]{:S(2)}) %all-to-all-start.1) | async-done | bytes 2097184 | tf_op jit(solution)/shard_map/all_to_all | solution.py:388
  186.0 6.1 %all-to-all-start.2 = ((s16[16,2,2,128,128]{4,3,2,1,0:T(8,128)(2,1)}), s16[16,2,2,128,128]{4,3,2,1,0:T(8,128)(2,1)S(1)}, u32[]{:S(2)}, u32[]{:S(2)}) async-start(s16[16,2,2,128,128]{4,3,2,1,0:T(8,128)(2,1)} %bitcast.19), calls=%async_computation.2 | async-start | bytes 4194304 | tf_op jit(solution)/shard_map/all_to_all | solution.py:388
  192.2 0.0 collective-permute-done.5.refs_3_
  192.2 5.1 %collective-permute-done.3.refs_1_ = s16[128,2048]{1,0:T(8,128)(2,1)} collective-permute-done((s16[128,2048]{1,0:T(8,128)(2,1)}, s16[128,2048]{1,0:T(8,128)(2,1)}, u32[]{:S(2)}, u32[]{:S(2)}) %collective-permute-start.3) | collective-permute-done | bytes 524320 | tf_op jit(solution)/shard_map/ppermute | solution.py:399
  197.3 14.5 %row_transform.4 = (s16[8,2,2,128,128]{4,3,2,1,0:T(8,128)(2,1)}, s16[8,2,2,128,128]{4,3,2,1,0:T(8,128)(2,1)}) custom-call(s32[1]{0:T(128)} %bitcast.z_ref, bf16[128,256]{1,0:T(8,128)(2,1)S(1)} %copy-done.5, bf16[128,256]{1,0:T(8,128)(2,1)S(1)} %copy-done.4, f32[64,128]{1,0:T(8,128)S(1)} %get-tuple-element.63.cos_ref, ...), custom_call_target="tpu_custom_call" | custom-call | flops 40265318400 | bytes 8388608 | tf_op jit(solution)/shard_map/row_transform/pallas_call | solution.py:210
  211.8 10.1 %all-to-all-done.2.in_ref = s16[16,2,2,128,128]{4,3,2,1,0:T(8,128)(2,1)S(1)} async-done(((s16[16,2,2,128,128]{4,3,2,1,0:T(8,128)(2,1)}), s16[16,2,2,128,128]{4,3,2,1,0:T(8,128)(2,1)S(1)}, u32[]{:S(2)}, u32[]{:S(2)}) %all-to-all-start.2) | async-done | bytes 2097184 | tf_op jit(solution)/shard_map/all_to_all | solution.py:388
  221.8 5.7 %all-to-all-start.4 = ((s16[16,1,2,128,128]{4,3,2,1,0:T(8,128)(2,1)}), s16[16,1,2,128,128]{4,3,2,1,0:T(8,128)(2,1)}, u32[]{:S(2)}, u32[]{:S(2)}) async-start(s16[16,1,2,128,128]{4,3,2,1,0:T(8,128)(2,1)} %bitcast.21), calls=%async_computation.4 | async-start | bytes 2097152 | tf_op jit(solution)/shard_map/all_to_all | solution.py:388
  227.5 7.2 %column_mix.4.refs_1_ = f32[16,2,256,128]{3,2,1,0:T(8,128)} custom-call(bf16[256,256]{1,0:T(8,128)(2,1)} %constant.56.clone.high_ref, bf16[256,256]{1,0:T(8,128)(2,1)} %constant.57.clone.low_ref, f32[64,128]{1,0:T(8,128)} %constant.58.clone.cos_ref, f32[64,128]{1,0:T(8,128)} %constant.59.clone.sin_ref, s16[16,2,2,128,128]{4,3,2,1,0:T(8,128)(2,1)} %all-to-all-done.1.in_ref), custom_call_target="tpu_custom_call" | custom-call | bytes 1024 | tf_op jit(solution)/shard_map/column_mix/pallas_call | solution.py:255
  234.7 7.2 %column_mix.5.refs_2_ = f32[16,2,256,128]{3,2,1,0:T(8,128)} custom-call(bf16[256,256]{1,0:T(8,128)(2,1)} %constant.56.clone.high_ref, bf16[256,256]{1,0:T(8,128)(2,1)} %constant.57.clone.low_ref, f32[64,128]{1,0:T(8,128)} %constant.58.clone.cos_ref, f32[64,128]{1,0:T(8,128)} %constant.59.clone.sin_ref, s16[16,2,2,128,128]{4,3,2,1,0:T(8,128)(2,1)} %copy-done.6), custom_call_target="tpu_custom_call" | custom-call | bytes 1024 | tf_op jit(solution)/shard_map/column_mix/pallas_call | solution.py:255
  241.9 0.1 all-to-all-done.4.in_ref
  242.0 5.0 %all-to-all-start.3 = ((s16[16,1,2,128,128]{4,3,2,1,0:T(8,128)(2,1)}), s16[16,1,2,128,128]{4,3,2,1,0:T(8,128)(2,1)S(1)}, u32[]{:S(2)}, u32[]{:S(2)}) async-start(s16[16,1,2,128,128]{4,3,2,1,0:T(8,128)(2,1)} %bitcast.20), calls=%async_computation.3 | async-start | bytes 2097152 | tf_op jit(solution)/shard_map/all_to_all | solution.py:388
  247.0 10.2 %column_finish.2 = (f32[256,8192]{1,0:T(8,128)}, f32[256,8192]{1,0:T(8,128)}) custom-call(bf16[256,256]{1,0:T(8,128)(2,1)} %constant.56.clone.high_ref, bf16[256,256]{1,0:T(8,128)(2,1)} %constant.57.clone.low_ref, f32[64,128]{1,0:T(8,128)} %constant.58.clone.cos_ref, f32[64,128]{1,0:T(8,128)} %constant.59.clone.sin_ref, ...), custom_call_target="tpu_custom_call" | custom-call | bytes 1024 | tf_op jit(solution)/shard_map/column_finish/pallas_call | solution.py:313
  257.2 4.1 %all-to-all-done.3.in_ref = s16[16,1,2,128,128]{4,3,2,1,0:T(8,128)(2,1)S(1)} async-done(((s16[16,1,2,128,128]{4,3,2,1,0:T(8,128)(2,1)}), s16[16,1,2,128,128]{4,3,2,1,0:T(8,128)(2,1)S(1)}, u32[]{:S(2)}, u32[]{:S(2)}) %all-to-all-start.3) | async-done | bytes 1048608 | tf_op jit(solution)/shard_map/all_to_all | solution.py:388
  261.4 1.0 copy-done.7
  262.3 10.2 %column_finish.3 = (f32[256,8192]{1,0:T(8,128)}, f32[256,8192]{1,0:T(8,128)}) custom-call(bf16[256,256]{1,0:T(8,128)(2,1)} %constant.56.clone.high_ref, bf16[256,256]{1,0:T(8,128)(2,1)} %constant.57.clone.low_ref, f32[64,128]{1,0:T(8,128)} %constant.58.clone.cos_ref, ...), custom_call_target="tpu_custom_call", output_to_operand_aliasing={{0}: (8, {}), {1}: (9, {})} | custom-call | bytes 1024 | tf_op jit(solution)/shard_map/column_finish/pallas_call | solution.py:313
  (26 shorter events, 0.2 us)
Async XLA Ops:
  1.8 2.2 copy-start
  4.0 13.1 %copy-start.8 = (f32[2,64,128]{2,1,0:T(8,128)S(1)}, f32[2,64,128]{2,1,0:T(8,128)}, u32[]{:S(2)}) copy-start(f32[2,64,128]{2,1,0:T(8,128)} %constant.53.clone) | copy-start | bytes 196612
  4.0 13.2 %copy-start.9 = (f32[2,64,128]{2,1,0:T(8,128)S(1)}, f32[2,64,128]{2,1,0:T(8,128)}, u32[]{:S(2)}) copy-start(f32[2,64,128]{2,1,0:T(8,128)} %constant.52.clone) | copy-start | bytes 196612
  5.2 24.1 %collective-permute-start.12 = (s16[128,2048]{1,0:T(8,128)(2,1)S(1)}, s16[128,2048]{1,0:T(8,128)(2,1)S(1)}, u32[]{:S(2)}, u32[]{:S(2)}) collective-permute-start(s16[128,2048]{1,0:T(8,128)(2,1)S(1)} %get-tuple-element.42), channel_id=1, source_target_pairs={{0,3},{1,2},{2,1},{3,0},{4,7},{5,6},{6,5},{7,4},{8,11},{9,10},{10,... | collective-permute-start | bytes 1572872 | tf_op jit(solution)/shard_map/ppermute | solution.py:399
  5.5 24.1 %collective-permute-start.10 = (s16[128,2048]{1,0:T(8,128)(2,1)S(1)}, s16[128,2048]{1,0:T(8,128)(2,1)S(1)}, u32[]{:S(2)}, u32[]{:S(2)}) collective-permute-start(s16[128,2048]{1,0:T(8,128)(2,1)S(1)} %get-tuple-element.42), channel_id=1, source_target_pairs={{0,1},{1,0},{2,3},{3,2},{4,5},{5,4},{6,7},{7,6},{8,9},{9,8},{10,11... | collective-permute-start | bytes 1572872 | tf_op jit(solution)/shard_map/ppermute | solution.py:399
  6.7 43.3 %collective-permute-start.11 = (s16[128,2048]{1,0:T(8,128)(2,1)S(1)}, s16[128,2048]{1,0:T(8,128)(2,1)S(1)}, u32[]{:S(2)}, u32[]{:S(2)}) collective-permute-start(s16[128,2048]{1,0:T(8,128)(2,1)S(1)} %get-tuple-element.30.refs_0_), channel_id=1, source_target_pairs={{0,2},{1,3},{2,0},{3,1},{4,6},{5,7},{6,4},{7,5},{8,10},{9,11},{10,... | collective-permute-start | bytes 1572872 | tf_op jit(solution)/shard_map/ppermute | solution.py:399
  12.6 5.0 %collective-permute-start = (bf16[1,2048]{1,0:T(2,128)(2,1)S(1)}, bf16[1,2048]{1,0:T(2,128)(2,1)S(1)}, u32[]{:S(2)}, u32[]{:S(2)}) collective-permute-start(bf16[1,2048]{1,0:T(2,128)(2,1)S(1)} %slice.73), channel_id=1, source_target_pairs={{0,4},{4,8},{8,12},{12,16},{16,20},{20,24},{24,28},{1,5},{5,9},{9,... | collective-permute-start | bytes 12296 | tf_op jit(solution)/shard_map/ppermute | solution.py:413
  17.7 2.2 copy-start.1
  19.9 30.1 %copy-start.4 = (bf16[128,256]{1,0:T(8,128)(2,1)S(1)}, bf16[128,256]{1,0:T(8,128)(2,1)}, u32[]{:S(2)}) copy-start(bf16[128,256]{1,0:T(8,128)(2,1)} %constant.55.clone.low_ref) | copy-start | bytes 196612
  19.9 30.1 %copy-start.5 = (bf16[128,256]{1,0:T(8,128)(2,1)S(1)}, bf16[128,256]{1,0:T(8,128)(2,1)}, u32[]{:S(2)}) copy-start(bf16[128,256]{1,0:T(8,128)(2,1)} %constant.54.clone.high_ref) | copy-start | bytes 196612
  22.1 70.6 %collective-permute-start.8 = (s16[128,2048]{1,0:T(8,128)(2,1)}, s16[128,2048]{1,0:T(8,128)(2,1)}, u32[]{:S(2)}, u32[]{:S(2)}) collective-permute-start(s16[128,2048]{1,0:T(8,128)(2,1)} %get-tuple-element.32), channel_id=1, source_target_pairs={{0,1},{1,0},{2,3},{3,2},{4,5},{5,4},{6,7},{7,6},{8,9},{9,8},{10,11... | collective-permute-start | bytes 1572872 | tf_op jit(solution)/shard_map/ppermute | solution.py:399
  23.8 61.8 %collective-permute-start.1 = (s16[128,2048]{1,0:T(8,128)(2,1)}, s16[128,2048]{1,0:T(8,128)(2,1)}, u32[]{:S(2)}, u32[]{:S(2)}) collective-permute-start(s16[128,2048]{1,0:T(8,128)(2,1)} %get-tuple-element.32), channel_id=1, source_target_pairs={{0,3},{1,2},{2,1},{3,0},{4,7},{5,6},{6,5},{7,4},{8,11},{9,10},{10,... | collective-permute-start | bytes 1572872 | tf_op jit(solution)/shard_map/ppermute | solution.py:399
  29.3 65.7 %collective-permute-start.9 = (s16[128,2048]{1,0:T(8,128)(2,1)}, s16[128,2048]{1,0:T(8,128)(2,1)}, u32[]{:S(2)}, u32[]{:S(2)}) collective-permute-start(s16[128,2048]{1,0:T(8,128)(2,1)} %get-tuple-element.41.refs_0_), channel_id=1, source_target_pairs={{0,2},{1,3},{2,0},{3,1},{4,6},{5,7},{6,4},{7,5},{8,10},{9,11},{10,... | collective-permute-start | bytes 1572872 | tf_op jit(solution)/shard_map/ppermute | solution.py:399
  63.4 46.6 %all-to-all-start = ((s16[16,2,2,128,128]{4,3,2,1,0:T(8,128)(2,1)}), s16[16,2,2,128,128]{4,3,2,1,0:T(8,128)(2,1)}, u32[]{:S(2)}, u32[]{:S(2)}) async-start(s16[16,2,2,128,128]{4,3,2,1,0:T(8,128)(2,1)} %bitcast.17), calls=%async_computation | async-start | bytes 4194304 | tf_op jit(solution)/shard_map/all_to_all | solution.py:388
  85.7 2.2 copy-start.2
  89.1 47.2 %collective-permute-start.6 = (s16[128,2048]{1,0:T(8,128)(2,1)S(1)}, s16[128,2048]{1,0:T(8,128)(2,1)S(1)}, u32[]{:S(2)}, u32[]{:S(2)}) collective-permute-start(s16[128,2048]{1,0:T(8,128)(2,1)S(1)} %get-tuple-element.34), channel_id=1, source_target_pairs={{0,1},{1,0},{2,3},{3,2},{4,5},{5,4},{6,7},{7,6},{8,9},{9,8},{10,11... | collective-permute-start | bytes 1572872 | tf_op jit(solution)/shard_map/ppermute | solution.py:399
  89.1 30.1 %collective-permute-start.2 = (s16[128,2048]{1,0:T(8,128)(2,1)S(1)}, s16[128,2048]{1,0:T(8,128)(2,1)S(1)}, u32[]{:S(2)}, u32[]{:S(2)}) collective-permute-start(s16[128,2048]{1,0:T(8,128)(2,1)S(1)} %get-tuple-element.34), channel_id=1, source_target_pairs={{0,3},{1,2},{2,1},{3,0},{4,7},{5,6},{6,5},{7,4},{8,11},{9,10},{10,... | collective-permute-start | bytes 1572872 | tf_op jit(solution)/shard_map/ppermute | solution.py:399
  89.6 50.4 %collective-permute-start.7 = (s16[128,2048]{1,0:T(8,128)(2,1)S(1)}, s16[128,2048]{1,0:T(8,128)(2,1)}, u32[]{:S(2)}, u32[]{:S(2)}) collective-permute-start(s16[128,2048]{1,0:T(8,128)(2,1)S(1)} %get-tuple-element.40.refs_0_), channel_id=1, source_target_pairs={{0,2},{1,3},{2,0},{3,1},{4,6},{5,7},{6,4},{7,5},{8,10},{9,11},{10,... | collective-permute-start | bytes 1572872 | tf_op jit(solution)/shard_map/ppermute | solution.py:399
  110.0 76.1 %all-to-all-start.1 = ((s16[16,2,2,128,128]{4,3,2,1,0:T(8,128)(2,1)}), s16[16,2,2,128,128]{4,3,2,1,0:T(8,128)(2,1)}, u32[]{:S(2)}, u32[]{:S(2)}) async-start(s16[16,2,2,128,128]{4,3,2,1,0:T(8,128)(2,1)} %bitcast.18), calls=%async_computation.1 | async-start | bytes 4194304 | tf_op jit(solution)/shard_map/all_to_all | solution.py:388
  119.2 2.2 copy-start.3
  123.4 68.7 %collective-permute-start.5 = (s16[128,2048]{1,0:T(8,128)(2,1)}, s16[128,2048]{1,0:T(8,128)(2,1)S(1)}, u32[]{:S(2)}, u32[]{:S(2)}) collective-permute-start(s16[128,2048]{1,0:T(8,128)(2,1)} %get-tuple-element.37), channel_id=1, source_target_pairs={{0,3},{1,2},{2,1},{3,0},{4,7},{5,6},{6,5},{7,4},{8,11},{9,10},{10,... | collective-permute-start | bytes 1572872 | tf_op jit(solution)/shard_map/ppermute | solution.py:399
  135.1 62.2 %collective-permute-start.3 = (s16[128,2048]{1,0:T(8,128)(2,1)}, s16[128,2048]{1,0:T(8,128)(2,1)}, u32[]{:S(2)}, u32[]{:S(2)}) collective-permute-start(s16[128,2048]{1,0:T(8,128)(2,1)} %get-tuple-element.37), channel_id=1, source_target_pairs={{0,1},{1,0},{2,3},{3,2},{4,5},{5,4},{6,7},{7,6},{8,9},{9,8},{10,11... | collective-permute-start | bytes 1572872 | tf_op jit(solution)/shard_map/ppermute | solution.py:399
  136.1 56.1 %collective-permute-start.4 = (s16[128,2048]{1,0:T(8,128)(2,1)S(1)}, s16[128,2048]{1,0:T(8,128)(2,1)}, u32[]{:S(2)}, u32[]{:S(2)}) collective-permute-start(s16[128,2048]{1,0:T(8,128)(2,1)S(1)} %get-tuple-element.36.refs_0_), channel_id=1, source_target_pairs={{0,2},{1,3},{2,0},{3,1},{4,6},{5,7},{6,4},{7,5},{8,10},{9,11},{10,... | collective-permute-start | bytes 1572872 | tf_op jit(solution)/shard_map/ppermute | solution.py:399
  186.0 35.8 %all-to-all-start.2 = ((s16[16,2,2,128,128]{4,3,2,1,0:T(8,128)(2,1)}), s16[16,2,2,128,128]{4,3,2,1,0:T(8,128)(2,1)S(1)}, u32[]{:S(2)}, u32[]{:S(2)}) async-start(s16[16,2,2,128,128]{4,3,2,1,0:T(8,128)(2,1)} %bitcast.19), calls=%async_computation.2 | async-start | bytes 4194304 | tf_op jit(solution)/shard_map/all_to_all | solution.py:388
  221.8 12.9 %copy-start.6 = (s16[16,2,2,128,128]{4,3,2,1,0:T(8,128)(2,1)}, s16[16,2,2,128,128]{4,3,2,1,0:T(8,128)(2,1)S(1)}, u32[]{:S(2)}) copy-start(s16[16,2,2,128,128]{4,3,2,1,0:T(8,128)(2,1)S(1)} %all-to-all-done.2.in_ref) | copy-start | bytes 6291460
  221.8 20.2 %all-to-all-start.4 = ((s16[16,1,2,128,128]{4,3,2,1,0:T(8,128)(2,1)}), s16[16,1,2,128,128]{4,3,2,1,0:T(8,128)(2,1)}, u32[]{:S(2)}, u32[]{:S(2)}) async-start(s16[16,1,2,128,128]{4,3,2,1,0:T(8,128)(2,1)} %bitcast.21), calls=%async_computation.4 | async-start | bytes 2097152 | tf_op jit(solution)/shard_map/all_to_all | solution.py:388
  242.0 19.4 %all-to-all-start.3 = ((s16[16,1,2,128,128]{4,3,2,1,0:T(8,128)(2,1)}), s16[16,1,2,128,128]{4,3,2,1,0:T(8,128)(2,1)S(1)}, u32[]{:S(2)}, u32[]{:S(2)}) async-start(s16[16,1,2,128,128]{4,3,2,1,0:T(8,128)(2,1)} %bitcast.20), calls=%async_computation.3 | async-start | bytes 2097152 | tf_op jit(solution)/shard_map/all_to_all | solution.py:388
  261.4 1.0 copy-start.7
